TPU v7x, 512 devices: a whole 4x4x16 slice. The times are simulated.
512 devices in a mesh: tm: 16 (over y, z_hi, core), space: 32 (over z_lo, x).
Axes of the slice: x: 4, y: 4, z: 16 (z_hi: 2, z_lo: 8; z = z_hi * 8 + z_lo), core: 2. Of those that a mesh axis runs over, the one named last changes fastest.
Arguments:
- phase_guess: float32 [16, 128, 32, 512], P('tm', 'space'), may hold values from -1 to 1
- solute_guess: float32 [16, 128, 32, 512], P('tm', 'space'), may hold values from -0.9 to 0.3
- solute_start: float32 [128, 32, 512], P('space'), may hold values from -0.8 to 0
- nuclei: int32 [8, 3], replicated, may hold values from 0 to 511, as said below
Outputs:
- phase_next: float32 [16, 128, 32, 512], P('tm', 'space')
- solute_next: float32 [16, 128, 32, 512], P('tm', 'space')
Inputs may be any that keep to these rules, and one draw needn't show every extreme that they name: `nuclei`: column 0 lies in 0 .. 127, column 1 in 0 .. 31, column 2 in 0 .. 511.
All inputs are finite; a program needn't handle non-finite values.
Results may differ from a plain program's by a relative error of at most 0.00002.
Values sent between devices are 32-bit elements; how exact they have to be, the bound alone decides.
No kernel may reach another device: no remote copies, remote signals or barrier semaphores. Data moves between devices by JAX's collectives and lax.ppermute only.
A program may use at most 64 MiB of HBM per device.

v0:
```python
import jax
import jax.numpy as jnp
from jax import lax
from jax.sharding import PartitionSpec as P

M = 4


FINE_RATE = 0.025
DIFFUSION = 1.5
COUPLING = 2.0
ANISO = 0.05
GRAD_FLOOR = 0.01
WIDTH_SQ = 18.0


def with_halo(cells, sides, width):
    for axis, dim in sides:
        count = lax.axis_size(axis)
        head = lax.slice_in_dim(cells, 0, width, axis=dim)
        tail = lax.slice_in_dim(cells, cells.shape[dim] - width, cells.shape[dim], axis=dim)
        cells = jnp.concatenate(
            [
                lax.ppermute(tail, axis, [(i, (i + 1) % count) for i in range(count)]),
                cells,
                lax.ppermute(head, axis, [((i + 1) % count, i) for i in range(count)]),
            ],
            axis=dim,
        )
    return cells


def shifted(block, axis, distance):
    devices = range(lax.axis_size(axis))
    route = [(i - distance, i) for i in devices if i - distance in devices]
    return lax.ppermute(block, axis, route)


def step_core(extended, rate):
    phase = extended[0]
    solute = extended[1]
    phase_mid = phase[1:-1]
    solute_mid = solute[1:-1]

    def laplacian(full, centre):
        zpad = jnp.concatenate([centre[:, :1], centre, centre[:, -1:]], axis=1)
        total = full[2:] + full[:-2] + jnp.roll(centre, 1, 2) + jnp.roll(centre, -1, 2)
        return total + zpad[:, 2:] + zpad[:, :-2] - 6.0 * centre

    zphase = jnp.concatenate([phase_mid[:, :1], phase_mid, phase_mid[:, -1:]], axis=1)
    grad_x = 0.5 * (phase[2:] - phase[:-2])
    grad_y = 0.5 * (jnp.roll(phase_mid, -1, 2) - jnp.roll(phase_mid, 1, 2))
    grad_z = 0.5 * (zphase[:, 2:] - zphase[:, :-2])
    squared = grad_x * grad_x + grad_y * grad_y + grad_z * grad_z
    quartic = (grad_x**4 + grad_y**4 + grad_z**4) / jnp.maximum(squared, GRAD_FLOOR) ** 2
    aniso = 1.0 + ANISO * (4.0 * quartic - 3.0)
    wetness = 1.0 - phase_mid * phase_mid
    phase_new = phase_mid + rate * (
        aniso * aniso * laplacian(phase, phase_mid)
        + phase_mid
        - phase_mid**3
        - COUPLING * solute_mid * wetness * wetness
    )
    solute_new = (
        solute_mid
        + rate * DIFFUSION * laplacian(solute, solute_mid)
        + 0.5 * (phase_new - phase_mid)
    )
    return jnp.stack([phase_new, solute_new])


def padded(state):
    return with_halo(state, (("space", 1),), 1)


def nucleus_phase(xs, zs, ys, nuclei, nx_total, ny_total):
    best = jnp.zeros((xs.shape[0], zs.shape[0], ys.shape[0]), jnp.float32)
    for nucleus in range(nuclei.shape[0]):
        dist_x = jnp.abs(xs - nuclei[nucleus, 0])
        dist_x = jnp.minimum(dist_x, nx_total - dist_x)
        dist_y = jnp.abs(ys - nuclei[nucleus, 2])
        dist_y = jnp.minimum(dist_y, ny_total - dist_y)
        dist_z = zs - nuclei[nucleus, 1]
        dist_sq = (
            (dist_x * dist_x)[:, None, None]
            + (dist_z * dist_z)[None, :, None]
            + (dist_y * dist_y)[None, None, :]
        )
        best = jnp.maximum(best, jnp.exp(-dist_sq.astype(jnp.float32) / WIDTH_SQ))
    return 2.0 * best - 1.0


def local(phase_guess, solute_guess, solute_start, nuclei):
    rows = solute_start.shape[0]
    depth = solute_start.shape[1]
    across = solute_start.shape[2]
    block_count = lax.axis_size("tm")
    time_index = lax.axis_index("tm")
    xs = lax.axis_index("space") * rows + jnp.arange(rows, dtype=jnp.int32)
    zs = jnp.arange(depth, dtype=jnp.int32)
    ys = jnp.arange(across, dtype=jnp.int32)
    initial = jnp.stack(
        [nucleus_phase(xs, zs, ys, nuclei, rows * lax.axis_size("space"), across), solute_start]
    )
    guess = jnp.stack([phase_guess[0], solute_guess[0]])
    start = jnp.where(time_index == 0, initial, guess)
    coarse_rate = M * FINE_RATE
    extended = padded(start)
    coarse_start = step_core(extended, coarse_rate)
    fine = step_core(extended, FINE_RATE)
    for turn in range(M - 1):
        fine = step_core(padded(fine), FINE_RATE)
    correction = fine - coarse_start
    incoming = shifted(correction, "tm", 1)

    def relay(turn, current):
        received = shifted(current, "tm", 1)
        updated = step_core(padded(received), coarse_rate) + incoming
        return jnp.where(time_index == 0, initial, updated)

    result = lax.fori_loop(0, block_count - 1, relay, initial)
    return (result[0][None], result[1][None])


def solution(mesh):
    return jax.shard_map(
        local,
        mesh=mesh,
        in_specs=(
            P("tm", "space", None, None),
            P("tm", "space", None, None),
            P("space", None, None),
            P(),
        ),
        out_specs=(P("tm", "space", None, None), P("tm", "space", None, None)),
        check_vma=False,
    )
```

profile of v0, /device:TPU:502, one launch (start us, length us, event | category | flops | bytes accessed | tf_op | source)
XLA Modules:
  0.0 859.6 jit_solution(10601251456542961377)
XLA Ops:
  22.7 11.8 %collective-permute-start.4 = (f32[2,1,32,512]{3,2,1,0:T(8,128)S(1)}, f32[2,1,32,512]{3,2,1,0:T(8,128)S(1)}, u32[]{:S(2)}, u32[]{:S(2)}) collective-permute-start(f32[2,1,32,512]{3,2,1,0:T(8,128)S(1)} %get-tuple-element.129), channel_id=1, source_target_pairs={{0,1},{1,2},{2,3},{3,4},{4,5},{5,6},{6,7},{7,8},{8,9},{9,10},{10,1... | collective-permute-start | bytes 393224 | tf_op jit(solution)/shard_map/ppermute | solution.py:24
  40.3 13.1 %collective-permute-start.6 = (f32[2,1,32,512]{3,2,1,0:T(8,128)S(1)}, f32[2,1,32,512]{3,2,1,0:T(8,128)S(1)}, u32[]{:S(2)}, u32[]{:S(2)}) collective-permute-start(f32[2,1,32,512]{3,2,1,0:T(8,128)S(1)} %get-tuple-element.125), channel_id=1, source_target_pairs={{0,1},{1,2},{2,3},{3,4},{4,5},{5,6},{6,7},{7,8},{8,9},{9,10},{10,1... | collective-permute-start | bytes 393224 | tf_op jit(solution)/shard_map/ppermute | solution.py:24
  59.0 13.1 %collective-permute-start.8 = (f32[2,1,32,512]{3,2,1,0:T(8,128)S(1)}, f32[2,1,32,512]{3,2,1,0:T(8,128)S(1)}, u32[]{:S(2)}, u32[]{:S(2)}) collective-permute-start(f32[2,1,32,512]{3,2,1,0:T(8,128)S(1)} %get-tuple-element.123), channel_id=1, source_target_pairs={{0,1},{1,2},{2,3},{3,4},{4,5},{5,6},{6,7},{7,8},{8,9},{9,10},{10,1... | collective-permute-start | bytes 393224 | tf_op jit(solution)/shard_map/ppermute | solution.py:24
  77.7 13.4 %collective-permute-start.10 = (f32[2,1,32,512]{3,2,1,0:T(8,128)S(1)}, f32[2,1,32,512]{3,2,1,0:T(8,128)S(1)}, u32[]{:S(2)}, u32[]{:S(2)}) collective-permute-start(f32[2,1,32,512]{3,2,1,0:T(8,128)S(1)} %get-tuple-element.121), channel_id=1, source_target_pairs={{0,1},{1,2},{2,3},{3,4},{4,5},{5,6},{6,7},{7,8},{8,9},{9,10},{10,1... | collective-permute-start | bytes 393224 | tf_op jit(solution)/shard_map/ppermute | solution.py:24
  91.1 6.3 collective-permute-done.9
  100.8 29.4 %collective-permute-done.11 = f32[2,4,32,512]{3,2,1,0:T(8,128)S(1)} collective-permute-done((f32[2,4,32,512]{3,2,1,0:T(8,128)S(1)}, f32[2,4,32,512]{3,2,1,0:T(8,128)S(1)}, u32[]{:S(2)}, u32[]{:S(2)}) %collective-permute-start.11) | collective-permute-done | bytes 524320 | tf_op jit(solution)/shard_map/ppermute | solution.py:36
  130.2 728.6 %while.12 = (s32[]{:T(128)}, f32[2,4,32,512]{3,2,1,0:T(8,128)S(1)}, pred[]{:T(512)}, f32[2,4,32,512]{3,2,1,0:T(8,128)S(1)}, f32[2,4,32,512]{3,2,1,0:T(8,128)S(1)}, /*index=5*/s32[]{:T(128)}) while((s32[]{:T(128)}, f32[2,4,32,512]{3,2,1,0:T(8,128)S(1)}, pred[]{:T(512)}, f32[2,4,32,512]{3,2,1,0:T(8,128)S(1)}, f32[2,4,32,512]{3,2,1,0:T(8,128)S(1)}, ...), condition=%wide.region_1.2_spmd, body=%wide.region_0.1_spmd.sunk | while | flops 4521986 | bytes 14778558 | solution.py:121
  132.1 17.3 %collective-permute-done = f32[2,4,32,512]{3,2,1,0:T(8,128)S(1)} collective-permute-done((f32[2,4,32,512]{3,2,1,0:T(8,128)S(1)}, f32[2,4,32,512]{3,2,1,0:T(8,128)S(1)}, u32[]{:S(2)}, u32[]{:S(2)}) %collective-permute-start) | collective-permute-done | bytes 524320 | tf_op jit(solution)/shard_map/while/body/eval_jaxpr/ppermute | solution.py:36
  156.1 6.0 collective-permute-done.1
  162.2 9.0 %collective-permute-done.2 = f32[2,1,32,512]{3,2,1,0:T(8,128)S(1)} collective-permute-done((f32[2,1,32,512]{3,2,1,0:T(8,128)S(1)}, f32[2,1,32,512]{3,2,1,0:T(8,128)S(1)}, u32[]{:S(2)}, u32[]{:S(2)}) %collective-permute-start.2) | collective-permute-done | bytes 131104 | tf_op jit(solution)/shard_map/while/body/eval_jaxpr/ppermute | solution.py:26
  174.1 17.3 %collective-permute-done = f32[2,4,32,512]{3,2,1,0:T(8,128)S(1)} collective-permute-done((f32[2,4,32,512]{3,2,1,0:T(8,128)S(1)}, f32[2,4,32,512]{3,2,1,0:T(8,128)S(1)}, u32[]{:S(2)}, u32[]{:S(2)}) %collective-permute-start) | collective-permute-done | bytes 524320 | tf_op jit(solution)/shard_map/while/body/eval_jaxpr/ppermute | solution.py:36
  199.7 21.7 %collective-permute-done.2 = f32[2,1,32,512]{3,2,1,0:T(8,128)S(1)} collective-permute-done((f32[2,1,32,512]{3,2,1,0:T(8,128)S(1)}, f32[2,1,32,512]{3,2,1,0:T(8,128)S(1)}, u32[]{:S(2)}, u32[]{:S(2)}) %collective-permute-start.2) | collective-permute-done | bytes 131104 | tf_op jit(solution)/shard_map/while/body/eval_jaxpr/ppermute | solution.py:26
  224.2 23.0 %collective-permute-done = f32[2,4,32,512]{3,2,1,0:T(8,128)S(1)} collective-permute-done((f32[2,4,32,512]{3,2,1,0:T(8,128)S(1)}, f32[2,4,32,512]{3,2,1,0:T(8,128)S(1)}, u32[]{:S(2)}, u32[]{:S(2)}) %collective-permute-start) | collective-permute-done | bytes 524320 | tf_op jit(solution)/shard_map/while/body/eval_jaxpr/ppermute | solution.py:36
  253.5 7.5 collective-permute-done.1
  261.2 7.0 collective-permute-done.2
  271.0 34.3 %collective-permute-done = f32[2,4,32,512]{3,2,1,0:T(8,128)S(1)} collective-permute-done((f32[2,4,32,512]{3,2,1,0:T(8,128)S(1)}, f32[2,4,32,512]{3,2,1,0:T(8,128)S(1)}, u32[]{:S(2)}, u32[]{:S(2)}) %collective-permute-start) | collective-permute-done | bytes 524320 | tf_op jit(solution)/shard_map/while/body/eval_jaxpr/ppermute | solution.py:36
  314.4 8.9 %collective-permute-done.2 = f32[2,1,32,512]{3,2,1,0:T(8,128)S(1)} collective-permute-done((f32[2,1,32,512]{3,2,1,0:T(8,128)S(1)}, f32[2,1,32,512]{3,2,1,0:T(8,128)S(1)}, u32[]{:S(2)}, u32[]{:S(2)}) %collective-permute-start.2) | collective-permute-done | bytes 131104 | tf_op jit(solution)/shard_map/while/body/eval_jaxpr/ppermute | solution.py:26
  326.1 23.3 %collective-permute-done = f32[2,4,32,512]{3,2,1,0:T(8,128)S(1)} collective-permute-done((f32[2,4,32,512]{3,2,1,0:T(8,128)S(1)}, f32[2,4,32,512]{3,2,1,0:T(8,128)S(1)}, u32[]{:S(2)}, u32[]{:S(2)}) %collective-permute-start) | collective-permute-done | bytes 524320 | tf_op jit(solution)/shard_map/while/body/eval_jaxpr/ppermute | solution.py:36
  349.8 9.7 %collective-permute-start.1 = (f32[2,1,32,512]{3,2,1,0:T(8,128)S(1)}, f32[2,1,32,512]{3,2,1,0:T(8,128)S(1)}, u32[]{:S(2)}, u32[]{:S(2)}) collective-permute-start(f32[2,1,32,512]{3,2,1,0:T(8,128)S(1)} %get-tuple-element.275), channel_id=1, source_target_pairs={{0,1},{1,2},{2,3},{3,4},{4,5},{5,6},{6,7},{7,8},{8,9},{9,10},{10,1... | collective-permute-start | bytes 393224 | tf_op jit(solution)/shard_map/while/body/eval_jaxpr/ppermute | solution.py:24
  365.4 13.9 %collective-permute-done.2 = f32[2,1,32,512]{3,2,1,0:T(8,128)S(1)} collective-permute-done((f32[2,1,32,512]{3,2,1,0:T(8,128)S(1)}, f32[2,1,32,512]{3,2,1,0:T(8,128)S(1)}, u32[]{:S(2)}, u32[]{:S(2)}) %collective-permute-start.2) | collective-permute-done | bytes 131104 | tf_op jit(solution)/shard_map/while/body/eval_jaxpr/ppermute | solution.py:26
  382.0 17.5 %collective-permute-done = f32[2,4,32,512]{3,2,1,0:T(8,128)S(1)} collective-permute-done((f32[2,4,32,512]{3,2,1,0:T(8,128)S(1)}, f32[2,4,32,512]{3,2,1,0:T(8,128)S(1)}, u32[]{:S(2)}, u32[]{:S(2)}) %collective-permute-start) | collective-permute-done | bytes 524320 | tf_op jit(solution)/shard_map/while/body/eval_jaxpr/ppermute | solution.py:36
  410.5 9.6 %collective-permute-done.2 = f32[2,1,32,512]{3,2,1,0:T(8,128)S(1)} collective-permute-done((f32[2,1,32,512]{3,2,1,0:T(8,128)S(1)}, f32[2,1,32,512]{3,2,1,0:T(8,128)S(1)}, u32[]{:S(2)}, u32[]{:S(2)}) %collective-permute-start.2) | collective-permute-done | bytes 131104 | tf_op jit(solution)/shard_map/while/body/eval_jaxpr/ppermute | solution.py:26
  422.9 19.4 %collective-permute-done = f32[2,4,32,512]{3,2,1,0:T(8,128)S(1)} collective-permute-done((f32[2,4,32,512]{3,2,1,0:T(8,128)S(1)}, f32[2,4,32,512]{3,2,1,0:T(8,128)S(1)}, u32[]{:S(2)}, u32[]{:S(2)}) %collective-permute-start) | collective-permute-done | bytes 524320 | tf_op jit(solution)/shard_map/while/body/eval_jaxpr/ppermute | solution.py:36
  442.6 6.6 collective-permute-start.1
  453.4 15.6 %collective-permute-done.2 = f32[2,1,32,512]{3,2,1,0:T(8,128)S(1)} collective-permute-done((f32[2,1,32,512]{3,2,1,0:T(8,128)S(1)}, f32[2,1,32,512]{3,2,1,0:T(8,128)S(1)}, u32[]{:S(2)}, u32[]{:S(2)}) %collective-permute-start.2) | collective-permute-done | bytes 131104 | tf_op jit(solution)/shard_map/while/body/eval_jaxpr/ppermute | solution.py:26
  471.9 18.4 %collective-permute-done = f32[2,4,32,512]{3,2,1,0:T(8,128)S(1)} collective-permute-done((f32[2,4,32,512]{3,2,1,0:T(8,128)S(1)}, f32[2,4,32,512]{3,2,1,0:T(8,128)S(1)}, u32[]{:S(2)}, u32[]{:S(2)}) %collective-permute-start) | collective-permute-done | bytes 524320 | tf_op jit(solution)/shard_map/while/body/eval_jaxpr/ppermute | solution.py:36
  496.6 9.7 %collective-permute-done.1 = f32[2,1,32,512]{3,2,1,0:T(8,128)S(1)} collective-permute-done((f32[2,1,32,512]{3,2,1,0:T(8,128)S(1)}, f32[2,1,32,512]{3,2,1,0:T(8,128)S(1)}, u32[]{:S(2)}, u32[]{:S(2)}) %collective-permute-start.1) | collective-permute-done | bytes 131104 | tf_op jit(solution)/shard_map/while/body/eval_jaxpr/ppermute | solution.py:24
  506.5 7.9 collective-permute-done.2
  517.2 20.2 %collective-permute-done = f32[2,4,32,512]{3,2,1,0:T(8,128)S(1)} collective-permute-done((f32[2,4,32,512]{3,2,1,0:T(8,128)S(1)}, f32[2,4,32,512]{3,2,1,0:T(8,128)S(1)}, u32[]{:S(2)}, u32[]{:S(2)}) %collective-permute-start) | collective-permute-done | bytes 524320 | tf_op jit(solution)/shard_map/while/body/eval_jaxpr/ppermute | solution.py:36
  537.8 15.0 %collective-permute-start.1 = (f32[2,1,32,512]{3,2,1,0:T(8,128)S(1)}, f32[2,1,32,512]{3,2,1,0:T(8,128)S(1)}, u32[]{:S(2)}, u32[]{:S(2)}) collective-permute-start(f32[2,1,32,512]{3,2,1,0:T(8,128)S(1)} %get-tuple-element.275), channel_id=1, source_target_pairs={{0,1},{1,2},{2,3},{3,4},{4,5},{5,6},{6,7},{7,8},{8,9},{9,10},{10,1... | collective-permute-start | bytes 393224 | tf_op jit(solution)/shard_map/while/body/eval_jaxpr/ppermute | solution.py:24
  556.9 13.2 %collective-permute-done.2 = f32[2,1,32,512]{3,2,1,0:T(8,128)S(1)} collective-permute-done((f32[2,1,32,512]{3,2,1,0:T(8,128)S(1)}, f32[2,1,32,512]{3,2,1,0:T(8,128)S(1)}, u32[]{:S(2)}, u32[]{:S(2)}) %collective-permute-start.2) | collective-permute-done | bytes 131104 | tf_op jit(solution)/shard_map/while/body/eval_jaxpr/ppermute | solution.py:26
  572.9 17.5 %collective-permute-done = f32[2,4,32,512]{3,2,1,0:T(8,128)S(1)} collective-permute-done((f32[2,4,32,512]{3,2,1,0:T(8,128)S(1)}, f32[2,4,32,512]{3,2,1,0:T(8,128)S(1)}, u32[]{:S(2)}, u32[]{:S(2)}) %collective-permute-start) | collective-permute-done | bytes 524320 | tf_op jit(solution)/shard_map/while/body/eval_jaxpr/ppermute | solution.py:36
  590.7 7.9 collective-permute-start.1
  601.2 15.2 %collective-permute-done.2 = f32[2,1,32,512]{3,2,1,0:T(8,128)S(1)} collective-permute-done((f32[2,1,32,512]{3,2,1,0:T(8,128)S(1)}, f32[2,1,32,512]{3,2,1,0:T(8,128)S(1)}, u32[]{:S(2)}, u32[]{:S(2)}) %collective-permute-start.2) | collective-permute-done | bytes 131104 | tf_op jit(solution)/shard_map/while/body/eval_jaxpr/ppermute | solution.py:26
  619.3 17.5 %collective-permute-done = f32[2,4,32,512]{3,2,1,0:T(8,128)S(1)} collective-permute-done((f32[2,4,32,512]{3,2,1,0:T(8,128)S(1)}, f32[2,4,32,512]{3,2,1,0:T(8,128)S(1)}, u32[]{:S(2)}, u32[]{:S(2)}) %collective-permute-start) | collective-permute-done | bytes 524320 | tf_op jit(solution)/shard_map/while/body/eval_jaxpr/ppermute | solution.py:36
  637.2 7.8 collective-permute-start.1
  648.5 14.9 %collective-permute-done.2 = f32[2,1,32,512]{3,2,1,0:T(8,128)S(1)} collective-permute-done((f32[2,1,32,512]{3,2,1,0:T(8,128)S(1)}, f32[2,1,32,512]{3,2,1,0:T(8,128)S(1)}, u32[]{:S(2)}, u32[]{:S(2)}) %collective-permute-start.2) | collective-permute-done | bytes 131104 | tf_op jit(solution)/shard_map/while/body/eval_jaxpr/ppermute | solution.py:26
  666.2 21.9 %collective-permute-done = f32[2,4,32,512]{3,2,1,0:T(8,128)S(1)} collective-permute-done((f32[2,4,32,512]{3,2,1,0:T(8,128)S(1)}, f32[2,4,32,512]{3,2,1,0:T(8,128)S(1)}, u32[]{:S(2)}, u32[]{:S(2)}) %collective-permute-start) | collective-permute-done | bytes 524320 | tf_op jit(solution)/shard_map/while/body/eval_jaxpr/ppermute | solution.py:36
  688.5 8.4 collective-permute-start.1
  701.8 13.4 %collective-permute-done.2 = f32[2,1,32,512]{3,2,1,0:T(8,128)S(1)} collective-permute-done((f32[2,1,32,512]{3,2,1,0:T(8,128)S(1)}, f32[2,1,32,512]{3,2,1,0:T(8,128)S(1)}, u32[]{:S(2)}, u32[]{:S(2)}) %collective-permute-start.2) | collective-permute-done | bytes 131104 | tf_op jit(solution)/shard_map/while/body/eval_jaxpr/ppermute | solution.py:26
  718.0 17.3 %collective-permute-done = f32[2,4,32,512]{3,2,1,0:T(8,128)S(1)} collective-permute-done((f32[2,4,32,512]{3,2,1,0:T(8,128)S(1)}, f32[2,4,32,512]{3,2,1,0:T(8,128)S(1)}, u32[]{:S(2)}, u32[]{:S(2)}) %collective-permute-start) | collective-permute-done | bytes 524320 | tf_op jit(solution)/shard_map/while/body/eval_jaxpr/ppermute | solution.py:36
  735.7 12.0 %collective-permute-start.1 = (f32[2,1,32,512]{3,2,1,0:T(8,128)S(1)}, f32[2,1,32,512]{3,2,1,0:T(8,128)S(1)}, u32[]{:S(2)}, u32[]{:S(2)}) collective-permute-start(f32[2,1,32,512]{3,2,1,0:T(8,128)S(1)} %get-tuple-element.275), channel_id=1, source_target_pairs={{0,1},{1,2},{2,3},{3,4},{4,5},{5,6},{6,7},{7,8},{8,9},{9,10},{10,1... | collective-permute-start | bytes 393224 | tf_op jit(solution)/shard_map/while/body/eval_jaxpr/ppermute | solution.py:24
  754.8 11.3 %collective-permute-done.2 = f32[2,1,32,512]{3,2,1,0:T(8,128)S(1)} collective-permute-done((f32[2,1,32,512]{3,2,1,0:T(8,128)S(1)}, f32[2,1,32,512]{3,2,1,0:T(8,128)S(1)}, u32[]{:S(2)}, u32[]{:S(2)}) %collective-permute-start.2) | collective-permute-done | bytes 131104 | tf_op jit(solution)/shard_map/while/body/eval_jaxpr/ppermute | solution.py:26
  768.9 19.9 %collective-permute-done = f32[2,4,32,512]{3,2,1,0:T(8,128)S(1)} collective-permute-done((f32[2,4,32,512]{3,2,1,0:T(8,128)S(1)}, f32[2,4,32,512]{3,2,1,0:T(8,128)S(1)}, u32[]{:S(2)}, u32[]{:S(2)}) %collective-permute-start) | collective-permute-done | bytes 524320 | tf_op jit(solution)/shard_map/while/body/eval_jaxpr/ppermute | solution.py:36
  789.2 12.7 %collective-permute-start.1 = (f32[2,1,32,512]{3,2,1,0:T(8,128)S(1)}, f32[2,1,32,512]{3,2,1,0:T(8,128)S(1)}, u32[]{:S(2)}, u32[]{:S(2)}) collective-permute-start(f32[2,1,32,512]{3,2,1,0:T(8,128)S(1)} %get-tuple-element.275), channel_id=1, source_target_pairs={{0,1},{1,2},{2,3},{3,4},{4,5},{5,6},{6,7},{7,8},{8,9},{9,10},{10,1... | collective-permute-start | bytes 393224 | tf_op jit(solution)/shard_map/while/body/eval_jaxpr/ppermute | solution.py:24
  806.0 13.0 %collective-permute-done.2 = f32[2,1,32,512]{3,2,1,0:T(8,128)S(1)} collective-permute-done((f32[2,1,32,512]{3,2,1,0:T(8,128)S(1)}, f32[2,1,32,512]{3,2,1,0:T(8,128)S(1)}, u32[]{:S(2)}, u32[]{:S(2)}) %collective-permute-start.2) | collective-permute-done | bytes 131104 | tf_op jit(solution)/shard_map/while/body/eval_jaxpr/ppermute | solution.py:26
  821.8 17.3 %collective-permute-done = f32[2,4,32,512]{3,2,1,0:T(8,128)S(1)} collective-permute-done((f32[2,4,32,512]{3,2,1,0:T(8,128)S(1)}, f32[2,4,32,512]{3,2,1,0:T(8,128)S(1)}, u32[]{:S(2)}, u32[]{:S(2)}) %collective-permute-start) | collective-permute-done | bytes 524320 | tf_op jit(solution)/shard_map/while/body/eval_jaxpr/ppermute | solution.py:36
  846.5 11.4 %collective-permute-done.2 = f32[2,1,32,512]{3,2,1,0:T(8,128)S(1)} collective-permute-done((f32[2,1,32,512]{3,2,1,0:T(8,128)S(1)}, f32[2,1,32,512]{3,2,1,0:T(8,128)S(1)}, u32[]{:S(2)}, u32[]{:S(2)}) %collective-permute-start.2) | collective-permute-done | bytes 131104 | tf_op jit(solution)/shard_map/while/body/eval_jaxpr/ppermute | solution.py:26
  (285 shorter events, 178.7 us)
Async XLA Ops:
  19.9 15.8 %collective-permute-start.3 = (f32[2,1,32,512]{3,2,1,0:T(8,128)S(1)}, f32[2,1,32,512]{3,2,1,0:T(8,128)S(1)}, u32[]{:S(2)}, u32[]{:S(2)}) collective-permute-start(f32[2,1,32,512]{3,2,1,0:T(8,128)S(1)} %get-tuple-element.128), channel_id=1, source_target_pairs={{1,0},{2,1},{3,2},{4,3},{5,4},{6,5},{7,6},{8,7},{9,8},{10,9},{11,1... | collective-permute-start | bytes 393224 | tf_op jit(solution)/shard_map/ppermute | solution.py:26
  22.7 14.3 %collective-permute-start.4 = (f32[2,1,32,512]{3,2,1,0:T(8,128)S(1)}, f32[2,1,32,512]{3,2,1,0:T(8,128)S(1)}, u32[]{:S(2)}, u32[]{:S(2)}) collective-permute-start(f32[2,1,32,512]{3,2,1,0:T(8,128)S(1)} %get-tuple-element.129), channel_id=1, source_target_pairs={{0,1},{1,2},{2,3},{3,4},{4,5},{5,6},{6,7},{7,8},{8,9},{9,10},{10,1... | collective-permute-start | bytes 393224 | tf_op jit(solution)/shard_map/ppermute | solution.py:24
  38.4 16.0 %collective-permute-start.5 = (f32[2,1,32,512]{3,2,1,0:T(8,128)S(1)}, f32[2,1,32,512]{3,2,1,0:T(8,128)S(1)}, u32[]{:S(2)}, u32[]{:S(2)}) collective-permute-start(f32[2,1,32,512]{3,2,1,0:T(8,128)S(1)} %get-tuple-element.124), channel_id=1, source_target_pairs={{1,0},{2,1},{3,2},{4,3},{5,4},{6,5},{7,6},{8,7},{9,8},{10,9},{11,1... | collective-permute-start | bytes 393224 | tf_op jit(solution)/shard_map/ppermute | solution.py:26
  40.3 15.6 %collective-permute-start.6 = (f32[2,1,32,512]{3,2,1,0:T(8,128)S(1)}, f32[2,1,32,512]{3,2,1,0:T(8,128)S(1)}, u32[]{:S(2)}, u32[]{:S(2)}) collective-permute-start(f32[2,1,32,512]{3,2,1,0:T(8,128)S(1)} %get-tuple-element.125), channel_id=1, source_target_pairs={{0,1},{1,2},{2,3},{3,4},{4,5},{5,6},{6,7},{7,8},{8,9},{9,10},{10,1... | collective-permute-start | bytes 393224 | tf_op jit(solution)/shard_map/ppermute | solution.py:24
  57.1 16.0 %collective-permute-start.7 = (f32[2,1,32,512]{3,2,1,0:T(8,128)S(1)}, f32[2,1,32,512]{3,2,1,0:T(8,128)S(1)}, u32[]{:S(2)}, u32[]{:S(2)}) collective-permute-start(f32[2,1,32,512]{3,2,1,0:T(8,128)S(1)} %get-tuple-element.122), channel_id=1, source_target_pairs={{1,0},{2,1},{3,2},{4,3},{5,4},{6,5},{7,6},{8,7},{9,8},{10,9},{11,1... | collective-permute-start | bytes 393224 | tf_op jit(solution)/shard_map/ppermute | solution.py:26
  59.0 15.6 %collective-permute-start.8 = (f32[2,1,32,512]{3,2,1,0:T(8,128)S(1)}, f32[2,1,32,512]{3,2,1,0:T(8,128)S(1)}, u32[]{:S(2)}, u32[]{:S(2)}) collective-permute-start(f32[2,1,32,512]{3,2,1,0:T(8,128)S(1)} %get-tuple-element.123), channel_id=1, source_target_pairs={{0,1},{1,2},{2,3},{3,4},{4,5},{5,6},{6,7},{7,8},{8,9},{9,10},{10,1... | collective-permute-start | bytes 393224 | tf_op jit(solution)/shard_map/ppermute | solution.py:24
  75.8 21.6 %collective-permute-start.9 = (f32[2,1,32,512]{3,2,1,0:T(8,128)S(1)}, f32[2,1,32,512]{3,2,1,0:T(8,128)S(1)}, u32[]{:S(2)}, u32[]{:S(2)}) collective-permute-start(f32[2,1,32,512]{3,2,1,0:T(8,128)S(1)} %get-tuple-element.120), channel_id=1, source_target_pairs={{1,0},{2,1},{3,2},{4,3},{5,4},{6,5},{7,6},{8,7},{9,8},{10,9},{11,1... | collective-permute-start | bytes 393224 | tf_op jit(solution)/shard_map/ppermute | solution.py:26
  77.7 20.3 %collective-permute-start.10 = (f32[2,1,32,512]{3,2,1,0:T(8,128)S(1)}, f32[2,1,32,512]{3,2,1,0:T(8,128)S(1)}, u32[]{:S(2)}, u32[]{:S(2)}) collective-permute-start(f32[2,1,32,512]{3,2,1,0:T(8,128)S(1)} %get-tuple-element.121), channel_id=1, source_target_pairs={{0,1},{1,2},{2,3},{3,4},{4,5},{5,6},{6,7},{7,8},{8,9},{9,10},{10,1... | collective-permute-start | bytes 393224 | tf_op jit(solution)/shard_map/ppermute | solution.py:24
  98.8 31.4 %collective-permute-start.11 = (f32[2,4,32,512]{3,2,1,0:T(8,128)S(1)}, f32[2,4,32,512]{3,2,1,0:T(8,128)S(1)}, u32[]{:S(2)}, u32[]{:S(2)}) collective-permute-start(f32[2,4,32,512]{3,2,1,0:T(8,128)S(1)} %maximum_subtract_fusion), channel_id=1, source_target_pairs={{0,32},{32,64},{64,96},{96,128},{128,160},{160,192},{192,224},{224... | collective-permute-start | bytes 1572872 | tf_op jit(solution)/shard_map/ppermute | solution.py:36
  130.2 19.2 %collective-permute-start = (f32[2,4,32,512]{3,2,1,0:T(8,128)S(1)}, f32[2,4,32,512]{3,2,1,0:T(8,128)S(1)}, u32[]{:S(2)}, u32[]{:S(2)}) collective-permute-start(f32[2,4,32,512]{3,2,1,0:T(8,128)S(1)} %get-tuple-element.298), channel_id=1, source_target_pairs={{0,32},{32,64},{64,96},{96,128},{128,160},{160,192},{192,224},{224... | collective-permute-start | bytes 1572872 | tf_op jit(solution)/shard_map/while/body/eval_jaxpr/ppermute | solution.py:36
  149.8 12.3 %collective-permute-start.1 = (f32[2,1,32,512]{3,2,1,0:T(8,128)S(1)}, f32[2,1,32,512]{3,2,1,0:T(8,128)S(1)}, u32[]{:S(2)}, u32[]{:S(2)}) collective-permute-start(f32[2,1,32,512]{3,2,1,0:T(8,128)S(1)} %get-tuple-element.275), channel_id=1, source_target_pairs={{0,1},{1,2},{2,3},{3,4},{4,5},{5,6},{6,7},{7,8},{8,9},{9,10},{10,1... | collective-permute-start | bytes 393224 | tf_op jit(solution)/shard_map/while/body/eval_jaxpr/ppermute | solution.py:24
  154.1 17.1 %collective-permute-start.2 = (f32[2,1,32,512]{3,2,1,0:T(8,128)S(1)}, f32[2,1,32,512]{3,2,1,0:T(8,128)S(1)}, u32[]{:S(2)}, u32[]{:S(2)}) collective-permute-start(f32[2,1,32,512]{3,2,1,0:T(8,128)S(1)} %get-tuple-element.278), channel_id=1, source_target_pairs={{1,0},{2,1},{3,2},{4,3},{5,4},{6,5},{7,6},{8,7},{9,8},{10,9},{11,1... | collective-permute-start | bytes 393224 | tf_op jit(solution)/shard_map/while/body/eval_jaxpr/ppermute | solution.py:26
  172.1 19.2 %collective-permute-start = (f32[2,4,32,512]{3,2,1,0:T(8,128)S(1)}, f32[2,4,32,512]{3,2,1,0:T(8,128)S(1)}, u32[]{:S(2)}, u32[]{:S(2)}) collective-permute-start(f32[2,4,32,512]{3,2,1,0:T(8,128)S(1)} %get-tuple-element.298), channel_id=1, source_target_pairs={{0,32},{32,64},{64,96},{96,128},{128,160},{160,192},{192,224},{224... | collective-permute-start | bytes 1572872 | tf_op jit(solution)/shard_map/while/body/eval_jaxpr/ppermute | solution.py:36
  197.1 24.4 %collective-permute-start.2 = (f32[2,1,32,512]{3,2,1,0:T(8,128)S(1)}, f32[2,1,32,512]{3,2,1,0:T(8,128)S(1)}, u32[]{:S(2)}, u32[]{:S(2)}) collective-permute-start(f32[2,1,32,512]{3,2,1,0:T(8,128)S(1)} %get-tuple-element.278), channel_id=1, source_target_pairs={{1,0},{2,1},{3,2},{4,3},{5,4},{6,5},{7,6},{8,7},{9,8},{10,9},{11,1... | collective-permute-start | bytes 393224 | tf_op jit(solution)/shard_map/while/body/eval_jaxpr/ppermute | solution.py:26
  222.3 24.9 %collective-permute-start = (f32[2,4,32,512]{3,2,1,0:T(8,128)S(1)}, f32[2,4,32,512]{3,2,1,0:T(8,128)S(1)}, u32[]{:S(2)}, u32[]{:S(2)}) collective-permute-start(f32[2,4,32,512]{3,2,1,0:T(8,128)S(1)} %get-tuple-element.298), channel_id=1, source_target_pairs={{0,32},{32,64},{64,96},{96,128},{128,160},{160,192},{192,224},{224... | collective-permute-start | bytes 1572872 | tf_op jit(solution)/shard_map/while/body/eval_jaxpr/ppermute | solution.py:36
  247.6 13.4 %collective-permute-start.1 = (f32[2,1,32,512]{3,2,1,0:T(8,128)S(1)}, f32[2,1,32,512]{3,2,1,0:T(8,128)S(1)}, u32[]{:S(2)}, u32[]{:S(2)}) collective-permute-start(f32[2,1,32,512]{3,2,1,0:T(8,128)S(1)} %get-tuple-element.275), channel_id=1, source_target_pairs={{0,1},{1,2},{2,3},{3,4},{4,5},{5,6},{6,7},{7,8},{8,9},{9,10},{10,1... | collective-permute-start | bytes 393224 | tf_op jit(solution)/shard_map/while/body/eval_jaxpr/ppermute | solution.py:24
  249.5 18.6 %collective-permute-start.2 = (f32[2,1,32,512]{3,2,1,0:T(8,128)S(1)}, f32[2,1,32,512]{3,2,1,0:T(8,128)S(1)}, u32[]{:S(2)}, u32[]{:S(2)}) collective-permute-start(f32[2,1,32,512]{3,2,1,0:T(8,128)S(1)} %get-tuple-element.278), channel_id=1, source_target_pairs={{1,0},{2,1},{3,2},{4,3},{5,4},{6,5},{7,6},{8,7},{9,8},{10,9},{11,1... | collective-permute-start | bytes 393224 | tf_op jit(solution)/shard_map/while/body/eval_jaxpr/ppermute | solution.py:26
  269.0 36.3 %collective-permute-start = (f32[2,4,32,512]{3,2,1,0:T(8,128)S(1)}, f32[2,4,32,512]{3,2,1,0:T(8,128)S(1)}, u32[]{:S(2)}, u32[]{:S(2)}) collective-permute-start(f32[2,4,32,512]{3,2,1,0:T(8,128)S(1)} %get-tuple-element.298), channel_id=1, source_target_pairs={{0,32},{32,64},{64,96},{96,128},{128,160},{160,192},{192,224},{224... | collective-permute-start | bytes 1572872 | tf_op jit(solution)/shard_map/while/body/eval_jaxpr/ppermute | solution.py:36
  307.6 15.7 %collective-permute-start.2 = (f32[2,1,32,512]{3,2,1,0:T(8,128)S(1)}, f32[2,1,32,512]{3,2,1,0:T(8,128)S(1)}, u32[]{:S(2)}, u32[]{:S(2)}) collective-permute-start(f32[2,1,32,512]{3,2,1,0:T(8,128)S(1)} %get-tuple-element.278), channel_id=1, source_target_pairs={{1,0},{2,1},{3,2},{4,3},{5,4},{6,5},{7,6},{8,7},{9,8},{10,9},{11,1... | collective-permute-start | bytes 393224 | tf_op jit(solution)/shard_map/while/body/eval_jaxpr/ppermute | solution.py:26
  324.2 25.2 %collective-permute-start = (f32[2,4,32,512]{3,2,1,0:T(8,128)S(1)}, f32[2,4,32,512]{3,2,1,0:T(8,128)S(1)}, u32[]{:S(2)}, u32[]{:S(2)}) collective-permute-start(f32[2,4,32,512]{3,2,1,0:T(8,128)S(1)} %get-tuple-element.298), channel_id=1, source_target_pairs={{0,32},{32,64},{64,96},{96,128},{128,160},{160,192},{192,224},{224... | collective-permute-start | bytes 1572872 | tf_op jit(solution)/shard_map/while/body/eval_jaxpr/ppermute | solution.py:36
  349.8 15.4 %collective-permute-start.1 = (f32[2,1,32,512]{3,2,1,0:T(8,128)S(1)}, f32[2,1,32,512]{3,2,1,0:T(8,128)S(1)}, u32[]{:S(2)}, u32[]{:S(2)}) collective-permute-start(f32[2,1,32,512]{3,2,1,0:T(8,128)S(1)} %get-tuple-element.275), channel_id=1, source_target_pairs={{0,1},{1,2},{2,3},{3,4},{4,5},{5,6},{6,7},{7,8},{8,9},{9,10},{10,1... | collective-permute-start | bytes 393224 | tf_op jit(solution)/shard_map/while/body/eval_jaxpr/ppermute | solution.py:24
  359.5 19.7 %collective-permute-start.2 = (f32[2,1,32,512]{3,2,1,0:T(8,128)S(1)}, f32[2,1,32,512]{3,2,1,0:T(8,128)S(1)}, u32[]{:S(2)}, u32[]{:S(2)}) collective-permute-start(f32[2,1,32,512]{3,2,1,0:T(8,128)S(1)} %get-tuple-element.278), channel_id=1, source_target_pairs={{1,0},{2,1},{3,2},{4,3},{5,4},{6,5},{7,6},{8,7},{9,8},{10,9},{11,1... | collective-permute-start | bytes 393224 | tf_op jit(solution)/shard_map/while/body/eval_jaxpr/ppermute | solution.py:26
  380.1 19.4 %collective-permute-start = (f32[2,4,32,512]{3,2,1,0:T(8,128)S(1)}, f32[2,4,32,512]{3,2,1,0:T(8,128)S(1)}, u32[]{:S(2)}, u32[]{:S(2)}) collective-permute-start(f32[2,4,32,512]{3,2,1,0:T(8,128)S(1)} %get-tuple-element.298), channel_id=1, source_target_pairs={{0,32},{32,64},{64,96},{96,128},{128,160},{160,192},{192,224},{224... | collective-permute-start | bytes 1572872 | tf_op jit(solution)/shard_map/while/body/eval_jaxpr/ppermute | solution.py:36
  404.4 15.7 %collective-permute-start.2 = (f32[2,1,32,512]{3,2,1,0:T(8,128)S(1)}, f32[2,1,32,512]{3,2,1,0:T(8,128)S(1)}, u32[]{:S(2)}, u32[]{:S(2)}) collective-permute-start(f32[2,1,32,512]{3,2,1,0:T(8,128)S(1)} %get-tuple-element.278), channel_id=1, source_target_pairs={{1,0},{2,1},{3,2},{4,3},{5,4},{6,5},{7,6},{8,7},{9,8},{10,9},{11,1... | collective-permute-start | bytes 393224 | tf_op jit(solution)/shard_map/while/body/eval_jaxpr/ppermute | solution.py:26
  421.0 21.3 %collective-permute-start = (f32[2,4,32,512]{3,2,1,0:T(8,128)S(1)}, f32[2,4,32,512]{3,2,1,0:T(8,128)S(1)}, u32[]{:S(2)}, u32[]{:S(2)}) collective-permute-start(f32[2,4,32,512]{3,2,1,0:T(8,128)S(1)} %get-tuple-element.298), channel_id=1, source_target_pairs={{0,32},{32,64},{64,96},{96,128},{128,160},{160,192},{192,224},{224... | collective-permute-start | bytes 1572872 | tf_op jit(solution)/shard_map/while/body/eval_jaxpr/ppermute | solution.py:36
  449.2 19.8 %collective-permute-start.2 = (f32[2,1,32,512]{3,2,1,0:T(8,128)S(1)}, f32[2,1,32,512]{3,2,1,0:T(8,128)S(1)}, u32[]{:S(2)}, u32[]{:S(2)}) collective-permute-start(f32[2,1,32,512]{3,2,1,0:T(8,128)S(1)} %get-tuple-element.278), channel_id=1, source_target_pairs={{1,0},{2,1},{3,2},{4,3},{5,4},{6,5},{7,6},{8,7},{9,8},{10,9},{11,1... | collective-permute-start | bytes 393224 | tf_op jit(solution)/shard_map/while/body/eval_jaxpr/ppermute | solution.py:26
  469.9 20.4 %collective-permute-start = (f32[2,4,32,512]{3,2,1,0:T(8,128)S(1)}, f32[2,4,32,512]{3,2,1,0:T(8,128)S(1)}, u32[]{:S(2)}, u32[]{:S(2)}) collective-permute-start(f32[2,4,32,512]{3,2,1,0:T(8,128)S(1)} %get-tuple-element.298), channel_id=1, source_target_pairs={{0,32},{32,64},{64,96},{96,128},{128,160},{160,192},{192,224},{224... | collective-permute-start | bytes 1572872 | tf_op jit(solution)/shard_map/while/body/eval_jaxpr/ppermute | solution.py:36
  490.7 15.6 %collective-permute-start.1 = (f32[2,1,32,512]{3,2,1,0:T(8,128)S(1)}, f32[2,1,32,512]{3,2,1,0:T(8,128)S(1)}, u32[]{:S(2)}, u32[]{:S(2)}) collective-permute-start(f32[2,1,32,512]{3,2,1,0:T(8,128)S(1)} %get-tuple-element.275), channel_id=1, source_target_pairs={{0,1},{1,2},{2,3},{3,4},{4,5},{5,6},{6,7},{7,8},{8,9},{9,10},{10,1... | collective-permute-start | bytes 393224 | tf_op jit(solution)/shard_map/while/body/eval_jaxpr/ppermute | solution.py:24
  494.5 19.8 %collective-permute-start.2 = (f32[2,1,32,512]{3,2,1,0:T(8,128)S(1)}, f32[2,1,32,512]{3,2,1,0:T(8,128)S(1)}, u32[]{:S(2)}, u32[]{:S(2)}) collective-permute-start(f32[2,1,32,512]{3,2,1,0:T(8,128)S(1)} %get-tuple-element.278), channel_id=1, source_target_pairs={{1,0},{2,1},{3,2},{4,3},{5,4},{6,5},{7,6},{8,7},{9,8},{10,9},{11,1... | collective-permute-start | bytes 393224 | tf_op jit(solution)/shard_map/while/body/eval_jaxpr/ppermute | solution.py:26
  515.2 22.2 %collective-permute-start = (f32[2,4,32,512]{3,2,1,0:T(8,128)S(1)}, f32[2,4,32,512]{3,2,1,0:T(8,128)S(1)}, u32[]{:S(2)}, u32[]{:S(2)}) collective-permute-start(f32[2,4,32,512]{3,2,1,0:T(8,128)S(1)} %get-tuple-element.298), channel_id=1, source_target_pairs={{0,32},{32,64},{64,96},{96,128},{128,160},{160,192},{192,224},{224... | collective-permute-start | bytes 1572872 | tf_op jit(solution)/shard_map/while/body/eval_jaxpr/ppermute | solution.py:36
  537.8 18.9 %collective-permute-start.1 = (f32[2,1,32,512]{3,2,1,0:T(8,128)S(1)}, f32[2,1,32,512]{3,2,1,0:T(8,128)S(1)}, u32[]{:S(2)}, u32[]{:S(2)}) collective-permute-start(f32[2,1,32,512]{3,2,1,0:T(8,128)S(1)} %get-tuple-element.275), channel_id=1, source_target_pairs={{0,1},{1,2},{2,3},{3,4},{4,5},{5,6},{6,7},{7,8},{8,9},{9,10},{10,1... | collective-permute-start | bytes 393224 | tf_op jit(solution)/shard_map/while/body/eval_jaxpr/ppermute | solution.py:24
  552.8 17.2 %collective-permute-start.2 = (f32[2,1,32,512]{3,2,1,0:T(8,128)S(1)}, f32[2,1,32,512]{3,2,1,0:T(8,128)S(1)}, u32[]{:S(2)}, u32[]{:S(2)}) collective-permute-start(f32[2,1,32,512]{3,2,1,0:T(8,128)S(1)} %get-tuple-element.278), channel_id=1, source_target_pairs={{1,0},{2,1},{3,2},{4,3},{5,4},{6,5},{7,6},{8,7},{9,8},{10,9},{11,1... | collective-permute-start | bytes 393224 | tf_op jit(solution)/shard_map/while/body/eval_jaxpr/ppermute | solution.py:26
  570.9 19.4 %collective-permute-start = (f32[2,4,32,512]{3,2,1,0:T(8,128)S(1)}, f32[2,4,32,512]{3,2,1,0:T(8,128)S(1)}, u32[]{:S(2)}, u32[]{:S(2)}) collective-permute-start(f32[2,4,32,512]{3,2,1,0:T(8,128)S(1)} %get-tuple-element.298), channel_id=1, source_target_pairs={{0,32},{32,64},{64,96},{96,128},{128,160},{160,192},{192,224},{224... | collective-permute-start | bytes 1572872 | tf_op jit(solution)/shard_map/while/body/eval_jaxpr/ppermute | solution.py:36
  598.6 17.9 %collective-permute-start.2 = (f32[2,1,32,512]{3,2,1,0:T(8,128)S(1)}, f32[2,1,32,512]{3,2,1,0:T(8,128)S(1)}, u32[]{:S(2)}, u32[]{:S(2)}) collective-permute-start(f32[2,1,32,512]{3,2,1,0:T(8,128)S(1)} %get-tuple-element.278), channel_id=1, source_target_pairs={{1,0},{2,1},{3,2},{4,3},{5,4},{6,5},{7,6},{8,7},{9,8},{10,9},{11,1... | collective-permute-start | bytes 393224 | tf_op jit(solution)/shard_map/while/body/eval_jaxpr/ppermute | solution.py:26
  617.4 19.4 %collective-permute-start = (f32[2,4,32,512]{3,2,1,0:T(8,128)S(1)}, f32[2,4,32,512]{3,2,1,0:T(8,128)S(1)}, u32[]{:S(2)}, u32[]{:S(2)}) collective-permute-start(f32[2,4,32,512]{3,2,1,0:T(8,128)S(1)} %get-tuple-element.298), channel_id=1, source_target_pairs={{0,32},{32,64},{64,96},{96,128},{128,160},{160,192},{192,224},{224... | collective-permute-start | bytes 1572872 | tf_op jit(solution)/shard_map/while/body/eval_jaxpr/ppermute | solution.py:36
  637.2 11.2 %collective-permute-start.1 = (f32[2,1,32,512]{3,2,1,0:T(8,128)S(1)}, f32[2,1,32,512]{3,2,1,0:T(8,128)S(1)}, u32[]{:S(2)}, u32[]{:S(2)}) collective-permute-start(f32[2,1,32,512]{3,2,1,0:T(8,128)S(1)} %get-tuple-element.275), channel_id=1, source_target_pairs={{0,1},{1,2},{2,3},{3,4},{4,5},{5,6},{6,7},{7,8},{8,9},{9,10},{10,1... | collective-permute-start | bytes 393224 | tf_op jit(solution)/shard_map/while/body/eval_jaxpr/ppermute | solution.py:24
  645.0 18.4 %collective-permute-start.2 = (f32[2,1,32,512]{3,2,1,0:T(8,128)S(1)}, f32[2,1,32,512]{3,2,1,0:T(8,128)S(1)}, u32[]{:S(2)}, u32[]{:S(2)}) collective-permute-start(f32[2,1,32,512]{3,2,1,0:T(8,128)S(1)} %get-tuple-element.278), channel_id=1, source_target_pairs={{1,0},{2,1},{3,2},{4,3},{5,4},{6,5},{7,6},{8,7},{9,8},{10,9},{11,1... | collective-permute-start | bytes 393224 | tf_op jit(solution)/shard_map/while/body/eval_jaxpr/ppermute | solution.py:26
  664.2 23.9 %collective-permute-start = (f32[2,4,32,512]{3,2,1,0:T(8,128)S(1)}, f32[2,4,32,512]{3,2,1,0:T(8,128)S(1)}, u32[]{:S(2)}, u32[]{:S(2)}) collective-permute-start(f32[2,4,32,512]{3,2,1,0:T(8,128)S(1)} %get-tuple-element.298), channel_id=1, source_target_pairs={{0,32},{32,64},{64,96},{96,128},{128,160},{160,192},{192,224},{224... | collective-permute-start | bytes 1572872 | tf_op jit(solution)/shard_map/while/body/eval_jaxpr/ppermute | solution.py:36
  688.5 13.2 %collective-permute-start.1 = (f32[2,1,32,512]{3,2,1,0:T(8,128)S(1)}, f32[2,1,32,512]{3,2,1,0:T(8,128)S(1)}, u32[]{:S(2)}, u32[]{:S(2)}) collective-permute-start(f32[2,1,32,512]{3,2,1,0:T(8,128)S(1)} %get-tuple-element.275), channel_id=1, source_target_pairs={{0,1},{1,2},{2,3},{3,4},{4,5},{5,6},{6,7},{7,8},{8,9},{9,10},{10,1... | collective-permute-start | bytes 393224 | tf_op jit(solution)/shard_map/while/body/eval_jaxpr/ppermute | solution.py:24
  696.9 18.3 %collective-permute-start.2 = (f32[2,1,32,512]{3,2,1,0:T(8,128)S(1)}, f32[2,1,32,512]{3,2,1,0:T(8,128)S(1)}, u32[]{:S(2)}, u32[]{:S(2)}) collective-permute-start(f32[2,1,32,512]{3,2,1,0:T(8,128)S(1)} %get-tuple-element.278), channel_id=1, source_target_pairs={{1,0},{2,1},{3,2},{4,3},{5,4},{6,5},{7,6},{8,7},{9,8},{10,9},{11,1... | collective-permute-start | bytes 393224 | tf_op jit(solution)/shard_map/while/body/eval_jaxpr/ppermute | solution.py:26
  716.1 19.2 %collective-permute-start = (f32[2,4,32,512]{3,2,1,0:T(8,128)S(1)}, f32[2,4,32,512]{3,2,1,0:T(8,128)S(1)}, u32[]{:S(2)}, u32[]{:S(2)}) collective-permute-start(f32[2,4,32,512]{3,2,1,0:T(8,128)S(1)} %get-tuple-element.298), channel_id=1, source_target_pairs={{0,32},{32,64},{64,96},{96,128},{128,160},{160,192},{192,224},{224... | collective-permute-start | bytes 1572872 | tf_op jit(solution)/shard_map/while/body/eval_jaxpr/ppermute | solution.py:36
  735.7 19.0 %collective-permute-start.1 = (f32[2,1,32,512]{3,2,1,0:T(8,128)S(1)}, f32[2,1,32,512]{3,2,1,0:T(8,128)S(1)}, u32[]{:S(2)}, u32[]{:S(2)}) collective-permute-start(f32[2,1,32,512]{3,2,1,0:T(8,128)S(1)} %get-tuple-element.275), channel_id=1, source_target_pairs={{0,1},{1,2},{2,3},{3,4},{4,5},{5,6},{6,7},{7,8},{8,9},{9,10},{10,1... | collective-permute-start | bytes 393224 | tf_op jit(solution)/shard_map/while/body/eval_jaxpr/ppermute | solution.py:24
  747.7 18.5 %collective-permute-start.2 = (f32[2,1,32,512]{3,2,1,0:T(8,128)S(1)}, f32[2,1,32,512]{3,2,1,0:T(8,128)S(1)}, u32[]{:S(2)}, u32[]{:S(2)}) collective-permute-start(f32[2,1,32,512]{3,2,1,0:T(8,128)S(1)} %get-tuple-element.278), channel_id=1, source_target_pairs={{1,0},{2,1},{3,2},{4,3},{5,4},{6,5},{7,6},{8,7},{9,8},{10,9},{11,1... | collective-permute-start | bytes 393224 | tf_op jit(solution)/shard_map/while/body/eval_jaxpr/ppermute | solution.py:26
  767.0 21.8 %collective-permute-start = (f32[2,4,32,512]{3,2,1,0:T(8,128)S(1)}, f32[2,4,32,512]{3,2,1,0:T(8,128)S(1)}, u32[]{:S(2)}, u32[]{:S(2)}) collective-permute-start(f32[2,4,32,512]{3,2,1,0:T(8,128)S(1)} %get-tuple-element.298), channel_id=1, source_target_pairs={{0,32},{32,64},{64,96},{96,128},{128,160},{160,192},{192,224},{224... | collective-permute-start | bytes 1572872 | tf_op jit(solution)/shard_map/while/body/eval_jaxpr/ppermute | solution.py:36
  789.2 16.7 %collective-permute-start.1 = (f32[2,1,32,512]{3,2,1,0:T(8,128)S(1)}, f32[2,1,32,512]{3,2,1,0:T(8,128)S(1)}, u32[]{:S(2)}, u32[]{:S(2)}) collective-permute-start(f32[2,1,32,512]{3,2,1,0:T(8,128)S(1)} %get-tuple-element.275), channel_id=1, source_target_pairs={{0,1},{1,2},{2,3},{3,4},{4,5},{5,6},{6,7},{7,8},{8,9},{9,10},{10,1... | collective-permute-start | bytes 393224 | tf_op jit(solution)/shard_map/while/body/eval_jaxpr/ppermute | solution.py:24
  801.9 17.0 %collective-permute-start.2 = (f32[2,1,32,512]{3,2,1,0:T(8,128)S(1)}, f32[2,1,32,512]{3,2,1,0:T(8,128)S(1)}, u32[]{:S(2)}, u32[]{:S(2)}) collective-permute-start(f32[2,1,32,512]{3,2,1,0:T(8,128)S(1)} %get-tuple-element.278), channel_id=1, source_target_pairs={{1,0},{2,1},{3,2},{4,3},{5,4},{6,5},{7,6},{8,7},{9,8},{10,9},{11,1... | collective-permute-start | bytes 393224 | tf_op jit(solution)/shard_map/while/body/eval_jaxpr/ppermute | solution.py:26
  819.9 19.2 %collective-permute-start = (f32[2,4,32,512]{3,2,1,0:T(8,128)S(1)}, f32[2,4,32,512]{3,2,1,0:T(8,128)S(1)}, u32[]{:S(2)}, u32[]{:S(2)}) collective-permute-start(f32[2,4,32,512]{3,2,1,0:T(8,128)S(1)} %get-tuple-element.298), channel_id=1, source_target_pairs={{0,32},{32,64},{64,96},{96,128},{128,160},{160,192},{192,224},{224... | collective-permute-start | bytes 1572872 | tf_op jit(solution)/shard_map/while/body/eval_jaxpr/ppermute | solution.py:36
  842.3 15.6 %collective-permute-start.2 = (f32[2,1,32,512]{3,2,1,0:T(8,128)S(1)}, f32[2,1,32,512]{3,2,1,0:T(8,128)S(1)}, u32[]{:S(2)}, u32[]{:S(2)}) collective-permute-start(f32[2,1,32,512]{3,2,1,0:T(8,128)S(1)} %get-tuple-element.278), channel_id=1, source_target_pairs={{1,0},{2,1},{3,2},{4,3},{5,4},{6,5},{7,6},{8,7},{9,8},{10,9},{11,1... | collective-permute-start | bytes 393224 | tf_op jit(solution)/shard_map/while/body/eval_jaxpr/ppermute | solution.py:26
  (10 other events, 59.4 us)
where the time goes:
time: 861 us; the launch traced here: 860 us
  waiting for transfers between devices  582 us (68%)
  starting transfers between devices  229 us (27%)
  other arithmetic  32 us (4%)
  local copies, waits for them, and re-layouts  13.6 us (2%)
    ppermute x16, waiting for transfers between devices, shifted(): return lax.ppermute(block, axis, route)  332 us
    ppermute x19, waiting for transfers between devices, with_halo(): lax.ppermute(head, axis, [((i + 1) % count, i) for i in range(count)])  195 us
    ppermute x19, starting transfers between devices, with_halo(): lax.ppermute(tail, axis, [(i, (i + 1) % count) for i in range(count)])  156 us
    ppermute x19, waiting for transfers between devices, with_halo(): lax.ppermute(tail, axis, [(i, (i + 1) % count) for i in range(count)])  55.8 us
    ppermute x19, starting transfers between devices, with_halo(): lax.ppermute(head, axis, [((i + 1) % count, i) for i in range(count)])  42.5 us
    ppermute x16, starting transfers between devices, shifted(): return lax.ppermute(block, axis, route)  30.7 us
  transfers between devices with their start and end apart: 54, of which 54 were waited for; matrix products, arithmetic and copies ran while one was open for 0% of the time, Pallas kernels for 0%

commit v1 on v0

v1 whole, which is shorter than its diff:
```python
import jax
import jax.numpy as jnp
from jax import lax
from jax.experimental import pallas as pl
from jax.experimental.pallas import tpu as pltpu
from jax.sharding import PartitionSpec as P

M = 4
FINE_RATE = 0.025
COARSE_RATE = M * FINE_RATE
DIFFUSION = 1.5
WIDTH_SQ = 18.0
AXES = ("tm", "space")


def device(x, y, z_lo, z_hi, core):
    return (y * 4 + z_hi * 2 + core) * 32 + z_lo * 4 + x


def ring_of(x, y, core):
    return 2 * (y * 4 + (3 - x if y & 1 else x)) + core


def place(ring):
    q, core = ring >> 1, ring & 1
    y, x = q >> 2, q & 3
    return (3 - x if y & 1 else x), y, core


PLANES = [(z_lo, z_hi) for z_hi in range(2) for z_lo in range(8)]


def on_ring(ring, plane):
    x, y, core = place(ring % 32)
    return device(x, y, plane[0], plane[1], core)


PLANE_GROUPS = [[on_ring(i, plane) for i in range(32)] for plane in PLANES]
RIGHT = [(on_ring(i, plane), on_ring(i + 1, plane)) for plane in PLANES for i in range(32)]
LEFT = [(b, a) for a, b in RIGHT]
ACROSS = [(i, i ^ 2) for i in range(16)]


def row_pairs(parity):
    pairs = []
    for z_lo in range(parity, 8, 2):
        for i in range(32):
            for z_hi in range(2):
                a, b = on_ring(i, (z_lo, z_hi)), on_ring(i, ((z_lo + 1) % 8, z_hi))
                pairs += [(a, b), (b, a)]
    return pairs


def space_pairs(parity):
    pairs = []
    for s in range(parity, 32, 2):
        pairs += [(s, (s + 1) % 32), ((s + 1) % 32, s)]
    return pairs


def growth(pc, uc, pxm, pxp, pym, pyp, pzm, pzp):
    dx, dy, dz = pxp - pxm, pyp - pym, pzp - pzm
    dx, dy, dz = dx * dx, dy * dy, dz * dz
    floor = jnp.maximum(dx + dy + dz, 0.04)
    quartic = (dx * dx + dy * dy + dz * dz) / (floor * floor)
    aniso = 0.85 + 0.2 * quartic
    lap = ((pxp + pxm) + (pyp + pym)) + (pzp + pzm) - 6.0 * pc
    wet = 1.0 - pc * pc
    return aniso * aniso * lap + wet * (pc - 2.0 * uc * wet)


def block_index():
    return lax.axis_index("tm"), lax.axis_index("space")


def start_kernel(nuclei, p_in, u_in, u_start, out):
    tm, space = block_index()

    @pl.when(tm != 0)
    def _():
        out[0] = p_in[0]
        out[1] = u_in[0]

    @pl.when(tm == 0)
    def _():
        zs = lax.broadcasted_iota(jnp.int32, (8, 512), 0)
        ys = lax.broadcasted_iota(jnp.int32, (8, 512), 1)
        for g in range(4):
            sides = []
            for n in range(8):
                dy = jnp.abs(ys - nuclei[n, 2])
                dy = jnp.minimum(dy, 512 - dy)
                dz = zs + 8 * g - nuclei[n, 1]
                sides.append(dy * dy + dz * dz)
            for r in range(4):
                best = None
                for n in range(8):
                    dx = jnp.abs(space * 4 + r - nuclei[n, 0])
                    dx = jnp.minimum(dx, 128 - dx)
                    here = sides[n] + dx * dx
                    best = here if best is None else jnp.minimum(best, here)
                b = jnp.exp(-best.astype(jnp.float32) / WIDTH_SQ)
                out[0, r, 8 * g : 8 * g + 8, :] = 2.0 * b - 1.0
        out[1] = u_start[...]


def transpose_lanes(parts):
    slot = lax.broadcasted_iota(jnp.int32, (8, 128), 1) // 16
    parts = list(parts)
    for d in (4, 2, 1):
        low = (slot & d) == 0
        for a in range(8):
            if not a & d:
                top, bottom = parts[a], parts[a + d]
                parts[a] = jnp.where(low, top, pltpu.roll(bottom, 16 * d, 1))
                parts[a + d] = jnp.where(low, pltpu.roll(top, 128 - 16 * d, 1), bottom)
    return parts


def relax_kernel(start, odd, even, out, one, two, coarse):
    tm, space = block_index()
    keep = jnp.where(tm == 0, 0.0, 1.0)

    def put(buf, f, row, g, value):
        buf[f, row, 8 + 8 * g : 16 + 8 * g, :] = value
        if g == 0:
            buf[f, row, 7:8, :] = value[0:1]
        if g == 3:
            buf[f, row, 40:41, :] = value[7:8]

    def fill(before, after):
        for f in range(2):
            for part, src in enumerate((before, start, after)):
                for r in range(4):
                    for g in range(4):
                        put(one, f, 4 * part + r, g, src[f, r, 8 * g : 8 * g + 8, :])

    @pl.when(space % 2 == 0)
    def _():
        fill(odd, even)

    @pl.when(space % 2 == 1)
    def _():
        fill(even, odd)

    def one_row(src, dst, row, first):
        for g in range(4):
            at = slice(8 + 8 * g, 16 + 8 * g)
            up = slice(9 + 8 * g, 17 + 8 * g)
            down = slice(7 + 8 * g, 15 + 8 * g)
            pc, uc = src[0, row, at, :], src[1, row, at, :]
            rate = growth(
                pc, uc,
                src[0, row - 1, at, :], src[0, row + 1, at, :],
                pltpu.roll(pc, 1, 1), pltpu.roll(pc, 511, 1),
                src[0, row, down, :], src[0, row, up, :],
            )
            ulap = (
                (src[1, row - 1, at, :] + src[1, row + 1, at, :])
                + (pltpu.roll(uc, 1, 1) + pltpu.roll(uc, 511, 1))
                + (src[1, row, down, :] + src[1, row, up, :])
                - 6.0 * uc
            )
            gain = FINE_RATE * rate
            put(dst, 0, row, g, pc + gain)
            put(dst, 1, row, g, uc + (FINE_RATE * DIFFUSION) * ulap + 0.5 * gain)
            if first:
                gain = COARSE_RATE * rate
                coarse[0, row - 4, 8 * g : 8 * g + 8, :] = pc + gain
                coarse[1, row - 4, 8 * g : 8 * g + 8, :] = (
                    uc + (COARSE_RATE * DIFFUSION) * ulap + 0.5 * gain
                )

    def sweep(src, dst, lo, hi, first=False):
        @pl.loop(lo, hi)
        def _(row):
            one_row(src, dst, row, first)

    sweep(one, two, 1, 4)
    sweep(one, two, 4, 8, True)
    sweep(one, two, 8, 11)
    sweep(two, one, 2, 10)
    sweep(one, two, 3, 9)
    sweep(two, one, 4, 8)

    for f in range(2):
        for rp in range(2):
            for b in range(4):
                parts = []
                for g in range(4):
                    for rr in range(2):
                        r = 2 * rp + rr
                        lanes = slice(128 * b, 128 * b + 128)
                        fine = one[f, 4 + r, 8 + 8 * g : 16 + 8 * g, lanes]
                        parts.append(fine - keep * coarse[f, r, 8 * g : 8 * g + 8, lanes])
                for j, part in enumerate(transpose_lanes(parts)):
                    out[8 * b + j, f, rp] = part


HALO_PAIRS = (4, 3, 3, 2, 2, 1, 1, 0)
PAIR_AT = (0, 4, 7, 10, 12, 14, 15, 16)
QUADS = (8, 7, 7, 6, 6, 5, 5)
QUAD_AT = (0, 8, 15, 22, 28, 34, 39)


def lane32():
    return lax.broadcasted_iota(jnp.int32, (8, 128), 1) % 32


def piece_of(phase, own, other, first, z_hi):
    def get(slot, f, pair):
        if slot == 0 and first is not None:
            return first[f, pair]
        k = slot + 7 * phase
        x, y, core = pair // 2, k >> 2, k & 1
        i = ring_of(x, y, core) - 16 * phase
        mine = ((k >> 1) & 1) == z_hi
        return jnp.where(mine, own[i, f, pair % 2], other[i, f, pair % 2])

    return get


def edges_kernel(phase, *refs):
    if phase == 0:
        own, other, odd, even = refs
        first = None
    else:
        own, other, first, odd, even = refs
    tm, space = block_index()
    get = piece_of(phase, own, other, first, (tm // 2) % 2)
    z_odd = (space // 4) % 2 == 1
    for slot in range(7):
        n = HALO_PAIRS[slot]
        for f in range(2):
            for m in range(n):
                top, bottom = get(slot, f, m), get(slot, f, 8 - n + m)
                odd[PAIR_AT[slot] + m, f] = jnp.where(z_odd, bottom, top)
                even[PAIR_AT[slot] + m, f] = jnp.where(z_odd, top, bottom)


def rows_of(get, odd, even, z_odd, slot, f):
    n = HALO_PAIRS[slot]
    pieces = []
    for m in range(n):
        at = PAIR_AT[slot] + m
        pieces.append(jnp.where(z_odd, even[at, f], odd[at, f]))
    pieces += [get(slot, f, pair) for pair in range(8)]
    for m in range(n):
        at = PAIR_AT[slot] + m
        pieces.append(jnp.where(z_odd, odd[at, f], even[at, f]))
    rows = []
    for piece in pieces:
        rows += [pltpu.roll(piece, 8, 1), pltpu.roll(piece, 120, 1)]
    return rows


def lanes_kernel(phase, *refs):
    if phase == 0:
        own, other, odd, even, right, left = refs
        first = None
    else:
        own, other, first, odd, even, right, left = refs
    tm, space = block_index()
    get = piece_of(phase, own, other, first, (tm // 2) % 2)
    z_odd = (space // 4) % 2 == 1
    part = lane32() // 8
    for slot in range(7):
        for f in range(2):
            rows = rows_of(get, odd, even, z_odd, slot, f)
            for a in range(QUADS[slot]):
                r_edge = l_edge = None
                for q in range(4):
                    row = rows[4 * a + q]
                    r_part = pltpu.roll(row, (8 * q - 16) % 128, 1) if q != 2 else row
                    l_part = pltpu.roll(row, (8 * q - 8) % 128, 1) if q != 1 else row
                    if q == 0:
                        r_edge, l_edge = r_part, l_part
                    else:
                        r_edge = jnp.where(part == q, r_part, r_edge)
                        l_edge = jnp.where(part == q, l_part, l_edge)
                right[QUAD_AT[slot] + a, f] = r_edge
                left[QUAD_AT[slot] + a, f] = l_edge


def chain_kernel(phase, *refs):
    if phase == 0:
        own, other, odd, even, from_left, from_right, out, last, state, taus = refs
        first = before = None
    else:
        own, other, first, odd, even, from_left, from_right, before, out, state, taus = refs
    tm, space = block_index()
    z_hi = (tm // 2) % 2
    get = piece_of(phase, own, other, first, z_hi)
    z_odd = (space // 4) % 2 == 1
    lane = lane32()
    part = lane // 8
    for slot in range(8):
        n = HALO_PAIRS[slot]
        for f in range(2):
            rows = rows_of(get, odd, even, z_odd, slot, f)
            for index, row in enumerate(rows):
                if slot < 7:
                    at, q = QUAD_AT[slot] + index // 4, index % 4
                    l_halo, r_halo = from_left[at, f], from_right[at, f]
                    if q != 0:
                        l_halo = pltpu.roll(l_halo, 128 - 8 * q, 1)
                    if q != 3:
                        r_halo = pltpu.roll(r_halo, 24 - 8 * q, 1)
                    row = jnp.where(part == 0, l_halo, jnp.where(part == 3, r_halo, row))
                if slot == 0:
                    state[0, f, 8 - 2 * n + index] = row
                else:
                    taus[slot - 1, f, 8 - 2 * n + index] = row

    def emit(k, pair, f, piece):
        x, y, core = pair // 2, k >> 2, k & 1
        out[ring_of(x, y, core), f, pair % 2] = piece

    offset = 0 if phase == 0 else 7
    if phase == 1:
        for i in range(16):
            out[i] = before[i]
    for f in range(2):
        for pair in range(8):
            if phase == 0:
                emit(0, pair, f, get(0, f, pair))

                @pl.when(z_hi == 0)
                def _(f=f, pair=pair):
                    emit(1, pair, f, get(0, f, pair))

            else:

                @pl.when(z_hi == 0)
                def _(f=f, pair=pair):
                    emit(8, pair, f, first[f, pair])

    sub = lax.broadcasted_iota(jnp.int32, (4, 8, 128), 1)
    lanes = lax.broadcasted_iota(jnp.int32, (4, 8, 128), 2)
    is_top, is_bottom = sub == 7, sub == 0
    end_up = is_top & (lanes >= 96)
    end_down = is_bottom & (lanes < 32)

    def z_up(v):
        w = jnp.where(is_bottom, pltpu.roll(v, 96, 2), v)
        return jnp.where(end_up, v, pltpu.roll(w, 7, 1))

    def z_down(v):
        w = jnp.where(is_top, pltpu.roll(v, 32, 2), v)
        return jnp.where(end_down, v, pltpu.roll(w, 1, 1))

    for j in range(1, 8):
        src, dst = (j + 1) % 2, j % 2
        lo, hi = 8 - (7 - j), 24 + (7 - j)
        starts = list(range(lo, hi - 3, 4))
        if starts[-1] + 4 < hi:
            starts.append(hi - 4)
        for r in starts:
            pc, uc = state[src, 0, r : r + 4], state[src, 1, r : r + 4]
            rate = growth(
                pc, uc,
                state[src, 0, r - 1 : r + 3], state[src, 0, r + 1 : r + 5],
                pltpu.roll(pc, 1, 2), pltpu.roll(pc, 127, 2),
                z_down(pc), z_up(pc),
            )
            ulap = (
                (state[src, 1, r - 1 : r + 3] + state[src, 1, r + 1 : r + 5])
                + (pltpu.roll(uc, 1, 2) + pltpu.roll(uc, 127, 2))
                + (z_down(uc) + z_up(uc))
                - 6.0 * uc
            )
            gain = COARSE_RATE * rate
            state[dst, 0, r : r + 4] = pc + gain + taus[j - 1, 0, r : r + 4]
            state[dst, 1, r : r + 4] = (
                uc + (COARSE_RATE * DIFFUSION) * ulap + 0.5 * gain + taus[j - 1, 1, r : r + 4]
            )
        k = 1 + offset + j

        def pack(f, pair, dst=dst):
            low, high = state[dst, f, 8 + 2 * pair], state[dst, f, 9 + 2 * pair]
            return jnp.where(lane < 16, pltpu.roll(low, 120, 1), pltpu.roll(high, 8, 1))

        if phase == 0 and j == 7:
            for f in range(2):
                for pair in range(8):
                    last[f, pair] = pack(f, pair)
        else:

            @pl.when(z_hi == ((k >> 1) & 1))
            def _(k=k, pack=pack):
                for f in range(2):
                    for pair in range(8):
                        emit(k, pair, f, pack(f, pair))


def finish_kernel(start, got, p_out, u_out):
    tm, _ = block_index()

    @pl.when(tm == 0)
    def _():
        p_out[0] = start[0]
        u_out[0] = start[1]

    @pl.when(tm != 0)
    def _():
        for f, out in enumerate((p_out, u_out)):
            for rp in range(2):
                for b in range(4):
                    parts = transpose_lanes([got[8 * b + j, f, rp] for j in range(8)])
                    for g in range(4):
                        for rr in range(2):
                            at = slice(8 * g, 8 * g + 8), slice(128 * b, 128 * b + 128)
                            out[0, 2 * rp + rr, at[0], at[1]] = parts[2 * g + rr]


VMEM = pl.BlockSpec(memory_space=pltpu.VMEM)
SMEM = pl.BlockSpec(memory_space=pltpu.SMEM)


def call(kernel, outs, args, scratch=(), specs=None):
    shapes = [jax.ShapeDtypeStruct(s, jnp.float32) for s in outs]
    return pl.pallas_call(
        kernel,
        out_shape=shapes if len(shapes) > 1 else shapes[0],
        in_specs=specs or [VMEM] * len(args),
        out_specs=[VMEM] * len(shapes) if len(shapes) > 1 else VMEM,
        scratch_shapes=[pltpu.VMEM(s, jnp.float32) for s in scratch],
        compiler_params=pltpu.CompilerParams(vmem_limit_bytes=40 * 1024 * 1024),
    )(*args)


def exchange_rows(payload, axis, pairs):
    odd, even = payload
    got_odd = lax.ppermute(odd, axis, pairs(1))
    got_even = lax.ppermute(even, axis, pairs(0))
    return got_odd, got_even


def local(phase_guess, solute_guess, solute_start, nuclei):
    start = call(
        start_kernel,
        [(2, 4, 32, 512)],
        [nuclei, phase_guess, solute_guess, solute_start],
        specs=[SMEM, VMEM, VMEM, VMEM],
    )
    odd, even = exchange_rows((start, start), "space", space_pairs)
    packed = call(
        relax_kernel,
        [(32, 2, 2, 8, 128)],
        [start, odd, even],
        scratch=[(2, 12, 48, 512), (2, 12, 48, 512), (2, 4, 32, 512)],
    )
    own = lax.all_to_all(packed, AXES, 0, 0, tiled=True, axis_index_groups=PLANE_GROUPS)
    owns = own[:16], own[16:]
    others = [lax.ppermute(part, "tm", ACROSS) for part in owns]

    first, before = [], []
    for phase in range(2):
        known = [owns[phase], others[phase]] + first
        edges = call(
            lambda *refs, phase=phase: edges_kernel(phase, *refs), [(16, 2, 8, 128)] * 2, known
        )
        known += exchange_rows(edges, AXES, row_pairs)
        right, left = call(
            lambda *refs, phase=phase: lanes_kernel(phase, *refs), [(44, 2, 8, 128)] * 2, known
        )
        known += [lax.ppermute(right, AXES, RIGHT), lax.ppermute(left, AXES, LEFT)]
        outs = [(32, 2, 2, 8, 128)] if phase else [(16, 2, 2, 8, 128), (2, 8, 8, 128)]
        got = call(
            lambda *refs, phase=phase: chain_kernel(phase, *refs),
            outs,
            known + before,
            scratch=[(2, 2, 32, 8, 128), (7, 2, 32, 8, 128)],
        )
        if phase == 0:
            before, first = [got[0]], [got[1]]
    back = lax.all_to_all(got, AXES, 0, 0, tiled=True, axis_index_groups=PLANE_GROUPS)
    return call(finish_kernel, [(1, 4, 32, 512)] * 2, [start, back])


def solution(mesh):
    return jax.shard_map(
        lambda *args: tuple(local(*args)),
        mesh=mesh,
        in_specs=(
            P("tm", "space", None, None),
            P("tm", "space", None, None),
            P("space", None, None),
            P(),
        ),
        out_specs=(P("tm", "space", None, None), P("tm", "space", None, None)),
        check_vma=False,
    )
```

time: 861 us -> 195 us (0.23)
  the two profiles are of different devices: /device:TPU:502 before, /device:TPU:1 now
where the time goes in v1:
time: 195 us; the launch traced here: 194 us
  waiting for transfers between devices  78.7 us (40%)
  starting transfers between devices  57 us (29%)
  blocking collectives  34.8 us (18%)
  Pallas kernels  19.3 us (10%)
  local copies, waits for them, and re-layouts  3.64 us (2%)
    ppermute x2, waiting for transfers between devices, local(): others = [lax.ppermute(part, 'tm', ACROSS) for part in owns]  40.4 us
    ppermute x3, starting transfers between devices, exchange_rows(): got_odd = lax.ppermute(odd, axis, pairs(1))  29.4 us
    pallas_call x9, Pallas kernels, call(): pl.pallas_call(kernel, out_shape=shapes if len(shapes) > 1 else shapes[0]...  19.3 us
    all_to_all x1, blocking collectives, local(): lax.all_to_all(packed, AXES, 0, 0, tiled=True, axis_index_groups=PLANE_GR...  18.1 us
    all_to_all x1, blocking collectives, local(): lax.all_to_all(got, AXES, 0, 0, tiled=True, axis_index_groups=PLANE_GROUPS)  16.7 us
    ppermute x3, waiting for transfers between devices, exchange_rows(): got_odd = lax.ppermute(odd, axis, pairs(1))  16.1 us
    ppermute x2, starting transfers between devices, local(): others = [lax.ppermute(part, 'tm', ACROSS) for part in owns]  12.3 us
    ppermute x3, waiting for transfers between devices, exchange_rows(): got_even = lax.ppermute(even, axis, pairs(0))  11.8 us
  transfers between devices with their start and end apart: 12, of which 11 were waited for; matrix products, arithmetic and copies ran while one was open for 0% of the time, Pallas kernels for 2%

profile of v1, /device:TPU:1, one launch (start us, length us, event | category | flops | bytes accessed | tf_op | source)
XLA Modules:
  0.0 194.2 jit_solution(10796615240020380404)
XLA Ops:
  0.6 0.8 copy.6.nuclei
  1.4 0.0 copy-start
  1.4 0.9 copy-done
  2.3 0.0 copy-start.1
  2.3 0.9 copy-done.1
  3.3 0.0 copy-start.2
  3.3 0.9 copy-done.2
  4.2 0.6 shard_map.59.start
  4.9 15.9 %collective-permute-start = (f32[2,4,32,512]{3,2,1,0:T(8,128)S(1)}, f32[2,4,32,512]{3,2,1,0:T(8,128)S(1)}, u32[]{:S(2)}, u32[]{:S(2)}) collective-permute-start(f32[2,4,32,512]{3,2,1,0:T(8,128)S(1)} %shard_map.59.start), channel_id=1, source_target_pairs={{1,2},{2,1},{3,4},{4,3},{5,6},{6,5},{7,8},{8,7},{9,10},{10,9},{11,... | collective-permute-start | bytes 1572872 | tf_op jit(solution)/shard_map/ppermute | solution.py:434
  20.8 1.9 collective-permute-start.1
  22.7 8.2 %collective-permute-done.odd = f32[2,4,32,512]{3,2,1,0:T(8,128)S(1)} collective-permute-done((f32[2,4,32,512]{3,2,1,0:T(8,128)S(1)}, f32[2,4,32,512]{3,2,1,0:T(8,128)S(1)}, u32[]{:S(2)}, u32[]{:S(2)}) %collective-permute-start) | collective-permute-done | bytes 524320 | tf_op jit(solution)/shard_map/ppermute | solution.py:434
  30.9 3.8 %collective-permute-done.1.even = f32[2,4,32,512]{3,2,1,0:T(8,128)S(1)} collective-permute-done((f32[2,4,32,512]{3,2,1,0:T(8,128)S(1)}, f32[2,4,32,512]{3,2,1,0:T(8,128)S(1)}, u32[]{:S(2)}, u32[]{:S(2)}) %collective-permute-start.1) | collective-permute-done | bytes 524320 | tf_op jit(solution)/shard_map/ppermute | solution.py:435
  34.7 6.7 %shard_map.60 = f32[32,2,2,8,128]{4,3,2,1,0:T(8,128)S(1)} custom-call(f32[2,4,32,512]{3,2,1,0:T(8,128)S(1)} %shard_map.59.start, f32[2,4,32,512]{3,2,1,0:T(8,128)S(1)} %collective-permute-done.odd, f32[2,4,32,512]{3,2,1,0:T(8,128)S(1)} %collective-permute-done.1.even), custom_call_target="tpu_custom_call" | custom-call | tf_op jit(solution)/shard_map/pallas_call | solution.py:422
  41.4 18.1 %all_to_all.10 = f32[32,2,2,8,128]{4,3,2,1,0:T(8,128)S(1)} all-to-all(f32[32,2,2,8,128]{4,3,2,1,0:T(8,128)S(1)} %shard_map.60), channel_id=1, replica_groups={{0,32,1,33,2,34,3,35,131,163,130,162,129,161,128,160,256,288,257,289,25..., dimensions={0} | all-to-all | bytes 1048576 | tf_op jit(solution)/shard_map/all_to_all | solution.py:453
  59.6 9.1 %collective-permute-start.3 = (f32[16,2,2,8,128]{4,3,2,1,0:T(8,128)S(1)}, f32[16,2,2,8,128]{4,3,2,1,0:T(8,128)S(1)}, u32[]{:S(2)}, u32[]{:S(2)}) collective-permute-start(f32[16,2,2,8,128]{4,3,2,1,0:T(8,128)S(1)} %get-tuple-element.22.refs_0_), channel_id=1, source_target_pairs={{0,64},{32,96},{64,0},{96,32},{128,192},{160,224},{192,128},{224,1... | collective-permute-start | bytes 786440 | tf_op jit(solution)/shard_map/ppermute | solution.py:455
  68.7 25.6 %collective-permute-done.3.refs_1_ = f32[16,2,2,8,128]{4,3,2,1,0:T(8,128)S(1)} collective-permute-done((f32[16,2,2,8,128]{4,3,2,1,0:T(8,128)S(1)}, f32[16,2,2,8,128]{4,3,2,1,0:T(8,128)S(1)}, u32[]{:S(2)}, u32[]{:S(2)}) %collective-permute-start.3) | collective-permute-done | bytes 262176 | tf_op jit(solution)/shard_map/ppermute | solution.py:455
  94.3 6.7 %collective-permute-start.4 = (f32[16,2,8,128]{3,2,1,0:T(8,128)S(1)}, f32[16,2,8,128]{3,2,1,0:T(8,128)S(1)}, u32[]{:S(2)}, u32[]{:S(2)}) collective-permute-start(f32[16,2,8,128]{3,2,1,0:T(8,128)S(1)} %get-tuple-element.12), channel_id=1, source_target_pairs={{4,8},{8,4},{68,72},{72,68},{36,40},{40,36},{100,104},{104,100},{5... | collective-permute-start | bytes 393224 | tf_op jit(solution)/shard_map/ppermute | solution.py:434
  101.0 1.9 collective-permute-start.5
  102.9 4.3 %collective-permute-done.4.refs_2_ = f32[16,2,8,128]{3,2,1,0:T(8,128)S(1)} collective-permute-done((f32[16,2,8,128]{3,2,1,0:T(8,128)S(1)}, f32[16,2,8,128]{3,2,1,0:T(8,128)S(1)}, u32[]{:S(2)}, u32[]{:S(2)}) %collective-permute-start.4) | collective-permute-done | bytes 131104 | tf_op jit(solution)/shard_map/ppermute | solution.py:434
  107.2 3.8 %collective-permute-done.5.refs_3_ = f32[16,2,8,128]{3,2,1,0:T(8,128)S(1)} collective-permute-done((f32[16,2,8,128]{3,2,1,0:T(8,128)S(1)}, f32[16,2,8,128]{3,2,1,0:T(8,128)S(1)}, u32[]{:S(2)}, u32[]{:S(2)}) %collective-permute-start.5) | collective-permute-done | bytes 131104 | tf_op jit(solution)/shard_map/ppermute | solution.py:435
  111.0 1.5 shard_map.62
  112.6 2.9 %collective-permute-start.6 = (f32[44,2,8,128]{3,2,1,0:T(8,128)S(1)}, f32[44,2,8,128]{3,2,1,0:T(8,128)S(1)}, u32[]{:S(2)}, u32[]{:S(2)}) collective-permute-start(f32[44,2,8,128]{3,2,1,0:T(8,128)S(1)} %get-tuple-element.14), channel_id=1, source_target_pairs={{0,32},{32,1},{1,33},{33,2},{2,34},{34,3},{3,35},{35,131},{131,163... | collective-permute-start | bytes 1081352 | tf_op jit(solution)/shard_map/ppermute | solution.py:467
  115.5 1.9 collective-permute-start.7
  117.4 3.2 %collective-permute-start.2 = (f32[16,2,2,8,128]{4,3,2,1,0:T(8,128)S(1)}, f32[16,2,2,8,128]{4,3,2,1,0:T(8,128)S(1)}, u32[]{:S(2)}, u32[]{:S(2)}) collective-permute-start(f32[16,2,2,8,128]{4,3,2,1,0:T(8,128)S(1)} %get-tuple-element.23.refs_0_), channel_id=1, source_target_pairs={{0,64},{32,96},{64,0},{96,32},{128,192},{160,224},{192,128},{224,1... | collective-permute-start | bytes 786440 | tf_op jit(solution)/shard_map/ppermute | solution.py:455
  120.6 0.0 collective-permute-done.6.refs_4_
  120.7 3.5 %collective-permute-done.7.refs_5_ = f32[44,2,8,128]{3,2,1,0:T(8,128)S(1)} collective-permute-done((f32[44,2,8,128]{3,2,1,0:T(8,128)S(1)}, f32[44,2,8,128]{3,2,1,0:T(8,128)S(1)}, u32[]{:S(2)}, u32[]{:S(2)}) %collective-permute-start.7) | collective-permute-done | bytes 360480 | tf_op jit(solution)/shard_map/ppermute | solution.py:467
  124.2 3.2 %shard_map.63 = (f32[16,2,2,8,128]{4,3,2,1,0:T(8,128)S(1)}, f32[2,8,8,128]{3,2,1,0:T(8,128)S(1)}) custom-call(f32[16,2,2,8,128]{4,3,2,1,0:T(8,128)S(1)} %get-tuple-element.22.refs_0_, f32[16,2,2,8,128]{4,3,2,1,0:T(8,128)S(1)} %collective-permute-done.3.refs_1_, f32[16,2,8,128]{3,2,1,0:T(8,128)S(1)} %collective-permute-done.4.refs_2_, ...), custom_call_target="tpu_custom_call" | custom-call | tf_op jit(solution)/shard_map/pallas_call | solution.py:422
  127.4 14.9 %collective-permute-done.2.refs_1_ = f32[16,2,2,8,128]{4,3,2,1,0:T(8,128)S(1)} collective-permute-done((f32[16,2,2,8,128]{4,3,2,1,0:T(8,128)S(1)}, f32[16,2,2,8,128]{4,3,2,1,0:T(8,128)S(1)}, u32[]{:S(2)}, u32[]{:S(2)}) %collective-permute-start.2) | collective-permute-done | bytes 262176 | tf_op jit(solution)/shard_map/ppermute | solution.py:455
  142.4 6.9 %collective-permute-start.8 = (f32[16,2,8,128]{3,2,1,0:T(8,128)S(1)}, f32[16,2,8,128]{3,2,1,0:T(8,128)S(1)}, u32[]{:S(2)}, u32[]{:S(2)}) collective-permute-start(f32[16,2,8,128]{3,2,1,0:T(8,128)S(1)} %get-tuple-element.17), channel_id=1, source_target_pairs={{4,8},{8,4},{68,72},{72,68},{36,40},{40,36},{100,104},{104,100},{5... | collective-permute-start | bytes 393224 | tf_op jit(solution)/shard_map/ppermute | solution.py:434
  149.2 1.9 collective-permute-start.9
  151.1 3.6 %collective-permute-done.8.refs_3_ = f32[16,2,8,128]{3,2,1,0:T(8,128)S(1)} collective-permute-done((f32[16,2,8,128]{3,2,1,0:T(8,128)S(1)}, f32[16,2,8,128]{3,2,1,0:T(8,128)S(1)}, u32[]{:S(2)}, u32[]{:S(2)}) %collective-permute-start.8) | collective-permute-done | bytes 131104 | tf_op jit(solution)/shard_map/ppermute | solution.py:434
  154.8 4.1 %collective-permute-done.9.refs_4_ = f32[16,2,8,128]{3,2,1,0:T(8,128)S(1)} collective-permute-done((f32[16,2,8,128]{3,2,1,0:T(8,128)S(1)}, f32[16,2,8,128]{3,2,1,0:T(8,128)S(1)}, u32[]{:S(2)}, u32[]{:S(2)}) %collective-permute-start.9) | collective-permute-done | bytes 131104 | tf_op jit(solution)/shard_map/ppermute | solution.py:435
  158.9 1.5 shard_map.65
  160.4 2.8 %collective-permute-start.10 = (f32[44,2,8,128]{3,2,1,0:T(8,128)S(1)}, f32[44,2,8,128]{3,2,1,0:T(8,128)S(1)}, u32[]{:S(2)}, u32[]{:S(2)}) collective-permute-start(f32[44,2,8,128]{3,2,1,0:T(8,128)S(1)} %get-tuple-element.19), channel_id=1, source_target_pairs={{0,32},{32,1},{1,33},{33,2},{2,34},{34,3},{3,35},{35,131},{131,163... | collective-permute-start | bytes 1081352 | tf_op jit(solution)/shard_map/ppermute | solution.py:467
  163.2 1.9 collective-permute-start.11
  165.2 2.4 %collective-permute-done.10.refs_5_ = f32[44,2,8,128]{3,2,1,0:T(8,128)S(1)} collective-permute-done((f32[44,2,8,128]{3,2,1,0:T(8,128)S(1)}, f32[44,2,8,128]{3,2,1,0:T(8,128)S(1)}, u32[]{:S(2)}, u32[]{:S(2)}) %collective-permute-start.10) | collective-permute-done | bytes 360480 | tf_op jit(solution)/shard_map/ppermute | solution.py:467
  167.6 4.4 %collective-permute-done.11.refs_6_ = f32[44,2,8,128]{3,2,1,0:T(8,128)S(1)} collective-permute-done((f32[44,2,8,128]{3,2,1,0:T(8,128)S(1)}, f32[44,2,8,128]{3,2,1,0:T(8,128)S(1)}, u32[]{:S(2)}, u32[]{:S(2)}) %collective-permute-start.11) | collective-permute-done | bytes 360480 | tf_op jit(solution)/shard_map/ppermute | solution.py:467
  172.0 3.2 %shard_map.66 = f32[32,2,2,8,128]{4,3,2,1,0:T(8,128)S(1)} custom-call(f32[16,2,2,8,128]{4,3,2,1,0:T(8,128)S(1)} %get-tuple-element.23.refs_0_, f32[16,2,2,8,128]{4,3,2,1,0:T(8,128)S(1)} %collective-permute-done.2.refs_1_, f32[2,8,8,128]{3,2,1,0:T(8,128)S(1)} %get-tuple-element.16.refs_2_, f32[16,2,8,128]{3,2,1,0:T(8,128)S(1)} %collective-permute-done.8.refs_3_, ...), custom_call_target="tpu_custom_call" | custom-call | tf_op jit(solution)/shard_map/pallas_call | solution.py:422
  175.2 16.7 %all_to_all.11.got = f32[32,2,2,8,128]{4,3,2,1,0:T(8,128)S(1)} all-to-all(f32[32,2,2,8,128]{4,3,2,1,0:T(8,128)S(1)} %shard_map.66), channel_id=1, replica_groups={{0,32,1,33,2,34,3,35,131,163,130,162,129,161,128,160,256,288,257,289,25..., dimensions={0} | all-to-all | bytes 1048576 | tf_op jit(solution)/shard_map/all_to_all | solution.py:477
  191.9 2.3 %shard_map.67 = (f32[1,4,32,512]{3,2,1,0:T(8,128)}, f32[1,4,32,512]{3,2,1,0:T(8,128)}) custom-call(f32[2,4,32,512]{3,2,1,0:T(8,128)S(1)} %shard_map.59.start, f32[32,2,2,8,128]{4,3,2,1,0:T(8,128)S(1)} %all_to_all.11.got), custom_call_target="tpu_custom_call" | custom-call | tf_op jit(solution)/shard_map/pallas_call | solution.py:422
  (3 shorter events, 0.1 us)
Async XLA Ops:
  1.4 0.9 copy-start
  2.3 0.9 copy-start.1
  3.3 0.9 copy-start.2
  4.9 26.0 %collective-permute-start = (f32[2,4,32,512]{3,2,1,0:T(8,128)S(1)}, f32[2,4,32,512]{3,2,1,0:T(8,128)S(1)}, u32[]{:S(2)}, u32[]{:S(2)}) collective-permute-start(f32[2,4,32,512]{3,2,1,0:T(8,128)S(1)} %shard_map.59.start), channel_id=1, source_target_pairs={{1,2},{2,1},{3,4},{4,3},{5,6},{6,5},{7,8},{8,7},{9,10},{10,9},{11,... | collective-permute-start | bytes 1572872 | tf_op jit(solution)/shard_map/ppermute | solution.py:434
  20.8 13.9 %collective-permute-start.1 = (f32[2,4,32,512]{3,2,1,0:T(8,128)S(1)}, f32[2,4,32,512]{3,2,1,0:T(8,128)S(1)}, u32[]{:S(2)}, u32[]{:S(2)}) collective-permute-start(f32[2,4,32,512]{3,2,1,0:T(8,128)S(1)} %shard_map.59.start), channel_id=1, source_target_pairs={{0,1},{1,0},{2,3},{3,2},{4,5},{5,4},{6,7},{7,6},{8,9},{9,8},{10,11... | collective-permute-start | bytes 1572872 | tf_op jit(solution)/shard_map/ppermute | solution.py:435
  59.6 34.7 %collective-permute-start.3 = (f32[16,2,2,8,128]{4,3,2,1,0:T(8,128)S(1)}, f32[16,2,2,8,128]{4,3,2,1,0:T(8,128)S(1)}, u32[]{:S(2)}, u32[]{:S(2)}) collective-permute-start(f32[16,2,2,8,128]{4,3,2,1,0:T(8,128)S(1)} %get-tuple-element.22.refs_0_), channel_id=1, source_target_pairs={{0,64},{32,96},{64,0},{96,32},{128,192},{160,224},{192,128},{224,1... | collective-permute-start | bytes 786440 | tf_op jit(solution)/shard_map/ppermute | solution.py:455
  94.3 12.9 %collective-permute-start.4 = (f32[16,2,8,128]{3,2,1,0:T(8,128)S(1)}, f32[16,2,8,128]{3,2,1,0:T(8,128)S(1)}, u32[]{:S(2)}, u32[]{:S(2)}) collective-permute-start(f32[16,2,8,128]{3,2,1,0:T(8,128)S(1)} %get-tuple-element.12), channel_id=1, source_target_pairs={{4,8},{8,4},{68,72},{72,68},{36,40},{40,36},{100,104},{104,100},{5... | collective-permute-start | bytes 393224 | tf_op jit(solution)/shard_map/ppermute | solution.py:434
  101.0 10.1 %collective-permute-start.5 = (f32[16,2,8,128]{3,2,1,0:T(8,128)S(1)}, f32[16,2,8,128]{3,2,1,0:T(8,128)S(1)}, u32[]{:S(2)}, u32[]{:S(2)}) collective-permute-start(f32[16,2,8,128]{3,2,1,0:T(8,128)S(1)} %get-tuple-element.13), channel_id=1, source_target_pairs={{0,4},{4,0},{64,68},{68,64},{32,36},{36,32},{96,100},{100,96},{1,5... | collective-permute-start | bytes 393224 | tf_op jit(solution)/shard_map/ppermute | solution.py:435
  112.6 8.1 %collective-permute-start.6 = (f32[44,2,8,128]{3,2,1,0:T(8,128)S(1)}, f32[44,2,8,128]{3,2,1,0:T(8,128)S(1)}, u32[]{:S(2)}, u32[]{:S(2)}) collective-permute-start(f32[44,2,8,128]{3,2,1,0:T(8,128)S(1)} %get-tuple-element.14), channel_id=1, source_target_pairs={{0,32},{32,1},{1,33},{33,2},{2,34},{34,3},{3,35},{35,131},{131,163... | collective-permute-start | bytes 1081352 | tf_op jit(solution)/shard_map/ppermute | solution.py:467
  115.5 8.7 %collective-permute-start.7 = (f32[44,2,8,128]{3,2,1,0:T(8,128)S(1)}, f32[44,2,8,128]{3,2,1,0:T(8,128)S(1)}, u32[]{:S(2)}, u32[]{:S(2)}) collective-permute-start(f32[44,2,8,128]{3,2,1,0:T(8,128)S(1)} %get-tuple-element.15), channel_id=1, source_target_pairs={{32,0},{1,32},{33,1},{2,33},{34,2},{3,34},{35,3},{131,35},{163,131... | collective-permute-start | bytes 1081352 | tf_op jit(solution)/shard_map/ppermute | solution.py:467
  117.4 24.9 %collective-permute-start.2 = (f32[16,2,2,8,128]{4,3,2,1,0:T(8,128)S(1)}, f32[16,2,2,8,128]{4,3,2,1,0:T(8,128)S(1)}, u32[]{:S(2)}, u32[]{:S(2)}) collective-permute-start(f32[16,2,2,8,128]{4,3,2,1,0:T(8,128)S(1)} %get-tuple-element.23.refs_0_), channel_id=1, source_target_pairs={{0,64},{32,96},{64,0},{96,32},{128,192},{160,224},{192,128},{224,1... | collective-permute-start | bytes 786440 | tf_op jit(solution)/shard_map/ppermute | solution.py:455
  142.4 12.4 %collective-permute-start.8 = (f32[16,2,8,128]{3,2,1,0:T(8,128)S(1)}, f32[16,2,8,128]{3,2,1,0:T(8,128)S(1)}, u32[]{:S(2)}, u32[]{:S(2)}) collective-permute-start(f32[16,2,8,128]{3,2,1,0:T(8,128)S(1)} %get-tuple-element.17), channel_id=1, source_target_pairs={{4,8},{8,4},{68,72},{72,68},{36,40},{40,36},{100,104},{104,100},{5... | collective-permute-start | bytes 393224 | tf_op jit(solution)/shard_map/ppermute | solution.py:434
  149.2 9.7 %collective-permute-start.9 = (f32[16,2,8,128]{3,2,1,0:T(8,128)S(1)}, f32[16,2,8,128]{3,2,1,0:T(8,128)S(1)}, u32[]{:S(2)}, u32[]{:S(2)}) collective-permute-start(f32[16,2,8,128]{3,2,1,0:T(8,128)S(1)} %get-tuple-element.18), channel_id=1, source_target_pairs={{0,4},{4,0},{64,68},{68,64},{32,36},{36,32},{96,100},{100,96},{1,5... | collective-permute-start | bytes 393224 | tf_op jit(solution)/shard_map/ppermute | solution.py:435
  160.4 7.2 %collective-permute-start.10 = (f32[44,2,8,128]{3,2,1,0:T(8,128)S(1)}, f32[44,2,8,128]{3,2,1,0:T(8,128)S(1)}, u32[]{:S(2)}, u32[]{:S(2)}) collective-permute-start(f32[44,2,8,128]{3,2,1,0:T(8,128)S(1)} %get-tuple-element.19), channel_id=1, source_target_pairs={{0,32},{32,1},{1,33},{33,2},{2,34},{34,3},{3,35},{35,131},{131,163... | collective-permute-start | bytes 1081352 | tf_op jit(solution)/shard_map/ppermute | solution.py:467
  163.2 8.7 %collective-permute-start.11 = (f32[44,2,8,128]{3,2,1,0:T(8,128)S(1)}, f32[44,2,8,128]{3,2,1,0:T(8,128)S(1)}, u32[]{:S(2)}, u32[]{:S(2)}) collective-permute-start(f32[44,2,8,128]{3,2,1,0:T(8,128)S(1)} %get-tuple-element.20), channel_id=1, source_target_pairs={{32,0},{1,32},{33,1},{2,33},{34,2},{3,34},{35,3},{131,35},{163,131... | collective-permute-start | bytes 1081352 | tf_op jit(solution)/shard_map/ppermute | solution.py:467

commit v2 on v1

v2 whole, which is shorter than its diff:
```python
import jax
import jax.numpy as jnp
from jax import lax
from jax.experimental import pallas as pl
from jax.experimental.pallas import tpu as pltpu
from jax.sharding import PartitionSpec as P

M = 4
FINE_RATE = 0.025
COARSE_RATE = M * FINE_RATE
DIFFUSION = 1.5
WIDTH_SQ = 18.0
AXES = ("tm", "space")


def device(x, y, z_lo, z_hi, core):
    return (y * 4 + z_hi * 2 + core) * 32 + z_lo * 4 + x


def ring_of(x, y, core):
    return 2 * (y * 4 + (3 - x if y & 1 else x)) + core


def place(ring):
    q, core = ring >> 1, ring & 1
    y, x = q >> 2, q & 3
    return (3 - x if y & 1 else x), y, core


PLANES = [(z_lo, z_hi) for z_hi in range(2) for z_lo in range(8)]


def on_ring(ring, plane):
    x, y, core = place(ring % 32)
    return device(x, y, plane[0], plane[1], core)


RING = [ring_of(n % 4, n // 8, (n // 4) % 2) for n in range(32)]
MEMBER = [RING.index(i) for i in range(32)]
PLANE_GROUPS = [[on_ring(i, plane) for i in RING] for plane in PLANES]
RIGHT = [(on_ring(i, plane), on_ring(i + 1, plane)) for plane in PLANES for i in range(32)]
LEFT = [(b, a) for a, b in RIGHT]
ACROSS = [(i, i ^ 2) for i in range(16)]


def row_pairs(parity):
    pairs = []
    for z in range(parity, 16, 2):
        for i in range(32):
            a, b = on_ring(i, (z % 8, z // 8)), on_ring(i, ((z + 1) % 8, (z + 1) // 8 % 2))
            pairs += [(a, b), (b, a)]
    return pairs


def space_pairs(parity):
    pairs = []
    for s in range(parity, 32, 2):
        pairs += [(s, (s + 1) % 32), ((s + 1) % 32, s)]
    return pairs


def growth(pc, uc, pxm, pxp, pym, pyp, pzm, pzp):
    dx, dy, dz = pxp - pxm, pyp - pym, pzp - pzm
    dx, dy, dz = dx * dx, dy * dy, dz * dz
    floor = jnp.maximum(dx + dy + dz, 0.04)
    quartic = (dx * dx + dy * dy + dz * dz) / (floor * floor)
    aniso = 0.85 + 0.2 * quartic
    lap = ((pxp + pxm) + (pyp + pym)) + (pzp + pzm) - 6.0 * pc
    wet = 1.0 - pc * pc
    return aniso * aniso * lap + wet * (pc - 2.0 * uc * wet)


def block_index():
    return lax.axis_index("tm"), lax.axis_index("space")


def start_kernel(nuclei, p_in, u_in, u_start, out, cells, sems):
    tm, space = block_index()
    whole = (tm == 0) | (tm == 15)

    @pl.when(~whole)
    def _():
        p_copy = pltpu.make_async_copy(p_in.at[0], out.at[0], sems.at[0])
        u_copy = pltpu.make_async_copy(u_in.at[0], out.at[1], sems.at[1])
        p_copy.start()
        u_copy.start()
        p_copy.wait()
        u_copy.wait()

    @pl.when(whole)
    def _():
        u_copy = pltpu.make_async_copy(u_start, out.at[1], sems.at[1])
        n_copy = pltpu.make_async_copy(nuclei, cells, sems.at[0])
        u_copy.start()
        n_copy.start()
        n_copy.wait()
        zs = lax.broadcasted_iota(jnp.int32, (8, 512), 0)
        ys = lax.broadcasted_iota(jnp.int32, (8, 512), 1)
        for g in range(4):
            sides = []
            for n in range(8):
                dy = jnp.abs(ys - cells[2, n])
                dy = jnp.minimum(dy, 512 - dy)
                dz = zs + 8 * g - cells[1, n]
                sides.append(dy * dy + dz * dz)
            for r in range(4):
                best = None
                for n in range(8):
                    dx = jnp.abs(space * 4 + r - cells[0, n])
                    dx = jnp.minimum(dx, 128 - dx)
                    here = sides[n] + dx * dx
                    best = here if best is None else jnp.minimum(best, here)
                b = jnp.exp(-best.astype(jnp.float32) / WIDTH_SQ)
                out[0, r, 8 * g : 8 * g + 8, :] = 2.0 * b - 1.0
        u_copy.wait()


def transpose_lanes(parts):
    slot = lax.broadcasted_iota(jnp.int32, (8, 128), 1) // 16
    parts = list(parts)
    for d in (4, 2, 1):
        low = (slot & d) == 0
        for a in range(8):
            if not a & d:
                top, bottom = parts[a], parts[a + d]
                parts[a] = jnp.where(low, top, pltpu.roll(bottom, 16 * d, 1))
                parts[a + d] = jnp.where(low, pltpu.roll(top, 128 - 16 * d, 1), bottom)
    return parts


def relax_kernel(start, odd, even, out, one, two, coarse):
    tm, space = block_index()
    keep = jnp.where((tm == 0) | (tm == 15), 0.0, 1.0)

    def put(buf, f, row, g, value):
        buf[f, row, 8 + 8 * g : 16 + 8 * g, :] = value
        if g == 0:
            buf[f, row, 7:8, :] = value[0:1]
        if g == 3:
            buf[f, row, 40:41, :] = value[7:8]

    def fill(before, after):
        for f in range(2):
            for part, src in enumerate((before, start, after)):
                for r in range(4):
                    for g in range(4):
                        put(one, f, 4 * part + r, g, src[f, r, 8 * g : 8 * g + 8, :])

    @pl.when(space % 2 == 0)
    def _():
        fill(odd, even)

    @pl.when(space % 2 == 1)
    def _():
        fill(even, odd)

    def one_row(src, dst, row, first):
        for g in range(4):
            at = slice(8 + 8 * g, 16 + 8 * g)
            up = slice(9 + 8 * g, 17 + 8 * g)
            down = slice(7 + 8 * g, 15 + 8 * g)
            pc, uc = src[0, row, at, :], src[1, row, at, :]
            rate = growth(
                pc, uc,
                src[0, row - 1, at, :], src[0, row + 1, at, :],
                pltpu.roll(pc, 1, 1), pltpu.roll(pc, 511, 1),
                src[0, row, down, :], src[0, row, up, :],
            )
            ulap = (
                (src[1, row - 1, at, :] + src[1, row + 1, at, :])
                + (pltpu.roll(uc, 1, 1) + pltpu.roll(uc, 511, 1))
                + (src[1, row, down, :] + src[1, row, up, :])
                - 6.0 * uc
            )
            gain = FINE_RATE * rate
            put(dst, 0, row, g, pc + gain)
            put(dst, 1, row, g, uc + (FINE_RATE * DIFFUSION) * ulap + 0.5 * gain)
            if first:
                gain = COARSE_RATE * rate
                coarse[0, row - 4, 8 * g : 8 * g + 8, :] = pc + gain
                coarse[1, row - 4, 8 * g : 8 * g + 8, :] = (
                    uc + (COARSE_RATE * DIFFUSION) * ulap + 0.5 * gain
                )

    def sweep(src, dst, lo, hi, first=False):
        @pl.loop(lo, hi)
        def _(row):
            one_row(src, dst, row, first)

    sweep(one, two, 1, 4)
    sweep(one, two, 4, 8, True)
    sweep(one, two, 8, 11)
    sweep(two, one, 2, 10)
    sweep(one, two, 3, 9)
    sweep(two, one, 4, 8)

    for f in range(2):
        for rp in range(2):
            for b in range(4):
                parts = []
                for g in range(4):
                    for rr in range(2):
                        r = 2 * rp + rr
                        lanes = slice(128 * b, 128 * b + 128)
                        fine = one[f, 4 + r, 8 + 8 * g : 16 + 8 * g, lanes]
                        parts.append(fine - keep * coarse[f, r, 8 * g : 8 * g + 8, lanes])
                for j, part in enumerate(transpose_lanes(parts)):
                    out[MEMBER[8 * b + j], f, rp] = part


STEPS = (6, 8)


class Phase:
    def __init__(self, index):
        self.index = index
        self.steps = STEPS[index]
        self.base = 1 + index * STEPS[0]
        self.halo = [self.steps - j for j in range(self.steps + 1)]
        self.halo_at = [sum(self.halo[:j]) for j in range(self.steps + 2)]


PHASES = Phase(0), Phase(1)


def half_of(k):
    return (k >> 1) & 1


def local_block(k):
    return 2 * (k >> 2) + (k & 1)


def lane32():
    return lax.broadcasted_iota(jnp.int32, (8, 128), 1) % 32


def piece_of(phase, own, other, first, z_hi):
    def get(slot, f, pair):
        x, rp = pair // 2, pair % 2
        if slot == 0 and phase.index:
            return first[f, pair]
        if slot == 0:
            return jnp.where(z_hi == 0, own[x, f, rp], own[28 + x, f, rp])
        k = phase.base + slot - 1
        m = local_block(k)
        sent = m - (4 * phase.index + (1 - phase.index) - half_of(k) * 1)
        return jnp.where(
            half_of(k) == z_hi, own[4 * m + x, f, rp], other[4 * sent + x, f, rp]
        )

    return get


def sent_from(phase, z_hi):
    return 4 * (4 * phase.index + (1 - phase.index) - z_hi)


def split(phase, refs, count):
    if phase.index == 0:
        return refs[0], refs[1], None, *refs[2 : 2 + count]
    return refs[0], refs[1], refs[2], *refs[3 : 3 + count]


def cut_kernel(own, near, middle, far, once, *blank):
    tm, _ = block_index()
    z_hi = (tm // 2) % 2
    at = 4 * (1 - z_hi)
    for out in (near, middle, far):
        out[...] = own[pl.ds(at, out.shape[0])]
        at = at + out.shape[0]
    once[0] = 1


def lanes_kernel(phase, *refs):
    own, other, first, right, left = split(phase, refs, 2)
    tm, _ = block_index()
    get = piece_of(phase, own, other, first, (tm // 2) % 2)
    part = lane32() // 8
    for slot in range(phase.steps):
        for f in range(2):
            for quad in range(4):
                r_edge = l_edge = None
                for q in range(4):
                    if q % 2 == 0:
                        piece = get(slot, f, 2 * quad + q // 2)
                    at = 16 * (q % 2)
                    r_part = pltpu.roll(piece, (8 * q - at - 8) % 128, 1)
                    l_part = pltpu.roll(piece, (8 * q - at) % 128, 1) if 8 * q != at else piece
                    if q == 0:
                        r_edge, l_edge = r_part, l_part
                    else:
                        r_edge = jnp.where(part == q, r_part, r_edge)
                        l_edge = jnp.where(part == q, l_part, l_edge)
                right[4 * slot + quad, f] = r_edge
                left[4 * slot + quad, f] = l_edge


def row_of(phase, get, from_left, from_right):
    part = lane32() // 8

    def row(slot, f, r):
        value = pltpu.roll(get(slot, f, r // 2), 120 if r % 2 else 8, 1)
        if slot == phase.steps:
            return value
        quad, q = 4 * slot + r // 4, r % 4
        l_halo, r_halo = from_left[quad, f], from_right[quad, f]
        if q != 0:
            l_halo = pltpu.roll(l_halo, 128 - 8 * q, 1)
        if q != 3:
            r_halo = pltpu.roll(r_halo, 24 - 8 * q, 1)
        return jnp.where(part == 0, l_halo, jnp.where(part == 3, r_halo, value))

    return row


def edges_kernel(phase, *refs):
    own, other, first, from_left, from_right, odd, even = split(phase, refs, 4)
    tm, space = block_index()
    get = piece_of(phase, own, other, first, (tm // 2) % 2)
    row = row_of(phase, get, from_left, from_right)
    z_odd = (space // 4) % 2 == 1
    for slot in range(phase.steps):
        n = phase.halo[slot]
        for f in range(2):
            for m in range(n):
                top, bottom = row(slot, f, m), row(slot, f, 16 - n + m)
                odd[phase.halo_at[slot] + m, f] = jnp.where(z_odd, bottom, top)
                even[phase.halo_at[slot] + m, f] = jnp.where(z_odd, top, bottom)


def chain_kernel(phase, *refs):
    if phase.index == 0:
        own, other, first, from_left, from_right, odd, even, out, last, state, taus = split(
            phase, refs, 8
        )
    else:
        own, other, first, from_left, from_right, odd, even, before, out, state, taus = split(
            phase, refs, 8
        )
    tm, space = block_index()
    z_hi = (tm // 2) % 2
    get = piece_of(phase, own, other, first, z_hi)
    row = row_of(phase, get, from_left, from_right)
    z_odd = (space // 4) % 2 == 1
    lane = lane32()
    for slot in range(phase.steps + 1):
        n, at = phase.halo[slot], phase.halo_at[slot]
        for f in range(2):
            put = state.at[0, f] if slot == 0 else taus.at[slot - 1, f]
            for m in range(n):
                put[8 - n + m] = jnp.where(z_odd, even[at + m, f], odd[at + m, f])
                put[24 + m] = jnp.where(z_odd, odd[at + m, f], even[at + m, f])
            for r in range(16):
                put[8 + r] = row(slot, f, r)

    def emit(k, pair, f, piece):
        out[4 * local_block(k) + pair // 2, f, pair % 2] = piece

    if phase.index:
        for i in range(16):
            out[i] = before[i]

    def given():
        for f in range(2):
            for pair in range(8):
                emit(phase.base, pair, f, get(0, f, pair))
                if phase.index == 0:
                    emit(0, pair, f, get(0, f, pair))

    pl.when(z_hi == half_of(phase.base))(given)

    sub = lax.broadcasted_iota(jnp.int32, (4, 8, 128), 1)
    lanes = lax.broadcasted_iota(jnp.int32, (4, 8, 128), 2)
    is_top, is_bottom = sub == 7, sub == 0
    end_up = is_top & (lanes >= 96)
    end_down = is_bottom & (lanes < 32)

    def z_up(v):
        w = jnp.where(is_bottom, pltpu.roll(v, 96, 2), v)
        return jnp.where(end_up, v, pltpu.roll(w, 7, 1))

    def z_down(v):
        w = jnp.where(is_top, pltpu.roll(v, 32, 2), v)
        return jnp.where(end_down, v, pltpu.roll(w, 1, 1))

    for j in range(1, phase.steps + 1):
        src, dst = (j + 1) % 2, j % 2
        lo, hi = 8 - (phase.steps - j), 24 + (phase.steps - j)
        starts = list(range(lo, hi - 3, 4))
        if starts[-1] + 4 < hi:
            starts.append(hi - 4)
        for r in starts:
            pc, uc = state[src, 0, r : r + 4], state[src, 1, r : r + 4]
            rate = growth(
                pc, uc,
                state[src, 0, r - 1 : r + 3], state[src, 0, r + 1 : r + 5],
                pltpu.roll(pc, 1, 2), pltpu.roll(pc, 127, 2),
                z_down(pc), z_up(pc),
            )
            ulap = (
                (state[src, 1, r - 1 : r + 3] + state[src, 1, r + 1 : r + 5])
                + (pltpu.roll(uc, 1, 2) + pltpu.roll(uc, 127, 2))
                + (z_down(uc) + z_up(uc))
                - 6.0 * uc
            )
            gain = COARSE_RATE * rate
            state[dst, 0, r : r + 4] = pc + gain + taus[j - 1, 0, r : r + 4]
            state[dst, 1, r : r + 4] = (
                uc + (COARSE_RATE * DIFFUSION) * ulap + 0.5 * gain + taus[j - 1, 1, r : r + 4]
            )
        k = phase.base + j

        def pack(f, pair, dst=dst):
            low, high = state[dst, f, 8 + 2 * pair], state[dst, f, 9 + 2 * pair]
            return jnp.where(lane < 16, pltpu.roll(low, 120, 1), pltpu.roll(high, 8, 1))

        if phase.index == 0 and j == phase.steps:
            for f in range(2):
                for pair in range(8):
                    last[f, pair] = pack(f, pair)
        else:

            @pl.when(z_hi == half_of(k))
            def _(k=k, pack=pack):
                for f in range(2):
                    for pair in range(8):
                        emit(k, pair, f, pack(f, pair))


def finish_kernel(start, got, p_out, u_out):
    tm, _ = block_index()

    @pl.when(tm == 0)
    def _():
        p_out[0] = start[0]
        u_out[0] = start[1]

    @pl.when(tm != 0)
    def _():
        for f, out in enumerate((p_out, u_out)):
            for rp in range(2):
                for b in range(4):
                    parts = transpose_lanes([got[MEMBER[8 * b + j], f, rp] for j in range(8)])
                    for g in range(4):
                        for rr in range(2):
                            at = slice(8 * g, 8 * g + 8), slice(128 * b, 128 * b + 128)
                            out[0, 2 * rp + rr, at[0], at[1]] = parts[2 * g + rr]


VMEM = pl.BlockSpec(memory_space=pltpu.VMEM)
ANY = pl.BlockSpec(memory_space=pl.ANY)


def call(kernel, outs, args, scratch=(), specs=None, grant=40):
    shapes = [jax.ShapeDtypeStruct(s, jnp.float32) for s in outs]
    return pl.pallas_call(
        kernel,
        out_shape=shapes if len(shapes) > 1 else shapes[0],
        in_specs=specs or [VMEM] * len(args),
        out_specs=[VMEM] * len(shapes) if len(shapes) > 1 else VMEM,
        scratch_shapes=[pltpu.VMEM(s, jnp.float32) if isinstance(s, tuple) else s for s in scratch],
        cost_estimate=pl.CostEstimate(flops=8, bytes_accessed=8, transcendentals=0),
        compiler_params=pltpu.CompilerParams(vmem_limit_bytes=grant * 1024 * 1024),
    )(*args)


def exchange_rows(payload, axis, pairs):
    odd, even = payload
    got_odd = lax.ppermute(odd, axis, pairs(1))
    got_even = lax.ppermute(even, axis, pairs(0))
    return got_odd, got_even


def local(phase_guess, solute_guess, solute_start, nuclei):
    start = call(
        start_kernel,
        [(2, 4, 32, 512)],
        [nuclei.T, phase_guess, solute_guess, solute_start],
        scratch=[pltpu.SMEM((3, 8), jnp.int32), pltpu.SemaphoreType.DMA((2,))],
        specs=[ANY] * 4,
        grant=60,
    )
    odd, even = exchange_rows((start, start), "space", space_pairs)
    packed = call(
        relax_kernel,
        [(32, 2, 2, 8, 128)],
        [start, odd, even],
        scratch=[(2, 12, 48, 512), (2, 12, 48, 512), (2, 4, 32, 512)],
    )
    own = lax.all_to_all(packed, AXES, 0, 0, tiled=True, axis_index_groups=PLANE_GROUPS)
    blank = [(16, 2, 2, 8, 128), (2, 8, 8, 128)]
    shapes = [(4 * blocks, 2, 2, 8, 128) for blocks in (2, 1, 4)]
    near, middle, far, once, *blank = pl.pallas_call(
        cut_kernel,
        out_shape=[jax.ShapeDtypeStruct(s, jnp.float32) for s in shapes]
        + [jax.ShapeDtypeStruct((1,), jnp.int32)]
        + [jax.ShapeDtypeStruct(s, jnp.float32) for s in blank],
        in_specs=[VMEM],
        out_specs=[VMEM, VMEM, VMEM, pl.BlockSpec(memory_space=pltpu.SMEM), ANY, ANY],
        compiler_params=pltpu.CompilerParams(vmem_limit_bytes=40 * 1024 * 1024),
    )(own)
    near = lax.ppermute(near, "tm", ACROSS)
    middle = lax.ppermute(middle, "tm", ACROSS)

    def lanes(phase, known):
        right, left = call(
            lambda *refs: lanes_kernel(phase, *refs), [(4 * phase.steps, 2, 8, 128)] * 2, known
        )
        return [lax.ppermute(right, AXES, RIGHT), lax.ppermute(left, AXES, LEFT)]

    def advance(phase, known, before=(), after=()):
        edges = call(
            lambda *refs: edges_kernel(phase, *refs[len(after) :]),
            [(phase.halo_at[-1], 2, 8, 128)] * 2,
            [*after, *known],
            specs=[ANY] * len(after) + [VMEM] * len(known),
        )
        return call(
            lambda *refs: chain_kernel(phase, *refs),
            [(32, 2, 2, 8, 128)] if phase.index else [(16, 2, 2, 8, 128), (2, 8, 8, 128)],
            [*known, *exchange_rows(edges, AXES, row_pairs), *before],
            scratch=[(2, 2, 32, 8, 128), (phase.steps, 2, 32, 8, 128)],
        )

    known = [own, jnp.concatenate([near, middle])]
    far, _ = lax.optimization_barrier((far, near))
    crossed = lax.ppermute(far, "tm", ACROSS)
    known += lanes(PHASES[0], known)
    before, first = lax.fori_loop(
        0, once[0], lambda i, state: tuple(advance(PHASES[0], known, (), state[1:])), tuple(blank)
    )
    known = [own, crossed, first]
    known += lanes(PHASES[1], known)
    got = advance(PHASES[1], known, [before])
    back = lax.all_to_all(got, AXES, 0, 0, tiled=True, axis_index_groups=PLANE_GROUPS)
    return call(finish_kernel, [(1, 4, 32, 512)] * 2, [start, back])


def solution(mesh):
    return jax.shard_map(
        lambda *args: tuple(local(*args)),
        mesh=mesh,
        in_specs=(
            P("tm", "space", None, None),
            P("tm", "space", None, None),
            P("space", None, None),
            P(),
        ),
        out_specs=(P("tm", "space", None, None), P("tm", "space", None, None)),
        check_vma=False,
    )
```

time: 195 us -> 169 us (0.87)
  waiting for transfers between devices: 78.7 us -> 46 us
  starting transfers between devices: 57 us -> 64.1 us
  local copies, waits for them, and re-layouts: 3.64 us -> 1.07 us
    ppermute x6 -> x7, waiting for transfers between devices: 50.8 us -> 20.1 us  [the longest x1 12.3 us: local(): near = lax.ppermute(near, 'tm', ACROSS)]
    ppermute x6 -> x7, starting transfers between devices: 21.9 us -> 33.7 us  [the longest x1 13.2 us: local(): near = lax.ppermute(near, 'tm', ACROSS)]
    ppermute x3, waiting for transfers between devices: 11.8 us -> 3.81 us  [exchange_rows(): got_even = lax.ppermute(even, axis, pairs(0))]
    ppermute x3, starting transfers between devices: 29.4 us -> 22.6 us  [exchange_rows(): got_odd = lax.ppermute(odd, axis, pairs(1))]
    ppermute x3, waiting for transfers between devices: 16.1 us -> 22 us  [exchange_rows(): got_odd = lax.ppermute(odd, axis, pairs(1))]
    unnamed x7, local copies, waits for them, and re-layouts: 3.61 us -> 1.06 us
    ppermute x3, starting transfers between devices: 5.76 us -> 7.79 us  [exchange_rows(): got_even = lax.ppermute(even, axis, pairs(0))]
  transfers between devices with their start and end apart: 12 -> 13, of which waited for: 11 -> 7; matrix products, arithmetic and copies ran while one was open for 0% -> 0% of each run, Pallas kernels for 2% -> 2%
where the time goes in v2:
time: 169 us; the launch traced here: 168 us
  starting transfers between devices  64.1 us (38%)
  waiting for transfers between devices  46 us (27%)
  blocking collectives  35.7 us (21%)
  Pallas kernels  19 us (11%)
    ppermute x3, starting transfers between devices, exchange_rows(): got_odd = lax.ppermute(odd, axis, pairs(1))  22.6 us
    ppermute x3, waiting for transfers between devices, exchange_rows(): got_odd = lax.ppermute(odd, axis, pairs(1))  22 us
    all_to_all x1, blocking collectives, local(): lax.all_to_all(packed, AXES, 0, 0, tiled=True, axis_index_groups=PLANE_GR...  18.6 us
    pallas_call x9, Pallas kernels, call(): pl.pallas_call(kernel, out_shape=shapes if len(shapes) > 1 else shapes[0]...  18.5 us
    all_to_all x1, blocking collectives, local(): lax.all_to_all(got, AXES, 0, 0, tiled=True, axis_index_groups=PLANE_GROUPS)  17.1 us
    ppermute x1, starting transfers between devices, local(): near = lax.ppermute(near, 'tm', ACROSS)  13.2 us
    ppermute x4, starting transfers between devices, lanes(): return [lax.ppermute(right, AXES, RIGHT), lax.ppermute(left, AXES, LEFT)]  12.6 us
    ppermute x1, waiting for transfers between devices, local(): near = lax.ppermute(near, 'tm', ACROSS)  12.3 us
  transfers between devices with their start and end apart: 13, of which 7 were waited for; matrix products, arithmetic and copies ran while one was open for 0% of the time, Pallas kernels for 2%

profile of v2, /device:TPU:1, one launch (start us, length us, event | category | flops | bytes accessed | tf_op | source)
XLA Modules:
  0.0 168.1 jit_solution(10692416581090908233)
XLA Ops:
  0.6 1.9 %shard_map.59.start = f32[2,4,32,512]{3,2,1,0:T(8,128)} custom-call(s32[3,8]{1,0:T(4,128)} %bitcast.2, f32[1,4,32,512]{3,2,1,0:T(8,128)} %p_in.1, f32[1,4,32,512]{3,2,1,0:T(8,128)} %u_in.1, f32[4,32,512]{2,1,0:T(8,128)} %u_start.1), custom_call_target="tpu_custom_call" | custom-call | flops 8 | bytes 8 | tf_op jit(solution)/shard_map/pallas_call | solution.py:457
  2.5 3.9 %collective-permute-start.3 = (f32[2,4,32,512]{3,2,1,0:T(8,128)}, f32[2,4,32,512]{3,2,1,0:T(8,128)S(1)}, u32[]{:S(2)}, u32[]{:S(2)}) collective-permute-start(f32[2,4,32,512]{3,2,1,0:T(8,128)} %shard_map.59.start), channel_id=1, source_target_pairs={{0,1},{1,0},{2,3},{3,2},{4,5},{5,4},{6,7},{7,6},{8,9},{9,8},{10,11... | collective-permute-start | bytes 1572872 | tf_op jit(solution)/shard_map/ppermute | solution.py:471
  6.5 14.4 %collective-permute-start.2 = (f32[2,4,32,512]{3,2,1,0:T(8,128)}, f32[2,4,32,512]{3,2,1,0:T(8,128)S(1)}, u32[]{:S(2)}, u32[]{:S(2)}) collective-permute-start(f32[2,4,32,512]{3,2,1,0:T(8,128)} %shard_map.59.start), channel_id=1, source_target_pairs={{1,2},{2,1},{3,4},{4,3},{5,6},{6,5},{7,8},{8,7},{9,10},{10,9},{11,... | collective-permute-start | bytes 1572872 | tf_op jit(solution)/shard_map/ppermute | solution.py:470
  20.9 0.0 collective-permute-done.3.even
  20.9 10.3 %collective-permute-done.2.odd = f32[2,4,32,512]{3,2,1,0:T(8,128)S(1)} collective-permute-done((f32[2,4,32,512]{3,2,1,0:T(8,128)}, f32[2,4,32,512]{3,2,1,0:T(8,128)S(1)}, u32[]{:S(2)}, u32[]{:S(2)}) %collective-permute-start.2) | collective-permute-done | bytes 524320 | tf_op jit(solution)/shard_map/ppermute | solution.py:470
  31.2 0.0 copy-start
  31.2 1.0 copy-done
  32.2 6.7 %shard_map.60 = f32[32,2,2,8,128]{4,3,2,1,0:T(8,128)S(1)} custom-call(f32[2,4,32,512]{3,2,1,0:T(8,128)S(1)} %copy-done, f32[2,4,32,512]{3,2,1,0:T(8,128)S(1)} %collective-permute-done.2.odd, f32[2,4,32,512]{3,2,1,0:T(8,128)S(1)} %collective-permute-done.3.even), custom_call_target="tpu_custom_call" | custom-call | flops 8 | bytes 8 | tf_op jit(solution)/shard_map/pallas_call | solution.py:457
  38.9 18.6 %all_to_all.10.own.refs_0_ = f32[32,2,2,8,128]{4,3,2,1,0:T(8,128)S(1)} all-to-all(f32[32,2,2,8,128]{4,3,2,1,0:T(8,128)S(1)} %shard_map.60), channel_id=1, replica_groups={{0,1,2,3,32,33,34,35,128,129,130,131,160,161,162,163,256,257,258,259,28..., dimensions={0} | all-to-all | bytes 1048576 | tf_op jit(solution)/shard_map/all_to_all | solution.py:491
  57.5 0.5 shard_map.61
  58.0 13.2 %collective-permute-start.4 = (f32[8,2,2,8,128]{4,3,2,1,0:T(8,128)S(1)}, f32[8,2,2,8,128]{4,3,2,1,0:T(8,128)S(1)}, u32[]{:S(2)}, u32[]{:S(2)}) collective-permute-start(f32[8,2,2,8,128]{4,3,2,1,0:T(8,128)S(1)} %get-tuple-element.63), channel_id=1, source_target_pairs={{0,64},{32,96},{64,0},{96,32},{128,192},{160,224},{192,128},{224,1... | collective-permute-start | bytes 393224 | tf_op jit(solution)/shard_map/ppermute | solution.py:503
  71.2 1.9 %collective-permute-start.6 = (f32[4,2,2,8,128]{4,3,2,1,0:T(8,128)S(1)}, f32[4,2,2,8,128]{4,3,2,1,0:T(8,128)S(1)}, u32[]{:S(2)}, u32[]{:S(2)}) collective-permute-start(f32[4,2,2,8,128]{4,3,2,1,0:T(8,128)S(1)} %get-tuple-element.68), channel_id=1, source_target_pairs={{0,64},{32,96},{64,0},{96,32},{128,192},{160,224},{192,128},{224,1... | collective-permute-start | bytes 196616 | tf_op jit(solution)/shard_map/ppermute | solution.py:504
  73.1 12.3 %collective-permute-done.4 = f32[8,2,2,8,128]{4,3,2,1,0:T(8,128)S(1)} collective-permute-done((f32[8,2,2,8,128]{4,3,2,1,0:T(8,128)S(1)}, f32[8,2,2,8,128]{4,3,2,1,0:T(8,128)S(1)}, u32[]{:S(2)}, u32[]{:S(2)}) %collective-permute-start.4) | collective-permute-done | bytes 131104 | tf_op jit(solution)/shard_map/ppermute | solution.py:503
  85.4 6.1 %collective-permute-start.5 = (f32[16,2,2,8,128]{4,3,2,1,0:T(8,128)S(1)}, f32[16,2,2,8,128]{4,3,2,1,0:T(8,128)S(1)}, u32[]{:S(2)}, u32[]{:S(2)}) collective-permute-start(f32[16,2,2,8,128]{4,3,2,1,0:T(8,128)S(1)} %get-tuple-element.64), channel_id=1, source_target_pairs={{0,64},{32,96},{64,0},{96,32},{128,192},{160,224},{192,128},{224,1... | collective-permute-start | bytes 786440 | tf_op jit(solution)/shard_map/ppermute | solution.py:528
  91.5 0.0 collective-permute-done.6
  91.5 0.3 shard_map.62
  91.8 3.1 %collective-permute-start.7 = (f32[24,2,8,128]{3,2,1,0:T(8,128)S(1)}, f32[24,2,8,128]{3,2,1,0:T(8,128)S(1)}, u32[]{:S(2)}, u32[]{:S(2)}) collective-permute-start(f32[24,2,8,128]{3,2,1,0:T(8,128)S(1)} %get-tuple-element.69), channel_id=1, source_target_pairs={{0,32},{32,1},{1,33},{33,2},{2,34},{34,3},{3,35},{35,131},{131,163... | collective-permute-start | bytes 589832 | tf_op jit(solution)/shard_map/ppermute | solution.py:510
  95.0 3.3 %collective-permute-start.8 = (f32[24,2,8,128]{3,2,1,0:T(8,128)S(1)}, f32[24,2,8,128]{3,2,1,0:T(8,128)S(1)}, u32[]{:S(2)}, u32[]{:S(2)}) collective-permute-start(f32[24,2,8,128]{3,2,1,0:T(8,128)S(1)} %get-tuple-element.70), channel_id=1, source_target_pairs={{32,0},{1,32},{33,1},{2,33},{34,2},{3,34},{35,3},{131,35},{163,131... | collective-permute-start | bytes 589832 | tf_op jit(solution)/shard_map/ppermute | solution.py:510
  98.3 0.0 collective-permute-done.7
  98.3 3.9 %collective-permute-done.8 = f32[24,2,8,128]{3,2,1,0:T(8,128)S(1)} collective-permute-done((f32[24,2,8,128]{3,2,1,0:T(8,128)S(1)}, f32[24,2,8,128]{3,2,1,0:T(8,128)S(1)}, u32[]{:S(2)}, u32[]{:S(2)}) %collective-permute-start.8) | collective-permute-done | bytes 196640 | tf_op jit(solution)/shard_map/ppermute | solution.py:510
  102.2 19.0 %while.12 = (s32[]{:T(128)}, f32[16,2,2,8,128]{4,3,2,1,0:T(8,128)}, f32[2,8,8,128]{3,2,1,0:T(8,128)S(1)}, s32[]{:T(128)}, f32[32,2,2,8,128]{4,3,2,1,0:T(8,128)S(...) while((s32[]{:T(128)}, f32[16,2,2,8,128]{4,3,2,1,0:T(8,128)}, ...), condition=%wide.region_1.0_spmd, body=%wide.region_0.0_spmd.sunk | while | flops 18 | bytes 1376445 | solution.py:530
  102.9 0.3 body.2
  103.2 4.3 %collective-permute-start = (f32[21,2,8,128]{3,2,1,0:T(8,128)S(1)}, f32[21,2,8,128]{3,2,1,0:T(8,128)S(1)}, u32[]{:S(2)}, u32[]{:S(2)}) collective-permute-start(f32[21,2,8,128]{3,2,1,0:T(8,128)S(1)} %get-tuple-element.145), channel_id=1, source_target_pairs={{4,8},{8,4},{36,40},{40,36},{5,9},{9,5},{37,41},{41,37},{6,10},{10... | collective-permute-start | bytes 516104 | tf_op jit(solution)/shard_map/while/body/ppermute | solution.py:470
  107.6 1.9 %collective-permute-start.1 = (f32[21,2,8,128]{3,2,1,0:T(8,128)S(1)}, f32[21,2,8,128]{3,2,1,0:T(8,128)S(1)}, u32[]{:S(2)}, u32[]{:S(2)}) collective-permute-start(f32[21,2,8,128]{3,2,1,0:T(8,128)S(1)} %get-tuple-element.146), channel_id=1, source_target_pairs={{0,4},{4,0},{32,36},{36,32},{1,5},{5,1},{33,37},{37,33},{2,6},{6,2... | collective-permute-start | bytes 516104 | tf_op jit(solution)/shard_map/while/body/ppermute | solution.py:471
  109.5 8.1 %collective-permute-done.refs_4_ = f32[21,2,8,128]{3,2,1,0:T(8,128)S(1)} collective-permute-done((f32[21,2,8,128]{3,2,1,0:T(8,128)S(1)}, f32[21,2,8,128]{3,2,1,0:T(8,128)S(1)}, u32[]{:S(2)}, u32[]{:S(2)}) %collective-permute-start) | collective-permute-done | bytes 172064 | tf_op jit(solution)/shard_map/while/body/ppermute | solution.py:470
  117.6 0.0 collective-permute-done.1.refs_5_
  117.6 2.9 %body.3 = (f32[16,2,2,8,128]{4,3,2,1,0:T(8,128)}, f32[2,8,8,128]{3,2,1,0:T(8,128)S(1)}) custom-call(f32[32,2,2,8,128]{4,3,2,1,0:T(8,128)S(1)} %get-tuple-element.171.refs_1_.refs_0_, f32[12,2,2,8,128]{4,3,2,1,0:T(8,128)S(1)} %get-tuple-element.172.refs_2_.refs_1_, f32[24,2,8,128]{3,2,1,0:T(8,128)S(1)} %get-tuple-element.173.refs_3_.refs_2_, ...), custom_call_target="tpu_custom_call" | custom-call | flops 8 | bytes 8 | tf_op jit(solution)/shard_map/while/body/pallas_call | solution.py:457
  121.2 0.0 collective-permute-done.5.refs_1_
  121.2 0.3 shard_map.63
  121.6 2.0 %collective-permute-start.9 = (f32[32,2,8,128]{3,2,1,0:T(8,128)S(1)}, f32[32,2,8,128]{3,2,1,0:T(8,128)S(1)}, u32[]{:S(2)}, u32[]{:S(2)}) collective-permute-start(f32[32,2,8,128]{3,2,1,0:T(8,128)S(1)} %get-tuple-element.72), channel_id=1, source_target_pairs={{0,32},{32,1},{1,33},{33,2},{2,34},{34,3},{3,35},{35,131},{131,163... | collective-permute-start | bytes 786440 | tf_op jit(solution)/shard_map/ppermute | solution.py:510
  123.5 0.0 copy-start.2
  123.5 4.2 %collective-permute-start.10 = (f32[32,2,8,128]{3,2,1,0:T(8,128)S(1)}, f32[32,2,8,128]{3,2,1,0:T(8,128)S(1)}, u32[]{:S(2)}, u32[]{:S(2)}) collective-permute-start(f32[32,2,8,128]{3,2,1,0:T(8,128)S(1)} %get-tuple-element.73), channel_id=1, source_target_pairs={{32,0},{1,32},{33,1},{2,33},{34,2},{3,34},{35,3},{131,35},{163,131... | collective-permute-start | bytes 786440 | tf_op jit(solution)/shard_map/ppermute | solution.py:510
  127.8 0.0 collective-permute-done.9.refs_3_
  127.8 3.9 %collective-permute-done.10.refs_4_ = f32[32,2,8,128]{3,2,1,0:T(8,128)S(1)} collective-permute-done((f32[32,2,8,128]{3,2,1,0:T(8,128)S(1)}, f32[32,2,8,128]{3,2,1,0:T(8,128)S(1)}, u32[]{:S(2)}, u32[]{:S(2)}) %collective-permute-start.10) | collective-permute-done | bytes 262176 | tf_op jit(solution)/shard_map/ppermute | solution.py:510
  131.7 0.4 shard_map.64
  132.1 3.8 %collective-permute-start.11 = (f32[36,2,8,128]{3,2,1,0:T(8,128)S(1)}, f32[36,2,8,128]{3,2,1,0:T(8,128)S(1)}, u32[]{:S(2)}, u32[]{:S(2)}) collective-permute-start(f32[36,2,8,128]{3,2,1,0:T(8,128)S(1)} %get-tuple-element.74), channel_id=1, source_target_pairs={{4,8},{8,4},{36,40},{40,36},{5,9},{9,5},{37,41},{41,37},{6,10},{10... | collective-permute-start | bytes 884744 | tf_op jit(solution)/shard_map/ppermute | solution.py:470
  136.0 1.9 %collective-permute-start.12 = (f32[36,2,8,128]{3,2,1,0:T(8,128)S(1)}, f32[36,2,8,128]{3,2,1,0:T(8,128)S(1)}, u32[]{:S(2)}, u32[]{:S(2)}) collective-permute-start(f32[36,2,8,128]{3,2,1,0:T(8,128)S(1)} %get-tuple-element.75), channel_id=1, source_target_pairs={{0,4},{4,0},{32,36},{36,32},{1,5},{5,1},{33,37},{37,33},{2,6},{6,2... | collective-permute-start | bytes 884744 | tf_op jit(solution)/shard_map/ppermute | solution.py:471
  137.9 3.6 %collective-permute-done.11.refs_5_ = f32[36,2,8,128]{3,2,1,0:T(8,128)S(1)} collective-permute-done((f32[36,2,8,128]{3,2,1,0:T(8,128)S(1)}, f32[36,2,8,128]{3,2,1,0:T(8,128)S(1)}, u32[]{:S(2)}, u32[]{:S(2)}) %collective-permute-start.11) | collective-permute-done | bytes 294944 | tf_op jit(solution)/shard_map/ppermute | solution.py:470
  141.5 3.8 %collective-permute-done.12.refs_6_ = f32[36,2,8,128]{3,2,1,0:T(8,128)S(1)} collective-permute-done((f32[36,2,8,128]{3,2,1,0:T(8,128)S(1)}, f32[36,2,8,128]{3,2,1,0:T(8,128)S(1)}, u32[]{:S(2)}, u32[]{:S(2)}) %collective-permute-start.12) | collective-permute-done | bytes 294944 | tf_op jit(solution)/shard_map/ppermute | solution.py:471
  145.3 0.0 copy-done.2
  145.3 3.4 %shard_map.65 = f32[32,2,2,8,128]{4,3,2,1,0:T(8,128)S(1)} custom-call(f32[32,2,2,8,128]{4,3,2,1,0:T(8,128)S(1)} %get-tuple-element.198, f32[16,2,2,8,128]{4,3,2,1,0:T(8,128)S(1)} %collective-permute-done.5.refs_1_, f32[2,8,8,128]{3,2,1,0:T(8,128)S(1)} %get-tuple-element.71.refs_2_, f32[32,2,8,128]{3,2,1,0:T(8,128)S(1)} %collective-permute-done.9.refs_3_, ...), custom_call_target="tpu_custom_call" | custom-call | flops 8 | bytes 8 | tf_op jit(solution)/shard_map/pallas_call | solution.py:457
  148.7 0.0 copy-start.1
  148.7 17.1 %all_to_all.11.got = f32[32,2,2,8,128]{4,3,2,1,0:T(8,128)S(1)} all-to-all(f32[32,2,2,8,128]{4,3,2,1,0:T(8,128)S(1)} %shard_map.65), channel_id=1, replica_groups={{0,1,2,3,32,33,34,35,128,129,130,131,160,161,162,163,256,257,258,259,28..., dimensions={0} | all-to-all | bytes 1048576 | tf_op jit(solution)/shard_map/all_to_all | solution.py:536
  165.8 0.0 copy-done.1
  165.8 2.3 %shard_map.66 = (f32[1,4,32,512]{3,2,1,0:T(8,128)}, f32[1,4,32,512]{3,2,1,0:T(8,128)}) custom-call(f32[2,4,32,512]{3,2,1,0:T(8,128)S(1)} %copy-done.1, f32[32,2,2,8,128]{4,3,2,1,0:T(8,128)S(1)} %all_to_all.11.got), custom_call_target="tpu_custom_call" | custom-call | flops 8 | bytes 8 | tf_op jit(solution)/shard_map/pallas_call | solution.py:457
  (2 shorter events, 0.0 us)
Async XLA Ops:
  2.5 18.4 %collective-permute-start.3 = (f32[2,4,32,512]{3,2,1,0:T(8,128)}, f32[2,4,32,512]{3,2,1,0:T(8,128)S(1)}, u32[]{:S(2)}, u32[]{:S(2)}) collective-permute-start(f32[2,4,32,512]{3,2,1,0:T(8,128)} %shard_map.59.start), channel_id=1, source_target_pairs={{0,1},{1,0},{2,3},{3,2},{4,5},{5,4},{6,7},{7,6},{8,9},{9,8},{10,11... | collective-permute-start | bytes 1572872 | tf_op jit(solution)/shard_map/ppermute | solution.py:471
  6.5 24.7 %collective-permute-start.2 = (f32[2,4,32,512]{3,2,1,0:T(8,128)}, f32[2,4,32,512]{3,2,1,0:T(8,128)S(1)}, u32[]{:S(2)}, u32[]{:S(2)}) collective-permute-start(f32[2,4,32,512]{3,2,1,0:T(8,128)} %shard_map.59.start), channel_id=1, source_target_pairs={{1,2},{2,1},{3,4},{4,3},{5,6},{6,5},{7,8},{8,7},{9,10},{10,9},{11,... | collective-permute-start | bytes 1572872 | tf_op jit(solution)/shard_map/ppermute | solution.py:470
  31.2 1.0 copy-start
  58.0 27.4 %collective-permute-start.4 = (f32[8,2,2,8,128]{4,3,2,1,0:T(8,128)S(1)}, f32[8,2,2,8,128]{4,3,2,1,0:T(8,128)S(1)}, u32[]{:S(2)}, u32[]{:S(2)}) collective-permute-start(f32[8,2,2,8,128]{4,3,2,1,0:T(8,128)S(1)} %get-tuple-element.63), channel_id=1, source_target_pairs={{0,64},{32,96},{64,0},{96,32},{128,192},{160,224},{192,128},{224,1... | collective-permute-start | bytes 393224 | tf_op jit(solution)/shard_map/ppermute | solution.py:503
  71.2 20.3 %collective-permute-start.6 = (f32[4,2,2,8,128]{4,3,2,1,0:T(8,128)S(1)}, f32[4,2,2,8,128]{4,3,2,1,0:T(8,128)S(1)}, u32[]{:S(2)}, u32[]{:S(2)}) collective-permute-start(f32[4,2,2,8,128]{4,3,2,1,0:T(8,128)S(1)} %get-tuple-element.68), channel_id=1, source_target_pairs={{0,64},{32,96},{64,0},{96,32},{128,192},{160,224},{192,128},{224,1... | collective-permute-start | bytes 196616 | tf_op jit(solution)/shard_map/ppermute | solution.py:504
  85.4 35.8 %collective-permute-start.5 = (f32[16,2,2,8,128]{4,3,2,1,0:T(8,128)S(1)}, f32[16,2,2,8,128]{4,3,2,1,0:T(8,128)S(1)}, u32[]{:S(2)}, u32[]{:S(2)}) collective-permute-start(f32[16,2,2,8,128]{4,3,2,1,0:T(8,128)S(1)} %get-tuple-element.64), channel_id=1, source_target_pairs={{0,64},{32,96},{64,0},{96,32},{128,192},{160,224},{192,128},{224,1... | collective-permute-start | bytes 786440 | tf_op jit(solution)/shard_map/ppermute | solution.py:528
  91.8 6.5 %collective-permute-start.7 = (f32[24,2,8,128]{3,2,1,0:T(8,128)S(1)}, f32[24,2,8,128]{3,2,1,0:T(8,128)S(1)}, u32[]{:S(2)}, u32[]{:S(2)}) collective-permute-start(f32[24,2,8,128]{3,2,1,0:T(8,128)S(1)} %get-tuple-element.69), channel_id=1, source_target_pairs={{0,32},{32,1},{1,33},{33,2},{2,34},{34,3},{3,35},{35,131},{131,163... | collective-permute-start | bytes 589832 | tf_op jit(solution)/shard_map/ppermute | solution.py:510
  95.0 7.3 %collective-permute-start.8 = (f32[24,2,8,128]{3,2,1,0:T(8,128)S(1)}, f32[24,2,8,128]{3,2,1,0:T(8,128)S(1)}, u32[]{:S(2)}, u32[]{:S(2)}) collective-permute-start(f32[24,2,8,128]{3,2,1,0:T(8,128)S(1)} %get-tuple-element.70), channel_id=1, source_target_pairs={{32,0},{1,32},{33,1},{2,33},{34,2},{3,34},{35,3},{131,35},{163,131... | collective-permute-start | bytes 589832 | tf_op jit(solution)/shard_map/ppermute | solution.py:510
  103.2 14.4 %collective-permute-start = (f32[21,2,8,128]{3,2,1,0:T(8,128)S(1)}, f32[21,2,8,128]{3,2,1,0:T(8,128)S(1)}, u32[]{:S(2)}, u32[]{:S(2)}) collective-permute-start(f32[21,2,8,128]{3,2,1,0:T(8,128)S(1)} %get-tuple-element.145), channel_id=1, source_target_pairs={{4,8},{8,4},{36,40},{40,36},{5,9},{9,5},{37,41},{41,37},{6,10},{10... | collective-permute-start | bytes 516104 | tf_op jit(solution)/shard_map/while/body/ppermute | solution.py:470
  107.6 10.1 %collective-permute-start.1 = (f32[21,2,8,128]{3,2,1,0:T(8,128)S(1)}, f32[21,2,8,128]{3,2,1,0:T(8,128)S(1)}, u32[]{:S(2)}, u32[]{:S(2)}) collective-permute-start(f32[21,2,8,128]{3,2,1,0:T(8,128)S(1)} %get-tuple-element.146), channel_id=1, source_target_pairs={{0,4},{4,0},{32,36},{36,32},{1,5},{5,1},{33,37},{37,33},{2,6},{6,2... | collective-permute-start | bytes 516104 | tf_op jit(solution)/shard_map/while/body/ppermute | solution.py:471
  121.6 6.2 %collective-permute-start.9 = (f32[32,2,8,128]{3,2,1,0:T(8,128)S(1)}, f32[32,2,8,128]{3,2,1,0:T(8,128)S(1)}, u32[]{:S(2)}, u32[]{:S(2)}) collective-permute-start(f32[32,2,8,128]{3,2,1,0:T(8,128)S(1)} %get-tuple-element.72), channel_id=1, source_target_pairs={{0,32},{32,1},{1,33},{33,2},{2,34},{34,3},{3,35},{35,131},{131,163... | collective-permute-start | bytes 786440 | tf_op jit(solution)/shard_map/ppermute | solution.py:510
  123.5 21.7 %copy-start.2 = (f32[16,2,2,8,128]{4,3,2,1,0:T(8,128)S(1)}, f32[16,2,2,8,128]{4,3,2,1,0:T(8,128)}, u32[]{:S(2)}) copy-start(f32[16,2,2,8,128]{4,3,2,1,0:T(8,128)} %get-tuple-element.76.refs_7_) | copy-start | bytes 786436
  123.5 8.1 %collective-permute-start.10 = (f32[32,2,8,128]{3,2,1,0:T(8,128)S(1)}, f32[32,2,8,128]{3,2,1,0:T(8,128)S(1)}, u32[]{:S(2)}, u32[]{:S(2)}) collective-permute-start(f32[32,2,8,128]{3,2,1,0:T(8,128)S(1)} %get-tuple-element.73), channel_id=1, source_target_pairs={{32,0},{1,32},{33,1},{2,33},{34,2},{3,34},{35,3},{131,35},{163,131... | collective-permute-start | bytes 786440 | tf_op jit(solution)/shard_map/ppermute | solution.py:510
  132.1 9.4 %collective-permute-start.11 = (f32[36,2,8,128]{3,2,1,0:T(8,128)S(1)}, f32[36,2,8,128]{3,2,1,0:T(8,128)S(1)}, u32[]{:S(2)}, u32[]{:S(2)}) collective-permute-start(f32[36,2,8,128]{3,2,1,0:T(8,128)S(1)} %get-tuple-element.74), channel_id=1, source_target_pairs={{4,8},{8,4},{36,40},{40,36},{5,9},{9,5},{37,41},{41,37},{6,10},{10... | collective-permute-start | bytes 884744 | tf_op jit(solution)/shard_map/ppermute | solution.py:470
  136.0 9.3 %collective-permute-start.12 = (f32[36,2,8,128]{3,2,1,0:T(8,128)S(1)}, f32[36,2,8,128]{3,2,1,0:T(8,128)S(1)}, u32[]{:S(2)}, u32[]{:S(2)}) collective-permute-start(f32[36,2,8,128]{3,2,1,0:T(8,128)S(1)} %get-tuple-element.75), channel_id=1, source_target_pairs={{0,4},{4,0},{32,36},{36,32},{1,5},{5,1},{33,37},{37,33},{2,6},{6,2... | collective-permute-start | bytes 884744 | tf_op jit(solution)/shard_map/ppermute | solution.py:471
  148.7 17.1 %copy-start.1 = (f32[2,4,32,512]{3,2,1,0:T(8,128)S(1)}, f32[2,4,32,512]{3,2,1,0:T(8,128)}, u32[]{:S(2)}) copy-start(f32[2,4,32,512]{3,2,1,0:T(8,128)} %shard_map.59.start) | copy-start | bytes 1572868

commit v3 on v2

--- a/solution.py
+++ b/solution.py
@@ -74,25 +74,34 @@
     return lax.axis_index("tm"), lax.axis_index("space")
 
 
-def start_kernel(nuclei, p_in, u_in, u_start, out, cells, sems):
+def start_kernel(nuclei, p_in, u_in, u_start, out, cells, made, sems):
     tm, space = block_index()
     whole = (tm == 0) | (tm == 15)
 
+    def move(f, r, source=None):
+        rows = pl.ds(2 * r, 2)
+        if source is None:
+            return pltpu.make_async_copy(made.at[f, rows], out.at[f, rows], sems.at[2 * f + r])
+        return pltpu.make_async_copy(source.at[rows], made.at[f, rows], sems.at[4 + 2 * f + r])
+
+    def through(fields):
+        for f, source in fields:
+            for r in range(2):
+                move(f, r, source).start()
+        for f, source in fields:
+            for r in range(2):
+                move(f, r, source).wait()
+                move(f, r).start()
+
     @pl.when(~whole)
     def _():
-        p_copy = pltpu.make_async_copy(p_in.at[0], out.at[0], sems.at[0])
-        u_copy = pltpu.make_async_copy(u_in.at[0], out.at[1], sems.at[1])
-        p_copy.start()
-        u_copy.start()
-        p_copy.wait()
-        u_copy.wait()
+        through([(0, p_in.at[0]), (1, u_in.at[0])])
 
     @pl.when(whole)
     def _():
-        u_copy = pltpu.make_async_copy(u_start, out.at[1], sems.at[1])
-        n_copy = pltpu.make_async_copy(nuclei, cells, sems.at[0])
-        u_copy.start()
+        n_copy = pltpu.make_async_copy(nuclei, cells, sems.at[8])
         n_copy.start()
+        through([(1, u_start)])
         n_copy.wait()
         zs = lax.broadcasted_iota(jnp.int32, (8, 512), 0)
         ys = lax.broadcasted_iota(jnp.int32, (8, 512), 1)
@@ -111,21 +120,24 @@
                     here = sides[n] + dx * dx
                     best = here if best is None else jnp.minimum(best, here)
                 b = jnp.exp(-best.astype(jnp.float32) / WIDTH_SQ)
-                out[0, r, 8 * g : 8 * g + 8, :] = 2.0 * b - 1.0
-        u_copy.wait()
+                made[0, r, 8 * g : 8 * g + 8, :] = 2.0 * b - 1.0
+        for r in range(2):
+            move(0, r).start()
+
+    for f in range(2):
+        for r in range(2):
+            move(f, r).wait()
 
 
 def transpose_lanes(parts):
     slot = lax.broadcasted_iota(jnp.int32, (8, 128), 1) // 16
-    parts = list(parts)
-    for d in (4, 2, 1):
-        low = (slot & d) == 0
-        for a in range(8):
-            if not a & d:
-                top, bottom = parts[a], parts[a + d]
-                parts[a] = jnp.where(low, top, pltpu.roll(bottom, 16 * d, 1))
-                parts[a + d] = jnp.where(low, pltpu.roll(top, 128 - 16 * d, 1), bottom)
-    return parts
+    parts = [pltpu.roll(part, 16 * a, 1) if a else part for a, part in enumerate(parts)]
+    for d in (1, 2, 4):
+        move = (slot & d) != 0
+        parts = [jnp.where(move, parts[(i + d) % 8], parts[i]) for i in range(8)]
+    return [
+        pltpu.roll(parts[-j % 8], 128 - 16 * j, 1) if j else parts[0] for j in range(8)
+    ]
 
 
 def relax_kernel(start, odd, even, out, one, two, coarse):
@@ -286,12 +298,12 @@
                         piece = get(slot, f, 2 * quad + q // 2)
                     at = 16 * (q % 2)
                     r_part = pltpu.roll(piece, (8 * q - at - 8) % 128, 1)
-                    l_part = pltpu.roll(piece, (8 * q - at) % 128, 1) if 8 * q != at else piece
+                    l_part = pltpu.roll(piece, (8 * q - at + 24) % 128, 1)
                     if q == 0:
                         r_edge, l_edge = r_part, l_part
                     else:
                         r_edge = jnp.where(part == q, r_part, r_edge)
-                        l_edge = jnp.where(part == q, l_part, l_edge)
+                        l_edge = jnp.where(part == (q + 3) % 4, l_part, l_edge)
                 right[4 * slot + quad, f] = r_edge
                 left[4 * slot + quad, f] = l_edge
 
@@ -304,12 +316,10 @@
         if slot == phase.steps:
             return value
         quad, q = 4 * slot + r // 4, r % 4
-        l_halo, r_halo = from_left[quad, f], from_right[quad, f]
+        halo = jnp.where(part == q, from_left[quad, f], from_right[quad, f])
         if q != 0:
-            l_halo = pltpu.roll(l_halo, 128 - 8 * q, 1)
-        if q != 3:
-            r_halo = pltpu.roll(r_halo, 24 - 8 * q, 1)
-        return jnp.where(part == 0, l_halo, jnp.where(part == 3, r_halo, value))
+            halo = pltpu.roll(halo, 128 - 8 * q, 1)
+        return jnp.where((part == 0) | (part == 3), halo, value)
 
     return row
 
@@ -428,37 +438,50 @@
                         emit(k, pair, f, pack(f, pair))
 
 
-def finish_kernel(start, got, p_out, u_out):
+def finish_kernel(start, got, p_out, u_out, made, sems):
     tm, _ = block_index()
+    outs = p_out, u_out
 
     @pl.when(tm == 0)
     def _():
-        p_out[0] = start[0]
-        u_out[0] = start[1]
+        copies = [pltpu.make_async_copy(start.at[f], outs[f].at[0], sems.at[f]) for f in range(2)]
+        for copy in copies:
+            copy.start()
+        for copy in copies:
+            copy.wait()
 
     @pl.when(tm != 0)
     def _():
-        for f, out in enumerate((p_out, u_out)):
+        copies = []
+        for f in range(2):
             for rp in range(2):
                 for b in range(4):
                     parts = transpose_lanes([got[MEMBER[8 * b + j], f, rp] for j in range(8)])
                     for g in range(4):
                         for rr in range(2):
                             at = slice(8 * g, 8 * g + 8), slice(128 * b, 128 * b + 128)
-                            out[0, 2 * rp + rr, at[0], at[1]] = parts[2 * g + rr]
+                            made[f, 2 * rp + rr, at[0], at[1]] = parts[2 * g + rr]
+                rows = pl.ds(2 * rp, 2)
+                copy = pltpu.make_async_copy(
+                    made.at[f, rows], outs[f].at[0, rows], sems.at[2 * f + rp]
+                )
+                copy.start()
+                copies.append(copy)
+        for copy in copies:
+            copy.wait()
 
 
 VMEM = pl.BlockSpec(memory_space=pltpu.VMEM)
 ANY = pl.BlockSpec(memory_space=pl.ANY)
 
 
-def call(kernel, outs, args, scratch=(), specs=None, grant=40):
+def call(kernel, outs, args, scratch=(), specs=None, grant=40, out_spec=None):
     shapes = [jax.ShapeDtypeStruct(s, jnp.float32) for s in outs]
     return pl.pallas_call(
         kernel,
         out_shape=shapes if len(shapes) > 1 else shapes[0],
         in_specs=specs or [VMEM] * len(args),
-        out_specs=[VMEM] * len(shapes) if len(shapes) > 1 else VMEM,
+        out_specs=[out_spec or VMEM] * len(shapes) if len(shapes) > 1 else out_spec or VMEM,
         scratch_shapes=[pltpu.VMEM(s, jnp.float32) if isinstance(s, tuple) else s for s in scratch],
         cost_estimate=pl.CostEstimate(flops=8, bytes_accessed=8, transcendentals=0),
         compiler_params=pltpu.CompilerParams(vmem_limit_bytes=grant * 1024 * 1024),
@@ -477,11 +500,13 @@
         start_kernel,
         [(2, 4, 32, 512)],
         [nuclei.T, phase_guess, solute_guess, solute_start],
-        scratch=[pltpu.SMEM((3, 8), jnp.int32), pltpu.SemaphoreType.DMA((2,))],
+        scratch=[pltpu.SMEM((3, 8), jnp.int32), (2, 4, 32, 512), pltpu.SemaphoreType.DMA((9,))],
+        out_spec=ANY,
         specs=[ANY] * 4,
         grant=60,
     )
-    odd, even = exchange_rows((start, start), "space", space_pairs)
+    even = lax.ppermute(start, "space", space_pairs(0))
+    odd = lax.ppermute(start, "space", space_pairs(1))
     packed = call(
         relax_kernel,
         [(32, 2, 2, 8, 128)],
@@ -534,7 +559,14 @@
     known += lanes(PHASES[1], known)
     got = advance(PHASES[1], known, [before])
     back = lax.all_to_all(got, AXES, 0, 0, tiled=True, axis_index_groups=PLANE_GROUPS)
-    return call(finish_kernel, [(1, 4, 32, 512)] * 2, [start, back])
+    return call(
+        finish_kernel,
+        [(1, 4, 32, 512)] * 2,
+        [start, back],
+        scratch=[(2, 4, 32, 512), pltpu.SemaphoreType.DMA((4,))],
+        specs=[ANY, VMEM],
+        out_spec=ANY,
+    )
 
 
 def solution(mesh):

time: 169 us -> 167 us (0.988)
  Pallas kernels: 19 us -> 17.3 us
    ppermute x0 -> x2, starting transfers between devices: none -> 18.4 us  [the longest x1 14.4 us: local(): odd = lax.ppermute(start, 'space', space_pairs(1))]
    ppermute x3 -> x2, starting transfers between devices: 22.6 us -> 8.42 us  [exchange_rows(): got_odd = lax.ppermute(odd, axis, pairs(1))]
    ppermute x0 -> x2, waiting for transfers between devices: none -> 10.2 us  [the longest x1 10.2 us: local(): odd = lax.ppermute(start, 'space', space_pairs(1))]
    ppermute x3 -> x2, waiting for transfers between devices: 22 us -> 12 us  [exchange_rows(): got_odd = lax.ppermute(odd, axis, pairs(1))]
    ppermute x3 -> x2, starting transfers between devices: 7.79 us -> 3.84 us  [exchange_rows(): got_even = lax.ppermute(even, axis, pairs(0))]
    pallas_call x9, Pallas kernels: 18.5 us -> 16.7 us  [call(): pl.pallas_call(kernel, out_shape=shapes if len(shapes) > 1 else shapes[0]...]
    ppermute x3 -> x2, waiting for transfers between devices: 3.81 us -> 3.8 us  [exchange_rows(): got_even = lax.ppermute(even, axis, pairs(0))]
where the time goes in v3:
time: 167 us
  starting transfers between devices  64 us (38%)
  waiting for transfers between devices  46.4 us (28%)
  blocking collectives  35.9 us (21%)
  Pallas kernels  17.3 us (10%)
    all_to_all x1, blocking collectives, local(): lax.all_to_all(packed, AXES, 0, 0, tiled=True, axis_index_groups=PLANE_GR...  18.7 us
    all_to_all x1, blocking collectives, local(): lax.all_to_all(got, AXES, 0, 0, tiled=True, axis_index_groups=PLANE_GROUPS)  17.2 us
    pallas_call x9, Pallas kernels, call(): pl.pallas_call(kernel, out_shape=shapes if len(shapes) > 1 else shapes[0]...  16.7 us
    ppermute x1, starting transfers between devices, local(): odd = lax.ppermute(start, 'space', space_pairs(1))  14.4 us
    ppermute x1, starting transfers between devices, local(): near = lax.ppermute(near, 'tm', ACROSS)  13.3 us
    ppermute x1, waiting for transfers between devices, local(): near = lax.ppermute(near, 'tm', ACROSS)  12.2 us
    ppermute x4, starting transfers between devices, lanes(): return [lax.ppermute(right, AXES, RIGHT), lax.ppermute(left, AXES, LEFT)]  12.2 us
    ppermute x2, waiting for transfers between devices, exchange_rows(): got_odd = lax.ppermute(odd, axis, pairs(1))  12 us
  transfers between devices with their start and end apart: 13, of which 7 were waited for; matrix products, arithmetic and copies ran while one was open for 0% of the time, Pallas kernels for 2%

profile of v3, /device:TPU:1, one launch (start us, length us, event | category | flops | bytes accessed | tf_op | source)
XLA Modules:
  0.0 166.9 jit_solution(1169337300406825914)
XLA Ops:
  0.6 1.8 %shard_map.59.start = f32[2,4,32,512]{3,2,1,0:T(8,128)} custom-call(s32[3,8]{1,0:T(4,128)} %bitcast.2, f32[1,4,32,512]{3,2,1,0:T(8,128)} %p_in.1, f32[1,4,32,512]{3,2,1,0:T(8,128)} %u_in.1, f32[4,32,512]{2,1,0:T(8,128)} %u_start.1), custom_call_target="tpu_custom_call" | custom-call | flops 8 | bytes 8 | tf_op jit(solution)/shard_map/pallas_call | solution.py:480
  2.5 3.9 %collective-permute-start.3 = (f32[2,4,32,512]{3,2,1,0:T(8,128)}, f32[2,4,32,512]{3,2,1,0:T(8,128)S(1)}, u32[]{:S(2)}, u32[]{:S(2)}) collective-permute-start(f32[2,4,32,512]{3,2,1,0:T(8,128)} %shard_map.59.start), channel_id=1, source_target_pairs={{0,1},{1,0},{2,3},{3,2},{4,5},{5,4},{6,7},{7,6},{8,9},{9,8},{10,11... | collective-permute-start | bytes 1572872 | tf_op jit(solution)/shard_map/ppermute | solution.py:508
  6.4 14.4 %collective-permute-start.2 = (f32[2,4,32,512]{3,2,1,0:T(8,128)}, f32[2,4,32,512]{3,2,1,0:T(8,128)S(1)}, u32[]{:S(2)}, u32[]{:S(2)}) collective-permute-start(f32[2,4,32,512]{3,2,1,0:T(8,128)} %shard_map.59.start), channel_id=1, source_target_pairs={{1,2},{2,1},{3,4},{4,3},{5,6},{6,5},{7,8},{8,7},{9,10},{10,9},{11,... | collective-permute-start | bytes 1572872 | tf_op jit(solution)/shard_map/ppermute | solution.py:509
  20.8 0.0 collective-permute-done.3.even
  20.9 10.2 %collective-permute-done.2.odd = f32[2,4,32,512]{3,2,1,0:T(8,128)S(1)} collective-permute-done((f32[2,4,32,512]{3,2,1,0:T(8,128)}, f32[2,4,32,512]{3,2,1,0:T(8,128)S(1)}, u32[]{:S(2)}, u32[]{:S(2)}) %collective-permute-start.2) | collective-permute-done | bytes 524320 | tf_op jit(solution)/shard_map/ppermute | solution.py:509
  31.0 0.0 copy-start
  31.0 1.0 copy-done
  32.1 5.9 %shard_map.60 = f32[32,2,2,8,128]{4,3,2,1,0:T(8,128)S(1)} custom-call(f32[2,4,32,512]{3,2,1,0:T(8,128)S(1)} %copy-done, f32[2,4,32,512]{3,2,1,0:T(8,128)S(1)} %collective-permute-done.2.odd, f32[2,4,32,512]{3,2,1,0:T(8,128)S(1)} %collective-permute-done.3.even), custom_call_target="tpu_custom_call" | custom-call | flops 8 | bytes 8 | tf_op jit(solution)/shard_map/pallas_call | solution.py:480
  38.0 18.7 %all_to_all.10.own.refs_0_ = f32[32,2,2,8,128]{4,3,2,1,0:T(8,128)S(1)} all-to-all(f32[32,2,2,8,128]{4,3,2,1,0:T(8,128)S(1)} %shard_map.60), channel_id=1, replica_groups={{0,1,2,3,32,33,34,35,128,129,130,131,160,161,162,163,256,257,258,259,28..., dimensions={0} | all-to-all | bytes 1048576 | tf_op jit(solution)/shard_map/all_to_all | solution.py:516
  56.7 0.5 shard_map.61
  57.2 13.3 %collective-permute-start.4 = (f32[8,2,2,8,128]{4,3,2,1,0:T(8,128)S(1)}, f32[8,2,2,8,128]{4,3,2,1,0:T(8,128)S(1)}, u32[]{:S(2)}, u32[]{:S(2)}) collective-permute-start(f32[8,2,2,8,128]{4,3,2,1,0:T(8,128)S(1)} %get-tuple-element.63), channel_id=1, source_target_pairs={{0,64},{32,96},{64,0},{96,32},{128,192},{160,224},{192,128},{224,1... | collective-permute-start | bytes 393224 | tf_op jit(solution)/shard_map/ppermute | solution.py:528
  70.5 1.9 %collective-permute-start.6 = (f32[4,2,2,8,128]{4,3,2,1,0:T(8,128)S(1)}, f32[4,2,2,8,128]{4,3,2,1,0:T(8,128)S(1)}, u32[]{:S(2)}, u32[]{:S(2)}) collective-permute-start(f32[4,2,2,8,128]{4,3,2,1,0:T(8,128)S(1)} %get-tuple-element.68), channel_id=1, source_target_pairs={{0,64},{32,96},{64,0},{96,32},{128,192},{160,224},{192,128},{224,1... | collective-permute-start | bytes 196616 | tf_op jit(solution)/shard_map/ppermute | solution.py:529
  72.5 12.2 %collective-permute-done.4 = f32[8,2,2,8,128]{4,3,2,1,0:T(8,128)S(1)} collective-permute-done((f32[8,2,2,8,128]{4,3,2,1,0:T(8,128)S(1)}, f32[8,2,2,8,128]{4,3,2,1,0:T(8,128)S(1)}, u32[]{:S(2)}, u32[]{:S(2)}) %collective-permute-start.4) | collective-permute-done | bytes 131104 | tf_op jit(solution)/shard_map/ppermute | solution.py:528
  84.7 6.0 %collective-permute-start.5 = (f32[16,2,2,8,128]{4,3,2,1,0:T(8,128)S(1)}, f32[16,2,2,8,128]{4,3,2,1,0:T(8,128)S(1)}, u32[]{:S(2)}, u32[]{:S(2)}) collective-permute-start(f32[16,2,2,8,128]{4,3,2,1,0:T(8,128)S(1)} %get-tuple-element.64), channel_id=1, source_target_pairs={{0,64},{32,96},{64,0},{96,32},{128,192},{160,224},{192,128},{224,1... | collective-permute-start | bytes 786440 | tf_op jit(solution)/shard_map/ppermute | solution.py:553
  90.7 0.0 collective-permute-done.6
  90.8 0.4 shard_map.62
  91.2 3.1 %collective-permute-start.7 = (f32[24,2,8,128]{3,2,1,0:T(8,128)S(1)}, f32[24,2,8,128]{3,2,1,0:T(8,128)S(1)}, u32[]{:S(2)}, u32[]{:S(2)}) collective-permute-start(f32[24,2,8,128]{3,2,1,0:T(8,128)S(1)} %get-tuple-element.69), channel_id=1, source_target_pairs={{0,32},{32,1},{1,33},{33,2},{2,34},{34,3},{3,35},{35,131},{131,163... | collective-permute-start | bytes 589832 | tf_op jit(solution)/shard_map/ppermute | solution.py:535
  94.4 3.3 %collective-permute-start.8 = (f32[24,2,8,128]{3,2,1,0:T(8,128)S(1)}, f32[24,2,8,128]{3,2,1,0:T(8,128)S(1)}, u32[]{:S(2)}, u32[]{:S(2)}) collective-permute-start(f32[24,2,8,128]{3,2,1,0:T(8,128)S(1)} %get-tuple-element.70), channel_id=1, source_target_pairs={{32,0},{1,32},{33,1},{2,33},{34,2},{3,34},{35,3},{131,35},{163,131... | collective-permute-start | bytes 589832 | tf_op jit(solution)/shard_map/ppermute | solution.py:535
  97.6 0.0 collective-permute-done.7
  97.7 3.9 %collective-permute-done.8 = f32[24,2,8,128]{3,2,1,0:T(8,128)S(1)} collective-permute-done((f32[24,2,8,128]{3,2,1,0:T(8,128)S(1)}, f32[24,2,8,128]{3,2,1,0:T(8,128)S(1)}, u32[]{:S(2)}, u32[]{:S(2)}) %collective-permute-start.8) | collective-permute-done | bytes 196640 | tf_op jit(solution)/shard_map/ppermute | solution.py:535
  101.6 19.2 %while.12 = (s32[]{:T(128)}, f32[16,2,2,8,128]{4,3,2,1,0:T(8,128)}, f32[2,8,8,128]{3,2,1,0:T(8,128)S(1)}, s32[]{:T(128)}, f32[32,2,2,8,128]{4,3,2,1,0:T(8,128)S(...) while((s32[]{:T(128)}, f32[16,2,2,8,128]{4,3,2,1,0:T(8,128)}, ...), condition=%wide.region_1.0_spmd, body=%wide.region_0.0_spmd.sunk | while | flops 18 | bytes 1376445 | solution.py:555
  102.3 0.2 body.2
  102.5 4.8 %collective-permute-start = (f32[21,2,8,128]{3,2,1,0:T(8,128)S(1)}, f32[21,2,8,128]{3,2,1,0:T(8,128)S(1)}, u32[]{:S(2)}, u32[]{:S(2)}) collective-permute-start(f32[21,2,8,128]{3,2,1,0:T(8,128)S(1)} %get-tuple-element.145), channel_id=1, source_target_pairs={{4,8},{8,4},{36,40},{40,36},{5,9},{9,5},{37,41},{41,37},{6,10},{10... | collective-permute-start | bytes 516104 | tf_op jit(solution)/shard_map/while/body/ppermute | solution.py:493
  107.3 1.9 %collective-permute-start.1 = (f32[21,2,8,128]{3,2,1,0:T(8,128)S(1)}, f32[21,2,8,128]{3,2,1,0:T(8,128)S(1)}, u32[]{:S(2)}, u32[]{:S(2)}) collective-permute-start(f32[21,2,8,128]{3,2,1,0:T(8,128)S(1)} %get-tuple-element.146), channel_id=1, source_target_pairs={{0,4},{4,0},{32,36},{36,32},{1,5},{5,1},{33,37},{37,33},{2,6},{6,2... | collective-permute-start | bytes 516104 | tf_op jit(solution)/shard_map/while/body/ppermute | solution.py:494
  109.2 8.1 %collective-permute-done.refs_4_ = f32[21,2,8,128]{3,2,1,0:T(8,128)S(1)} collective-permute-done((f32[21,2,8,128]{3,2,1,0:T(8,128)S(1)}, f32[21,2,8,128]{3,2,1,0:T(8,128)S(1)}, u32[]{:S(2)}, u32[]{:S(2)}) %collective-permute-start) | collective-permute-done | bytes 172064 | tf_op jit(solution)/shard_map/while/body/ppermute | solution.py:493
  117.4 0.0 collective-permute-done.1.refs_5_
  117.4 2.7 %body.3 = (f32[16,2,2,8,128]{4,3,2,1,0:T(8,128)}, f32[2,8,8,128]{3,2,1,0:T(8,128)S(1)}) custom-call(f32[32,2,2,8,128]{4,3,2,1,0:T(8,128)S(1)} %get-tuple-element.171.refs_1_.refs_0_, f32[12,2,2,8,128]{4,3,2,1,0:T(8,128)S(1)} %get-tuple-element.172.refs_2_.refs_1_, f32[24,2,8,128]{3,2,1,0:T(8,128)S(1)} %get-tuple-element.173.refs_3_.refs_2_, ...), custom_call_target="tpu_custom_call" | custom-call | flops 8 | bytes 8 | tf_op jit(solution)/shard_map/while/body/pallas_call | solution.py:480
  120.8 0.0 collective-permute-done.5.refs_1_
  120.8 0.5 shard_map.63
  121.4 1.9 %collective-permute-start.9 = (f32[32,2,8,128]{3,2,1,0:T(8,128)S(1)}, f32[32,2,8,128]{3,2,1,0:T(8,128)S(1)}, u32[]{:S(2)}, u32[]{:S(2)}) collective-permute-start(f32[32,2,8,128]{3,2,1,0:T(8,128)S(1)} %get-tuple-element.72), channel_id=1, source_target_pairs={{0,32},{32,1},{1,33},{33,2},{2,34},{34,3},{3,35},{35,131},{131,163... | collective-permute-start | bytes 786440 | tf_op jit(solution)/shard_map/ppermute | solution.py:535
  123.3 0.0 copy-start.2
  123.3 3.8 %collective-permute-start.10 = (f32[32,2,8,128]{3,2,1,0:T(8,128)S(1)}, f32[32,2,8,128]{3,2,1,0:T(8,128)S(1)}, u32[]{:S(2)}, u32[]{:S(2)}) collective-permute-start(f32[32,2,8,128]{3,2,1,0:T(8,128)S(1)} %get-tuple-element.73), channel_id=1, source_target_pairs={{32,0},{1,32},{33,1},{2,33},{34,2},{3,34},{35,3},{131,35},{163,131... | collective-permute-start | bytes 786440 | tf_op jit(solution)/shard_map/ppermute | solution.py:535
  127.1 0.0 collective-permute-done.9.refs_3_
  127.1 4.3 %collective-permute-done.10.refs_4_ = f32[32,2,8,128]{3,2,1,0:T(8,128)S(1)} collective-permute-done((f32[32,2,8,128]{3,2,1,0:T(8,128)S(1)}, f32[32,2,8,128]{3,2,1,0:T(8,128)S(1)}, u32[]{:S(2)}, u32[]{:S(2)}) %collective-permute-start.10) | collective-permute-done | bytes 262176 | tf_op jit(solution)/shard_map/ppermute | solution.py:535
  131.4 0.3 shard_map.64
  131.8 3.7 %collective-permute-start.11 = (f32[36,2,8,128]{3,2,1,0:T(8,128)S(1)}, f32[36,2,8,128]{3,2,1,0:T(8,128)S(1)}, u32[]{:S(2)}, u32[]{:S(2)}) collective-permute-start(f32[36,2,8,128]{3,2,1,0:T(8,128)S(1)} %get-tuple-element.74), channel_id=1, source_target_pairs={{4,8},{8,4},{36,40},{40,36},{5,9},{9,5},{37,41},{41,37},{6,10},{10... | collective-permute-start | bytes 884744 | tf_op jit(solution)/shard_map/ppermute | solution.py:493
  135.4 1.9 %collective-permute-start.12 = (f32[36,2,8,128]{3,2,1,0:T(8,128)S(1)}, f32[36,2,8,128]{3,2,1,0:T(8,128)S(1)}, u32[]{:S(2)}, u32[]{:S(2)}) collective-permute-start(f32[36,2,8,128]{3,2,1,0:T(8,128)S(1)} %get-tuple-element.75), channel_id=1, source_target_pairs={{0,4},{4,0},{32,36},{36,32},{1,5},{5,1},{33,37},{37,33},{2,6},{6,2... | collective-permute-start | bytes 884744 | tf_op jit(solution)/shard_map/ppermute | solution.py:494
  137.4 3.8 %collective-permute-done.11.refs_5_ = f32[36,2,8,128]{3,2,1,0:T(8,128)S(1)} collective-permute-done((f32[36,2,8,128]{3,2,1,0:T(8,128)S(1)}, f32[36,2,8,128]{3,2,1,0:T(8,128)S(1)}, u32[]{:S(2)}, u32[]{:S(2)}) %collective-permute-start.11) | collective-permute-done | bytes 294944 | tf_op jit(solution)/shard_map/ppermute | solution.py:493
  141.2 3.8 %collective-permute-done.12.refs_6_ = f32[36,2,8,128]{3,2,1,0:T(8,128)S(1)} collective-permute-done((f32[36,2,8,128]{3,2,1,0:T(8,128)S(1)}, f32[36,2,8,128]{3,2,1,0:T(8,128)S(1)}, u32[]{:S(2)}, u32[]{:S(2)}) %collective-permute-start.12) | collective-permute-done | bytes 294944 | tf_op jit(solution)/shard_map/ppermute | solution.py:494
  145.0 0.0 copy-done.2
  145.0 3.2 %shard_map.65 = f32[32,2,2,8,128]{4,3,2,1,0:T(8,128)S(1)} custom-call(f32[32,2,2,8,128]{4,3,2,1,0:T(8,128)S(1)} %get-tuple-element.198, f32[16,2,2,8,128]{4,3,2,1,0:T(8,128)S(1)} %collective-permute-done.5.refs_1_, f32[2,8,8,128]{3,2,1,0:T(8,128)S(1)} %get-tuple-element.71.refs_2_, f32[32,2,8,128]{3,2,1,0:T(8,128)S(1)} %collective-permute-done.9.refs_3_, ...), custom_call_target="tpu_custom_call" | custom-call | flops 8 | bytes 8 | tf_op jit(solution)/shard_map/pallas_call | solution.py:480
  148.2 0.0 copy-start.1
  148.2 17.2 %all_to_all.11.got = f32[32,2,2,8,128]{4,3,2,1,0:T(8,128)S(1)} all-to-all(f32[32,2,2,8,128]{4,3,2,1,0:T(8,128)S(1)} %shard_map.65), channel_id=1, replica_groups={{0,1,2,3,32,33,34,35,128,129,130,131,160,161,162,163,256,257,258,259,28..., dimensions={0} | all-to-all | bytes 1048576 | tf_op jit(solution)/shard_map/all_to_all | solution.py:561
  165.4 0.0 copy-done.1
  165.4 1.5 shard_map.66
  (2 shorter events, 0.0 us)
Async XLA Ops:
  2.5 18.4 %collective-permute-start.3 = (f32[2,4,32,512]{3,2,1,0:T(8,128)}, f32[2,4,32,512]{3,2,1,0:T(8,128)S(1)}, u32[]{:S(2)}, u32[]{:S(2)}) collective-permute-start(f32[2,4,32,512]{3,2,1,0:T(8,128)} %shard_map.59.start), channel_id=1, source_target_pairs={{0,1},{1,0},{2,3},{3,2},{4,5},{5,4},{6,7},{7,6},{8,9},{9,8},{10,11... | collective-permute-start | bytes 1572872 | tf_op jit(solution)/shard_map/ppermute | solution.py:508
  6.4 24.6 %collective-permute-start.2 = (f32[2,4,32,512]{3,2,1,0:T(8,128)}, f32[2,4,32,512]{3,2,1,0:T(8,128)S(1)}, u32[]{:S(2)}, u32[]{:S(2)}) collective-permute-start(f32[2,4,32,512]{3,2,1,0:T(8,128)} %shard_map.59.start), channel_id=1, source_target_pairs={{1,2},{2,1},{3,4},{4,3},{5,6},{6,5},{7,8},{8,7},{9,10},{10,9},{11,... | collective-permute-start | bytes 1572872 | tf_op jit(solution)/shard_map/ppermute | solution.py:509
  31.0 1.0 copy-start
  57.2 27.4 %collective-permute-start.4 = (f32[8,2,2,8,128]{4,3,2,1,0:T(8,128)S(1)}, f32[8,2,2,8,128]{4,3,2,1,0:T(8,128)S(1)}, u32[]{:S(2)}, u32[]{:S(2)}) collective-permute-start(f32[8,2,2,8,128]{4,3,2,1,0:T(8,128)S(1)} %get-tuple-element.63), channel_id=1, source_target_pairs={{0,64},{32,96},{64,0},{96,32},{128,192},{160,224},{192,128},{224,1... | collective-permute-start | bytes 393224 | tf_op jit(solution)/shard_map/ppermute | solution.py:528
  70.5 20.2 %collective-permute-start.6 = (f32[4,2,2,8,128]{4,3,2,1,0:T(8,128)S(1)}, f32[4,2,2,8,128]{4,3,2,1,0:T(8,128)S(1)}, u32[]{:S(2)}, u32[]{:S(2)}) collective-permute-start(f32[4,2,2,8,128]{4,3,2,1,0:T(8,128)S(1)} %get-tuple-element.68), channel_id=1, source_target_pairs={{0,64},{32,96},{64,0},{96,32},{128,192},{160,224},{192,128},{224,1... | collective-permute-start | bytes 196616 | tf_op jit(solution)/shard_map/ppermute | solution.py:529
  84.7 36.2 %collective-permute-start.5 = (f32[16,2,2,8,128]{4,3,2,1,0:T(8,128)S(1)}, f32[16,2,2,8,128]{4,3,2,1,0:T(8,128)S(1)}, u32[]{:S(2)}, u32[]{:S(2)}) collective-permute-start(f32[16,2,2,8,128]{4,3,2,1,0:T(8,128)S(1)} %get-tuple-element.64), channel_id=1, source_target_pairs={{0,64},{32,96},{64,0},{96,32},{128,192},{160,224},{192,128},{224,1... | collective-permute-start | bytes 786440 | tf_op jit(solution)/shard_map/ppermute | solution.py:553
  91.2 6.5 %collective-permute-start.7 = (f32[24,2,8,128]{3,2,1,0:T(8,128)S(1)}, f32[24,2,8,128]{3,2,1,0:T(8,128)S(1)}, u32[]{:S(2)}, u32[]{:S(2)}) collective-permute-start(f32[24,2,8,128]{3,2,1,0:T(8,128)S(1)} %get-tuple-element.69), channel_id=1, source_target_pairs={{0,32},{32,1},{1,33},{33,2},{2,34},{34,3},{3,35},{35,131},{131,163... | collective-permute-start | bytes 589832 | tf_op jit(solution)/shard_map/ppermute | solution.py:535
  94.4 7.3 %collective-permute-start.8 = (f32[24,2,8,128]{3,2,1,0:T(8,128)S(1)}, f32[24,2,8,128]{3,2,1,0:T(8,128)S(1)}, u32[]{:S(2)}, u32[]{:S(2)}) collective-permute-start(f32[24,2,8,128]{3,2,1,0:T(8,128)S(1)} %get-tuple-element.70), channel_id=1, source_target_pairs={{32,0},{1,32},{33,1},{2,33},{34,2},{3,34},{35,3},{131,35},{163,131... | collective-permute-start | bytes 589832 | tf_op jit(solution)/shard_map/ppermute | solution.py:535
  102.5 14.8 %collective-permute-start = (f32[21,2,8,128]{3,2,1,0:T(8,128)S(1)}, f32[21,2,8,128]{3,2,1,0:T(8,128)S(1)}, u32[]{:S(2)}, u32[]{:S(2)}) collective-permute-start(f32[21,2,8,128]{3,2,1,0:T(8,128)S(1)} %get-tuple-element.145), channel_id=1, source_target_pairs={{4,8},{8,4},{36,40},{40,36},{5,9},{9,5},{37,41},{41,37},{6,10},{10... | collective-permute-start | bytes 516104 | tf_op jit(solution)/shard_map/while/body/ppermute | solution.py:493
  107.3 10.1 %collective-permute-start.1 = (f32[21,2,8,128]{3,2,1,0:T(8,128)S(1)}, f32[21,2,8,128]{3,2,1,0:T(8,128)S(1)}, u32[]{:S(2)}, u32[]{:S(2)}) collective-permute-start(f32[21,2,8,128]{3,2,1,0:T(8,128)S(1)} %get-tuple-element.146), channel_id=1, source_target_pairs={{0,4},{4,0},{32,36},{36,32},{1,5},{5,1},{33,37},{37,33},{2,6},{6,2... | collective-permute-start | bytes 516104 | tf_op jit(solution)/shard_map/while/body/ppermute | solution.py:494
  121.4 5.8 %collective-permute-start.9 = (f32[32,2,8,128]{3,2,1,0:T(8,128)S(1)}, f32[32,2,8,128]{3,2,1,0:T(8,128)S(1)}, u32[]{:S(2)}, u32[]{:S(2)}) collective-permute-start(f32[32,2,8,128]{3,2,1,0:T(8,128)S(1)} %get-tuple-element.72), channel_id=1, source_target_pairs={{0,32},{32,1},{1,33},{33,2},{2,34},{34,3},{3,35},{35,131},{131,163... | collective-permute-start | bytes 786440 | tf_op jit(solution)/shard_map/ppermute | solution.py:535
  123.3 21.7 %copy-start.2 = (f32[16,2,2,8,128]{4,3,2,1,0:T(8,128)S(1)}, f32[16,2,2,8,128]{4,3,2,1,0:T(8,128)}, u32[]{:S(2)}) copy-start(f32[16,2,2,8,128]{4,3,2,1,0:T(8,128)} %get-tuple-element.76.refs_7_) | copy-start | bytes 786436
  123.3 8.1 %collective-permute-start.10 = (f32[32,2,8,128]{3,2,1,0:T(8,128)S(1)}, f32[32,2,8,128]{3,2,1,0:T(8,128)S(1)}, u32[]{:S(2)}, u32[]{:S(2)}) collective-permute-start(f32[32,2,8,128]{3,2,1,0:T(8,128)S(1)} %get-tuple-element.73), channel_id=1, source_target_pairs={{32,0},{1,32},{33,1},{2,33},{34,2},{3,34},{35,3},{131,35},{163,131... | collective-permute-start | bytes 786440 | tf_op jit(solution)/shard_map/ppermute | solution.py:535
  131.8 9.4 %collective-permute-start.11 = (f32[36,2,8,128]{3,2,1,0:T(8,128)S(1)}, f32[36,2,8,128]{3,2,1,0:T(8,128)S(1)}, u32[]{:S(2)}, u32[]{:S(2)}) collective-permute-start(f32[36,2,8,128]{3,2,1,0:T(8,128)S(1)} %get-tuple-element.74), channel_id=1, source_target_pairs={{4,8},{8,4},{36,40},{40,36},{5,9},{9,5},{37,41},{41,37},{6,10},{10... | collective-permute-start | bytes 884744 | tf_op jit(solution)/shard_map/ppermute | solution.py:493
  135.4 9.5 %collective-permute-start.12 = (f32[36,2,8,128]{3,2,1,0:T(8,128)S(1)}, f32[36,2,8,128]{3,2,1,0:T(8,128)S(1)}, u32[]{:S(2)}, u32[]{:S(2)}) collective-permute-start(f32[36,2,8,128]{3,2,1,0:T(8,128)S(1)} %get-tuple-element.75), channel_id=1, source_target_pairs={{0,4},{4,0},{32,36},{36,32},{1,5},{5,1},{33,37},{37,33},{2,6},{6,2... | collective-permute-start | bytes 884744 | tf_op jit(solution)/shard_map/ppermute | solution.py:494
  148.2 17.2 %copy-start.1 = (f32[2,4,32,512]{3,2,1,0:T(8,128)S(1)}, f32[2,4,32,512]{3,2,1,0:T(8,128)}, u32[]{:S(2)}) copy-start(f32[2,4,32,512]{3,2,1,0:T(8,128)} %shard_map.59.start) | copy-start | bytes 1572868

commit v4 on v3

--- a/solution.py
+++ b/solution.py
@@ -127,6 +127,12 @@
     for f in range(2):
         for r in range(2):
             move(f, r).wait()
+
+
+def stage_kernel(start, out, sem):
+    copy = pltpu.make_async_copy(start, out, sem)
+    copy.start()
+    copy.wait()
 
 
 def transpose_lanes(parts):
@@ -475,7 +481,7 @@
 ANY = pl.BlockSpec(memory_space=pl.ANY)
 
 
-def call(kernel, outs, args, scratch=(), specs=None, grant=40, out_spec=None):
+def call(kernel, outs, args, scratch=(), specs=None, grant=40, out_spec=None, cost=8):
     shapes = [jax.ShapeDtypeStruct(s, jnp.float32) for s in outs]
     return pl.pallas_call(
         kernel,
@@ -483,7 +489,7 @@
         in_specs=specs or [VMEM] * len(args),
         out_specs=[out_spec or VMEM] * len(shapes) if len(shapes) > 1 else out_spec or VMEM,
         scratch_shapes=[pltpu.VMEM(s, jnp.float32) if isinstance(s, tuple) else s for s in scratch],
-        cost_estimate=pl.CostEstimate(flops=8, bytes_accessed=8, transcendentals=0),
+        cost_estimate=pl.CostEstimate(flops=8, bytes_accessed=cost, transcendentals=0),
         compiler_params=pltpu.CompilerParams(vmem_limit_bytes=grant * 1024 * 1024),
     )(*args)
 
@@ -507,10 +513,18 @@
     )
     even = lax.ppermute(start, "space", space_pairs(0))
     odd = lax.ppermute(start, "space", space_pairs(1))
+    staged = call(
+        stage_kernel,
+        [(2, 4, 32, 512)],
+        [start],
+        scratch=[pltpu.SemaphoreType.DMA],
+        specs=[ANY],
+        cost=4 * 10**6,
+    )
     packed = call(
         relax_kernel,
         [(32, 2, 2, 8, 128)],
-        [start, odd, even],
+        [staged, odd, even],
         scratch=[(2, 12, 48, 512), (2, 12, 48, 512), (2, 4, 32, 512)],
     )
     own = lax.all_to_all(packed, AXES, 0, 0, tiled=True, axis_index_groups=PLANE_GROUPS)

time: 167 us -> 166 us (level)
    pallas_call x9 -> x10, Pallas kernels: 16.7 us -> 16.8 us  [call(): pl.pallas_call(kernel, out_shape=shapes if len(shapes) > 1 else shapes[0]...]
where the time goes in v4:
time: 166 us
  starting transfers between devices  64 us (39%)
  waiting for transfers between devices  45.3 us (27%)
  blocking collectives  35.9 us (22%)
  Pallas kernels  17.3 us (10%)
    all_to_all x1, blocking collectives, local(): lax.all_to_all(packed, AXES, 0, 0, tiled=True, axis_index_groups=PLANE_GR...  18.7 us
    all_to_all x1, blocking collectives, local(): lax.all_to_all(got, AXES, 0, 0, tiled=True, axis_index_groups=PLANE_GROUPS)  17.2 us
    pallas_call x10, Pallas kernels, call(): pl.pallas_call(kernel, out_shape=shapes if len(shapes) > 1 else shapes[0]...  16.8 us
    ppermute x1, starting transfers between devices, local(): odd = lax.ppermute(start, 'space', space_pairs(1))  14.4 us
    ppermute x1, starting transfers between devices, local(): near = lax.ppermute(near, 'tm', ACROSS)  13.3 us
    ppermute x1, waiting for transfers between devices, local(): near = lax.ppermute(near, 'tm', ACROSS)  12.2 us
    ppermute x4, starting transfers between devices, lanes(): return [lax.ppermute(right, AXES, RIGHT), lax.ppermute(left, AXES, LEFT)]  12.2 us
    ppermute x2, waiting for transfers between devices, exchange_rows(): got_odd = lax.ppermute(odd, axis, pairs(1))  12 us
  transfers between devices with their start and end apart: 13, of which 7 were waited for; matrix products, arithmetic and copies ran while one was open for 0% of the time, Pallas kernels for 2%

profile of v4, /device:TPU:1, one launch (start us, length us, event | category | flops | bytes accessed | tf_op | source)
XLA Modules:
  0.0 165.8 jit_solution(8892383872129929728)
XLA Ops:
  0.6 1.8 %shard_map.59.start = f32[2,4,32,512]{3,2,1,0:T(8,128)} custom-call(s32[3,8]{1,0:T(4,128)} %bitcast.2, f32[1,4,32,512]{3,2,1,0:T(8,128)} %p_in.1, f32[1,4,32,512]{3,2,1,0:T(8,128)} %u_in.1, f32[4,32,512]{2,1,0:T(8,128)} %u_start.1), custom_call_target="tpu_custom_call" | custom-call | flops 8 | bytes 8 | tf_op jit(solution)/shard_map/pallas_call | solution.py:486
  2.5 3.9 %collective-permute-start.3 = (f32[2,4,32,512]{3,2,1,0:T(8,128)}, f32[2,4,32,512]{3,2,1,0:T(8,128)S(1)}, u32[]{:S(2)}, u32[]{:S(2)}) collective-permute-start(f32[2,4,32,512]{3,2,1,0:T(8,128)} %shard_map.59.start), channel_id=1, source_target_pairs={{0,1},{1,0},{2,3},{3,2},{4,5},{5,4},{6,7},{7,6},{8,9},{9,8},{10,11... | collective-permute-start | bytes 1572872 | tf_op jit(solution)/shard_map/ppermute | solution.py:514
  6.4 14.4 %collective-permute-start.2 = (f32[2,4,32,512]{3,2,1,0:T(8,128)}, f32[2,4,32,512]{3,2,1,0:T(8,128)S(1)}, u32[]{:S(2)}, u32[]{:S(2)}) collective-permute-start(f32[2,4,32,512]{3,2,1,0:T(8,128)} %shard_map.59.start), channel_id=1, source_target_pairs={{1,2},{2,1},{3,4},{4,3},{5,6},{6,5},{7,8},{8,7},{9,10},{10,9},{11,... | collective-permute-start | bytes 1572872 | tf_op jit(solution)/shard_map/ppermute | solution.py:515
  20.8 0.0 copy-start
  20.9 1.0 copy-done
  22.0 0.0 collective-permute-done.3.even
  22.0 9.1 %collective-permute-done.2.odd = f32[2,4,32,512]{3,2,1,0:T(8,128)S(1)} collective-permute-done((f32[2,4,32,512]{3,2,1,0:T(8,128)}, f32[2,4,32,512]{3,2,1,0:T(8,128)S(1)}, u32[]{:S(2)}, u32[]{:S(2)}) %collective-permute-start.2) | collective-permute-done | bytes 524320 | tf_op jit(solution)/shard_map/ppermute | solution.py:515
  31.0 5.9 %shard_map.61 = f32[32,2,2,8,128]{4,3,2,1,0:T(8,128)S(1)} custom-call(f32[2,4,32,512]{3,2,1,0:T(8,128)S(1)} %shard_map.60.start, f32[2,4,32,512]{3,2,1,0:T(8,128)S(1)} %collective-permute-done.2.odd, f32[2,4,32,512]{3,2,1,0:T(8,128)S(1)} %collective-permute-done.3.even), custom_call_target="tpu_custom_call" | custom-call | flops 8 | bytes 8 | tf_op jit(solution)/shard_map/pallas_call | solution.py:486
  37.0 18.7 %all_to_all.10.own.refs_0_ = f32[32,2,2,8,128]{4,3,2,1,0:T(8,128)S(1)} all-to-all(f32[32,2,2,8,128]{4,3,2,1,0:T(8,128)S(1)} %shard_map.61), channel_id=1, replica_groups={{0,1,2,3,32,33,34,35,128,129,130,131,160,161,162,163,256,257,258,259,28..., dimensions={0} | all-to-all | bytes 1048576 | tf_op jit(solution)/shard_map/all_to_all | solution.py:530
  55.7 0.5 shard_map.62
  56.2 13.3 %collective-permute-start.4 = (f32[8,2,2,8,128]{4,3,2,1,0:T(8,128)S(1)}, f32[8,2,2,8,128]{4,3,2,1,0:T(8,128)S(1)}, u32[]{:S(2)}, u32[]{:S(2)}) collective-permute-start(f32[8,2,2,8,128]{4,3,2,1,0:T(8,128)S(1)} %get-tuple-element.63), channel_id=1, source_target_pairs={{0,64},{32,96},{64,0},{96,32},{128,192},{160,224},{192,128},{224,1... | collective-permute-start | bytes 393224 | tf_op jit(solution)/shard_map/ppermute | solution.py:542
  69.5 1.9 %collective-permute-start.6 = (f32[4,2,2,8,128]{4,3,2,1,0:T(8,128)S(1)}, f32[4,2,2,8,128]{4,3,2,1,0:T(8,128)S(1)}, u32[]{:S(2)}, u32[]{:S(2)}) collective-permute-start(f32[4,2,2,8,128]{4,3,2,1,0:T(8,128)S(1)} %get-tuple-element.68), channel_id=1, source_target_pairs={{0,64},{32,96},{64,0},{96,32},{128,192},{160,224},{192,128},{224,1... | collective-permute-start | bytes 196616 | tf_op jit(solution)/shard_map/ppermute | solution.py:543
  71.4 12.2 %collective-permute-done.4 = f32[8,2,2,8,128]{4,3,2,1,0:T(8,128)S(1)} collective-permute-done((f32[8,2,2,8,128]{4,3,2,1,0:T(8,128)S(1)}, f32[8,2,2,8,128]{4,3,2,1,0:T(8,128)S(1)}, u32[]{:S(2)}, u32[]{:S(2)}) %collective-permute-start.4) | collective-permute-done | bytes 131104 | tf_op jit(solution)/shard_map/ppermute | solution.py:542
  83.6 6.0 %collective-permute-start.5 = (f32[16,2,2,8,128]{4,3,2,1,0:T(8,128)S(1)}, f32[16,2,2,8,128]{4,3,2,1,0:T(8,128)S(1)}, u32[]{:S(2)}, u32[]{:S(2)}) collective-permute-start(f32[16,2,2,8,128]{4,3,2,1,0:T(8,128)S(1)} %get-tuple-element.64), channel_id=1, source_target_pairs={{0,64},{32,96},{64,0},{96,32},{128,192},{160,224},{192,128},{224,1... | collective-permute-start | bytes 786440 | tf_op jit(solution)/shard_map/ppermute | solution.py:567
  89.7 0.0 collective-permute-done.6
  89.7 0.4 shard_map.63
  90.2 3.1 %collective-permute-start.7 = (f32[24,2,8,128]{3,2,1,0:T(8,128)S(1)}, f32[24,2,8,128]{3,2,1,0:T(8,128)S(1)}, u32[]{:S(2)}, u32[]{:S(2)}) collective-permute-start(f32[24,2,8,128]{3,2,1,0:T(8,128)S(1)} %get-tuple-element.69), channel_id=1, source_target_pairs={{0,32},{32,1},{1,33},{33,2},{2,34},{34,3},{3,35},{35,131},{131,163... | collective-permute-start | bytes 589832 | tf_op jit(solution)/shard_map/ppermute | solution.py:549
  93.3 3.3 %collective-permute-start.8 = (f32[24,2,8,128]{3,2,1,0:T(8,128)S(1)}, f32[24,2,8,128]{3,2,1,0:T(8,128)S(1)}, u32[]{:S(2)}, u32[]{:S(2)}) collective-permute-start(f32[24,2,8,128]{3,2,1,0:T(8,128)S(1)} %get-tuple-element.70), channel_id=1, source_target_pairs={{32,0},{1,32},{33,1},{2,33},{34,2},{3,34},{35,3},{131,35},{163,131... | collective-permute-start | bytes 589832 | tf_op jit(solution)/shard_map/ppermute | solution.py:549
  96.6 0.0 collective-permute-done.7
  96.6 3.9 %collective-permute-done.8 = f32[24,2,8,128]{3,2,1,0:T(8,128)S(1)} collective-permute-done((f32[24,2,8,128]{3,2,1,0:T(8,128)S(1)}, f32[24,2,8,128]{3,2,1,0:T(8,128)S(1)}, u32[]{:S(2)}, u32[]{:S(2)}) %collective-permute-start.8) | collective-permute-done | bytes 196640 | tf_op jit(solution)/shard_map/ppermute | solution.py:549
  100.6 19.2 %while.12 = (s32[]{:T(128)}, f32[16,2,2,8,128]{4,3,2,1,0:T(8,128)}, f32[2,8,8,128]{3,2,1,0:T(8,128)S(1)}, s32[]{:T(128)}, f32[32,2,2,8,128]{4,3,2,1,0:T(8,128)S(...) while((s32[]{:T(128)}, f32[16,2,2,8,128]{4,3,2,1,0:T(8,128)}, ...), condition=%wide.region_1.0_spmd, body=%wide.region_0.0_spmd.sunk | while | flops 18 | bytes 1376445 | solution.py:569
  101.3 0.2 body.2
  101.5 4.8 %collective-permute-start = (f32[21,2,8,128]{3,2,1,0:T(8,128)S(1)}, f32[21,2,8,128]{3,2,1,0:T(8,128)S(1)}, u32[]{:S(2)}, u32[]{:S(2)}) collective-permute-start(f32[21,2,8,128]{3,2,1,0:T(8,128)S(1)} %get-tuple-element.145), channel_id=1, source_target_pairs={{4,8},{8,4},{36,40},{40,36},{5,9},{9,5},{37,41},{41,37},{6,10},{10... | collective-permute-start | bytes 516104 | tf_op jit(solution)/shard_map/while/body/ppermute | solution.py:499
  106.3 1.9 %collective-permute-start.1 = (f32[21,2,8,128]{3,2,1,0:T(8,128)S(1)}, f32[21,2,8,128]{3,2,1,0:T(8,128)S(1)}, u32[]{:S(2)}, u32[]{:S(2)}) collective-permute-start(f32[21,2,8,128]{3,2,1,0:T(8,128)S(1)} %get-tuple-element.146), channel_id=1, source_target_pairs={{0,4},{4,0},{32,36},{36,32},{1,5},{5,1},{33,37},{37,33},{2,6},{6,2... | collective-permute-start | bytes 516104 | tf_op jit(solution)/shard_map/while/body/ppermute | solution.py:500
  108.2 8.1 %collective-permute-done.refs_4_ = f32[21,2,8,128]{3,2,1,0:T(8,128)S(1)} collective-permute-done((f32[21,2,8,128]{3,2,1,0:T(8,128)S(1)}, f32[21,2,8,128]{3,2,1,0:T(8,128)S(1)}, u32[]{:S(2)}, u32[]{:S(2)}) %collective-permute-start) | collective-permute-done | bytes 172064 | tf_op jit(solution)/shard_map/while/body/ppermute | solution.py:499
  116.3 0.0 collective-permute-done.1.refs_5_
  116.3 2.7 %body.3 = (f32[16,2,2,8,128]{4,3,2,1,0:T(8,128)}, f32[2,8,8,128]{3,2,1,0:T(8,128)S(1)}) custom-call(f32[32,2,2,8,128]{4,3,2,1,0:T(8,128)S(1)} %get-tuple-element.171.refs_1_.refs_0_, f32[12,2,2,8,128]{4,3,2,1,0:T(8,128)S(1)} %get-tuple-element.172.refs_2_.refs_1_, f32[24,2,8,128]{3,2,1,0:T(8,128)S(1)} %get-tuple-element.173.refs_3_.refs_2_, ...), custom_call_target="tpu_custom_call" | custom-call | flops 8 | bytes 8 | tf_op jit(solution)/shard_map/while/body/pallas_call | solution.py:486
  119.8 0.0 collective-permute-done.5.refs_1_
  119.8 0.5 shard_map.64
  120.3 1.9 %collective-permute-start.9 = (f32[32,2,8,128]{3,2,1,0:T(8,128)S(1)}, f32[32,2,8,128]{3,2,1,0:T(8,128)S(1)}, u32[]{:S(2)}, u32[]{:S(2)}) collective-permute-start(f32[32,2,8,128]{3,2,1,0:T(8,128)S(1)} %get-tuple-element.72), channel_id=1, source_target_pairs={{0,32},{32,1},{1,33},{33,2},{2,34},{34,3},{3,35},{35,131},{131,163... | collective-permute-start | bytes 786440 | tf_op jit(solution)/shard_map/ppermute | solution.py:549
  122.2 0.0 copy-start.2
  122.3 3.8 %collective-permute-start.10 = (f32[32,2,8,128]{3,2,1,0:T(8,128)S(1)}, f32[32,2,8,128]{3,2,1,0:T(8,128)S(1)}, u32[]{:S(2)}, u32[]{:S(2)}) collective-permute-start(f32[32,2,8,128]{3,2,1,0:T(8,128)S(1)} %get-tuple-element.73), channel_id=1, source_target_pairs={{32,0},{1,32},{33,1},{2,33},{34,2},{3,34},{35,3},{131,35},{163,131... | collective-permute-start | bytes 786440 | tf_op jit(solution)/shard_map/ppermute | solution.py:549
  126.1 0.0 collective-permute-done.9.refs_3_
  126.1 4.3 %collective-permute-done.10.refs_4_ = f32[32,2,8,128]{3,2,1,0:T(8,128)S(1)} collective-permute-done((f32[32,2,8,128]{3,2,1,0:T(8,128)S(1)}, f32[32,2,8,128]{3,2,1,0:T(8,128)S(1)}, u32[]{:S(2)}, u32[]{:S(2)}) %collective-permute-start.10) | collective-permute-done | bytes 262176 | tf_op jit(solution)/shard_map/ppermute | solution.py:549
  130.4 0.3 shard_map.65
  130.7 3.7 %collective-permute-start.11 = (f32[36,2,8,128]{3,2,1,0:T(8,128)S(1)}, f32[36,2,8,128]{3,2,1,0:T(8,128)S(1)}, u32[]{:S(2)}, u32[]{:S(2)}) collective-permute-start(f32[36,2,8,128]{3,2,1,0:T(8,128)S(1)} %get-tuple-element.74), channel_id=1, source_target_pairs={{4,8},{8,4},{36,40},{40,36},{5,9},{9,5},{37,41},{41,37},{6,10},{10... | collective-permute-start | bytes 884744 | tf_op jit(solution)/shard_map/ppermute | solution.py:499
  134.4 1.9 %collective-permute-start.12 = (f32[36,2,8,128]{3,2,1,0:T(8,128)S(1)}, f32[36,2,8,128]{3,2,1,0:T(8,128)S(1)}, u32[]{:S(2)}, u32[]{:S(2)}) collective-permute-start(f32[36,2,8,128]{3,2,1,0:T(8,128)S(1)} %get-tuple-element.75), channel_id=1, source_target_pairs={{0,4},{4,0},{32,36},{36,32},{1,5},{5,1},{33,37},{37,33},{2,6},{6,2... | collective-permute-start | bytes 884744 | tf_op jit(solution)/shard_map/ppermute | solution.py:500
  136.3 3.8 %collective-permute-done.11.refs_5_ = f32[36,2,8,128]{3,2,1,0:T(8,128)S(1)} collective-permute-done((f32[36,2,8,128]{3,2,1,0:T(8,128)S(1)}, f32[36,2,8,128]{3,2,1,0:T(8,128)S(1)}, u32[]{:S(2)}, u32[]{:S(2)}) %collective-permute-start.11) | collective-permute-done | bytes 294944 | tf_op jit(solution)/shard_map/ppermute | solution.py:499
  140.1 3.8 %collective-permute-done.12.refs_6_ = f32[36,2,8,128]{3,2,1,0:T(8,128)S(1)} collective-permute-done((f32[36,2,8,128]{3,2,1,0:T(8,128)S(1)}, f32[36,2,8,128]{3,2,1,0:T(8,128)S(1)}, u32[]{:S(2)}, u32[]{:S(2)}) %collective-permute-start.12) | collective-permute-done | bytes 294944 | tf_op jit(solution)/shard_map/ppermute | solution.py:500
  143.9 0.0 copy-done.2
  143.9 3.2 %shard_map.66 = f32[32,2,2,8,128]{4,3,2,1,0:T(8,128)S(1)} custom-call(f32[32,2,2,8,128]{4,3,2,1,0:T(8,128)S(1)} %get-tuple-element.198, f32[16,2,2,8,128]{4,3,2,1,0:T(8,128)S(1)} %collective-permute-done.5.refs_1_, f32[2,8,8,128]{3,2,1,0:T(8,128)S(1)} %get-tuple-element.71.refs_2_, f32[32,2,8,128]{3,2,1,0:T(8,128)S(1)} %collective-permute-done.9.refs_3_, ...), custom_call_target="tpu_custom_call" | custom-call | flops 8 | bytes 8 | tf_op jit(solution)/shard_map/pallas_call | solution.py:486
  147.1 0.0 copy-start.1
  147.1 17.2 %all_to_all.11.got = f32[32,2,2,8,128]{4,3,2,1,0:T(8,128)S(1)} all-to-all(f32[32,2,2,8,128]{4,3,2,1,0:T(8,128)S(1)} %shard_map.66), channel_id=1, replica_groups={{0,1,2,3,32,33,34,35,128,129,130,131,160,161,162,163,256,257,258,259,28..., dimensions={0} | all-to-all | bytes 1048576 | tf_op jit(solution)/shard_map/all_to_all | solution.py:575
  164.3 0.0 copy-done.1
  164.3 1.5 shard_map.67
  (3 shorter events, 0.1 us)
Async XLA Ops:
  2.5 19.5 %collective-permute-start.3 = (f32[2,4,32,512]{3,2,1,0:T(8,128)}, f32[2,4,32,512]{3,2,1,0:T(8,128)S(1)}, u32[]{:S(2)}, u32[]{:S(2)}) collective-permute-start(f32[2,4,32,512]{3,2,1,0:T(8,128)} %shard_map.59.start), channel_id=1, source_target_pairs={{0,1},{1,0},{2,3},{3,2},{4,5},{5,4},{6,7},{7,6},{8,9},{9,8},{10,11... | collective-permute-start | bytes 1572872 | tf_op jit(solution)/shard_map/ppermute | solution.py:514
  6.4 24.6 %collective-permute-start.2 = (f32[2,4,32,512]{3,2,1,0:T(8,128)}, f32[2,4,32,512]{3,2,1,0:T(8,128)S(1)}, u32[]{:S(2)}, u32[]{:S(2)}) collective-permute-start(f32[2,4,32,512]{3,2,1,0:T(8,128)} %shard_map.59.start), channel_id=1, source_target_pairs={{1,2},{2,1},{3,4},{4,3},{5,6},{6,5},{7,8},{8,7},{9,10},{10,9},{11,... | collective-permute-start | bytes 1572872 | tf_op jit(solution)/shard_map/ppermute | solution.py:515
  20.8 1.1 copy-start
  56.2 27.4 %collective-permute-start.4 = (f32[8,2,2,8,128]{4,3,2,1,0:T(8,128)S(1)}, f32[8,2,2,8,128]{4,3,2,1,0:T(8,128)S(1)}, u32[]{:S(2)}, u32[]{:S(2)}) collective-permute-start(f32[8,2,2,8,128]{4,3,2,1,0:T(8,128)S(1)} %get-tuple-element.63), channel_id=1, source_target_pairs={{0,64},{32,96},{64,0},{96,32},{128,192},{160,224},{192,128},{224,1... | collective-permute-start | bytes 393224 | tf_op jit(solution)/shard_map/ppermute | solution.py:542
  69.5 20.2 %collective-permute-start.6 = (f32[4,2,2,8,128]{4,3,2,1,0:T(8,128)S(1)}, f32[4,2,2,8,128]{4,3,2,1,0:T(8,128)S(1)}, u32[]{:S(2)}, u32[]{:S(2)}) collective-permute-start(f32[4,2,2,8,128]{4,3,2,1,0:T(8,128)S(1)} %get-tuple-element.68), channel_id=1, source_target_pairs={{0,64},{32,96},{64,0},{96,32},{128,192},{160,224},{192,128},{224,1... | collective-permute-start | bytes 196616 | tf_op jit(solution)/shard_map/ppermute | solution.py:543
  83.6 36.2 %collective-permute-start.5 = (f32[16,2,2,8,128]{4,3,2,1,0:T(8,128)S(1)}, f32[16,2,2,8,128]{4,3,2,1,0:T(8,128)S(1)}, u32[]{:S(2)}, u32[]{:S(2)}) collective-permute-start(f32[16,2,2,8,128]{4,3,2,1,0:T(8,128)S(1)} %get-tuple-element.64), channel_id=1, source_target_pairs={{0,64},{32,96},{64,0},{96,32},{128,192},{160,224},{192,128},{224,1... | collective-permute-start | bytes 786440 | tf_op jit(solution)/shard_map/ppermute | solution.py:567
  90.2 6.5 %collective-permute-start.7 = (f32[24,2,8,128]{3,2,1,0:T(8,128)S(1)}, f32[24,2,8,128]{3,2,1,0:T(8,128)S(1)}, u32[]{:S(2)}, u32[]{:S(2)}) collective-permute-start(f32[24,2,8,128]{3,2,1,0:T(8,128)S(1)} %get-tuple-element.69), channel_id=1, source_target_pairs={{0,32},{32,1},{1,33},{33,2},{2,34},{34,3},{3,35},{35,131},{131,163... | collective-permute-start | bytes 589832 | tf_op jit(solution)/shard_map/ppermute | solution.py:549
  93.3 7.3 %collective-permute-start.8 = (f32[24,2,8,128]{3,2,1,0:T(8,128)S(1)}, f32[24,2,8,128]{3,2,1,0:T(8,128)S(1)}, u32[]{:S(2)}, u32[]{:S(2)}) collective-permute-start(f32[24,2,8,128]{3,2,1,0:T(8,128)S(1)} %get-tuple-element.70), channel_id=1, source_target_pairs={{32,0},{1,32},{33,1},{2,33},{34,2},{3,34},{35,3},{131,35},{163,131... | collective-permute-start | bytes 589832 | tf_op jit(solution)/shard_map/ppermute | solution.py:549
  101.5 14.8 %collective-permute-start = (f32[21,2,8,128]{3,2,1,0:T(8,128)S(1)}, f32[21,2,8,128]{3,2,1,0:T(8,128)S(1)}, u32[]{:S(2)}, u32[]{:S(2)}) collective-permute-start(f32[21,2,8,128]{3,2,1,0:T(8,128)S(1)} %get-tuple-element.145), channel_id=1, source_target_pairs={{4,8},{8,4},{36,40},{40,36},{5,9},{9,5},{37,41},{41,37},{6,10},{10... | collective-permute-start | bytes 516104 | tf_op jit(solution)/shard_map/while/body/ppermute | solution.py:499
  106.3 10.1 %collective-permute-start.1 = (f32[21,2,8,128]{3,2,1,0:T(8,128)S(1)}, f32[21,2,8,128]{3,2,1,0:T(8,128)S(1)}, u32[]{:S(2)}, u32[]{:S(2)}) collective-permute-start(f32[21,2,8,128]{3,2,1,0:T(8,128)S(1)} %get-tuple-element.146), channel_id=1, source_target_pairs={{0,4},{4,0},{32,36},{36,32},{1,5},{5,1},{33,37},{37,33},{2,6},{6,2... | collective-permute-start | bytes 516104 | tf_op jit(solution)/shard_map/while/body/ppermute | solution.py:500
  120.3 5.8 %collective-permute-start.9 = (f32[32,2,8,128]{3,2,1,0:T(8,128)S(1)}, f32[32,2,8,128]{3,2,1,0:T(8,128)S(1)}, u32[]{:S(2)}, u32[]{:S(2)}) collective-permute-start(f32[32,2,8,128]{3,2,1,0:T(8,128)S(1)} %get-tuple-element.72), channel_id=1, source_target_pairs={{0,32},{32,1},{1,33},{33,2},{2,34},{34,3},{3,35},{35,131},{131,163... | collective-permute-start | bytes 786440 | tf_op jit(solution)/shard_map/ppermute | solution.py:549
  122.2 21.7 %copy-start.2 = (f32[16,2,2,8,128]{4,3,2,1,0:T(8,128)S(1)}, f32[16,2,2,8,128]{4,3,2,1,0:T(8,128)}, u32[]{:S(2)}) copy-start(f32[16,2,2,8,128]{4,3,2,1,0:T(8,128)} %get-tuple-element.76.refs_7_) | copy-start | bytes 786436
  122.3 8.1 %collective-permute-start.10 = (f32[32,2,8,128]{3,2,1,0:T(8,128)S(1)}, f32[32,2,8,128]{3,2,1,0:T(8,128)S(1)}, u32[]{:S(2)}, u32[]{:S(2)}) collective-permute-start(f32[32,2,8,128]{3,2,1,0:T(8,128)S(1)} %get-tuple-element.73), channel_id=1, source_target_pairs={{32,0},{1,32},{33,1},{2,33},{34,2},{3,34},{35,3},{131,35},{163,131... | collective-permute-start | bytes 786440 | tf_op jit(solution)/shard_map/ppermute | solution.py:549
  130.7 9.4 %collective-permute-start.11 = (f32[36,2,8,128]{3,2,1,0:T(8,128)S(1)}, f32[36,2,8,128]{3,2,1,0:T(8,128)S(1)}, u32[]{:S(2)}, u32[]{:S(2)}) collective-permute-start(f32[36,2,8,128]{3,2,1,0:T(8,128)S(1)} %get-tuple-element.74), channel_id=1, source_target_pairs={{4,8},{8,4},{36,40},{40,36},{5,9},{9,5},{37,41},{41,37},{6,10},{10... | collective-permute-start | bytes 884744 | tf_op jit(solution)/shard_map/ppermute | solution.py:499
  134.4 9.5 %collective-permute-start.12 = (f32[36,2,8,128]{3,2,1,0:T(8,128)S(1)}, f32[36,2,8,128]{3,2,1,0:T(8,128)S(1)}, u32[]{:S(2)}, u32[]{:S(2)}) collective-permute-start(f32[36,2,8,128]{3,2,1,0:T(8,128)S(1)} %get-tuple-element.75), channel_id=1, source_target_pairs={{0,4},{4,0},{32,36},{36,32},{1,5},{5,1},{33,37},{37,33},{2,6},{6,2... | collective-permute-start | bytes 884744 | tf_op jit(solution)/shard_map/ppermute | solution.py:500
  147.1 17.2 %copy-start.1 = (f32[2,4,32,512]{3,2,1,0:T(8,128)S(1)}, f32[2,4,32,512]{3,2,1,0:T(8,128)}, u32[]{:S(2)}) copy-start(f32[2,4,32,512]{3,2,1,0:T(8,128)} %shard_map.59.start) | copy-start | bytes 1572868

commit v5 on v4

--- a/solution.py
+++ b/solution.py
@@ -38,9 +38,16 @@
 RING = [ring_of(n % 4, n // 8, (n // 4) % 2) for n in range(32)]
 MEMBER = [RING.index(i) for i in range(32)]
 PLANE_GROUPS = [[on_ring(i, plane) for i in RING] for plane in PLANES]
-RIGHT = [(on_ring(i, plane), on_ring(i + 1, plane)) for plane in PLANES for i in range(32)]
-LEFT = [(b, a) for a, b in RIGHT]
 ACROSS = [(i, i ^ 2) for i in range(16)]
+
+
+def lane_pairs(parity):
+    pairs = []
+    for plane in PLANES:
+        for i in range(parity, 32, 2):
+            a, b = on_ring(i, plane), on_ring(i + 1, plane)
+            pairs += [(a, b), (b, a)]
+    return pairs
 
 
 def row_pairs(parity):
@@ -291,10 +298,11 @@
 
 
 def lanes_kernel(phase, *refs):
-    own, other, first, right, left = split(phase, refs, 2)
+    own, other, first, odd, even = split(phase, refs, 2)
     tm, _ = block_index()
     get = piece_of(phase, own, other, first, (tm // 2) % 2)
     part = lane32() // 8
+    is_odd = tm % 2 == 1
     for slot in range(phase.steps):
         for f in range(2):
             for quad in range(4):
@@ -310,11 +318,11 @@
                     else:
                         r_edge = jnp.where(part == q, r_part, r_edge)
                         l_edge = jnp.where(part == (q + 3) % 4, l_part, l_edge)
-                right[4 * slot + quad, f] = r_edge
-                left[4 * slot + quad, f] = l_edge
-
-
-def row_of(phase, get, from_left, from_right):
+                odd[4 * slot + quad, f] = jnp.where(is_odd, r_edge, l_edge)
+                even[4 * slot + quad, f] = jnp.where(is_odd, l_edge, r_edge)
+
+
+def row_of(phase, get, odd, even, is_odd):
     part = lane32() // 8
 
     def row(slot, f, r):
@@ -322,7 +330,7 @@
         if slot == phase.steps:
             return value
         quad, q = 4 * slot + r // 4, r % 4
-        halo = jnp.where(part == q, from_left[quad, f], from_right[quad, f])
+        halo = jnp.where((part == q) ^ is_odd, odd[quad, f], even[quad, f])
         if q != 0:
             halo = pltpu.roll(halo, 128 - 8 * q, 1)
         return jnp.where((part == 0) | (part == 3), halo, value)
@@ -331,10 +339,10 @@
 
 
 def edges_kernel(phase, *refs):
-    own, other, first, from_left, from_right, odd, even = split(phase, refs, 4)
+    own, other, first, lanes_odd, lanes_even, odd, even = split(phase, refs, 4)
     tm, space = block_index()
     get = piece_of(phase, own, other, first, (tm // 2) % 2)
-    row = row_of(phase, get, from_left, from_right)
+    row = row_of(phase, get, lanes_odd, lanes_even, tm % 2 == 1)
     z_odd = (space // 4) % 2 == 1
     for slot in range(phase.steps):
         n = phase.halo[slot]
@@ -347,17 +355,17 @@
 
 def chain_kernel(phase, *refs):
     if phase.index == 0:
-        own, other, first, from_left, from_right, odd, even, out, last, state, taus = split(
+        own, other, first, lanes_odd, lanes_even, odd, even, out, last, state, taus = split(
             phase, refs, 8
         )
     else:
-        own, other, first, from_left, from_right, odd, even, before, out, state, taus = split(
+        own, other, first, lanes_odd, lanes_even, odd, even, before, out, state, taus = split(
             phase, refs, 8
         )
     tm, space = block_index()
     z_hi = (tm // 2) % 2
     get = piece_of(phase, own, other, first, z_hi)
-    row = row_of(phase, get, from_left, from_right)
+    row = row_of(phase, get, lanes_odd, lanes_even, tm % 2 == 1)
     z_odd = (space // 4) % 2 == 1
     lane = lane32()
     for slot in range(phase.steps + 1):
@@ -494,7 +502,7 @@
     )(*args)
 
 
-def exchange_rows(payload, axis, pairs):
+def exchange(payload, axis, pairs):
     odd, even = payload
     got_odd = lax.ppermute(odd, axis, pairs(1))
     got_even = lax.ppermute(even, axis, pairs(0))
@@ -543,10 +551,10 @@
     middle = lax.ppermute(middle, "tm", ACROSS)
 
     def lanes(phase, known):
-        right, left = call(
+        edges = call(
             lambda *refs: lanes_kernel(phase, *refs), [(4 * phase.steps, 2, 8, 128)] * 2, known
         )
-        return [lax.ppermute(right, AXES, RIGHT), lax.ppermute(left, AXES, LEFT)]
+        return exchange(edges, AXES, lane_pairs)
 
     def advance(phase, known, before=(), after=()):
         edges = call(
@@ -558,7 +566,7 @@
         return call(
             lambda *refs: chain_kernel(phase, *refs),
             [(32, 2, 2, 8, 128)] if phase.index else [(16, 2, 2, 8, 128), (2, 8, 8, 128)],
-            [*known, *exchange_rows(edges, AXES, row_pairs), *before],
+            [*known, *exchange(edges, AXES, row_pairs), *before],
             scratch=[(2, 2, 32, 8, 128), (phase.steps, 2, 32, 8, 128)],
         )
 

time: 166 us -> 164 us (0.988)
  waiting for transfers between devices: 45.3 us -> 37.8 us
  starting transfers between devices: 64 us -> 67.4 us
    ppermute x8, waiting for transfers between devices: 24 us -> 16.5 us  [the longest x4 13.5 us: exchange(): got_odd = lax.ppermute(odd, axis, pairs(1))]
    ppermute x8, starting transfers between devices: 24.4 us -> 27.8 us  [the longest x4 17.9 us: exchange(): got_odd = lax.ppermute(odd, axis, pairs(1))]
  transfers between devices with their start and end apart: 13 -> 13, of which waited for: 7 -> 8; matrix products, arithmetic and copies ran while one was open for 0% -> 0% of each run, Pallas kernels for 2% -> 2%
where the time goes in v5:
time: 164 us; the launch traced here: 163 us
  starting transfers between devices  67.4 us (41%)
  waiting for transfers between devices  37.8 us (23%)
  blocking collectives  37.4 us (23%)
  Pallas kernels  17.3 us (11%)
    all_to_all x1, blocking collectives, local(): lax.all_to_all(got, AXES, 0, 0, tiled=True, axis_index_groups=PLANE_GROUPS)  18.7 us
    all_to_all x1, blocking collectives, local(): lax.all_to_all(packed, AXES, 0, 0, tiled=True, axis_index_groups=PLANE_GR...  18.7 us
    ppermute x4, starting transfers between devices, exchange(): got_odd = lax.ppermute(odd, axis, pairs(1))  17.9 us
    pallas_call x10, Pallas kernels, call(): pl.pallas_call(kernel, out_shape=shapes if len(shapes) > 1 else shapes[0]...  16.8 us
    ppermute x1, starting transfers between devices, local(): odd = lax.ppermute(start, 'space', space_pairs(1))  14.4 us
    ppermute x4, waiting for transfers between devices, exchange(): got_odd = lax.ppermute(odd, axis, pairs(1))  13.5 us
    ppermute x1, starting transfers between devices, local(): near = lax.ppermute(near, 'tm', ACROSS)  13.3 us
    ppermute x1, waiting for transfers between devices, local(): near = lax.ppermute(near, 'tm', ACROSS)  12.2 us
  transfers between devices with their start and end apart: 13, of which 8 were waited for; matrix products, arithmetic and copies ran while one was open for 0% of the time, Pallas kernels for 2%

profile of v5, /device:TPU:1, one launch (start us, length us, event | category | flops | bytes accessed | tf_op | source)
XLA Modules:
  0.0 163.3 jit_solution(17806522438541751294)
XLA Ops:
  0.6 1.8 %shard_map.59.start = f32[2,4,32,512]{3,2,1,0:T(8,128)} custom-call(s32[3,8]{1,0:T(4,128)} %bitcast.2, f32[1,4,32,512]{3,2,1,0:T(8,128)} %p_in.1, f32[1,4,32,512]{3,2,1,0:T(8,128)} %u_in.1, f32[4,32,512]{2,1,0:T(8,128)} %u_start.1), custom_call_target="tpu_custom_call" | custom-call | flops 8 | bytes 8 | tf_op jit(solution)/shard_map/pallas_call | solution.py:494
  2.5 3.9 %collective-permute-start.3 = (f32[2,4,32,512]{3,2,1,0:T(8,128)}, f32[2,4,32,512]{3,2,1,0:T(8,128)S(1)}, u32[]{:S(2)}, u32[]{:S(2)}) collective-permute-start(f32[2,4,32,512]{3,2,1,0:T(8,128)} %shard_map.59.start), channel_id=1, source_target_pairs={{0,1},{1,0},{2,3},{3,2},{4,5},{5,4},{6,7},{7,6},{8,9},{9,8},{10,11... | collective-permute-start | bytes 1572872 | tf_op jit(solution)/shard_map/ppermute | solution.py:522
  6.4 14.4 %collective-permute-start.2 = (f32[2,4,32,512]{3,2,1,0:T(8,128)}, f32[2,4,32,512]{3,2,1,0:T(8,128)S(1)}, u32[]{:S(2)}, u32[]{:S(2)}) collective-permute-start(f32[2,4,32,512]{3,2,1,0:T(8,128)} %shard_map.59.start), channel_id=1, source_target_pairs={{1,2},{2,1},{3,4},{4,3},{5,6},{6,5},{7,8},{8,7},{9,10},{10,9},{11,... | collective-permute-start | bytes 1572872 | tf_op jit(solution)/shard_map/ppermute | solution.py:523
  20.8 0.0 copy-start
  20.9 1.0 copy-done
  22.0 0.0 collective-permute-done.3.even
  22.0 9.1 %collective-permute-done.2.odd = f32[2,4,32,512]{3,2,1,0:T(8,128)S(1)} collective-permute-done((f32[2,4,32,512]{3,2,1,0:T(8,128)}, f32[2,4,32,512]{3,2,1,0:T(8,128)S(1)}, u32[]{:S(2)}, u32[]{:S(2)}) %collective-permute-start.2) | collective-permute-done | bytes 524320 | tf_op jit(solution)/shard_map/ppermute | solution.py:523
  31.0 5.9 %shard_map.61 = f32[32,2,2,8,128]{4,3,2,1,0:T(8,128)S(1)} custom-call(f32[2,4,32,512]{3,2,1,0:T(8,128)S(1)} %shard_map.60.start, f32[2,4,32,512]{3,2,1,0:T(8,128)S(1)} %collective-permute-done.2.odd, f32[2,4,32,512]{3,2,1,0:T(8,128)S(1)} %collective-permute-done.3.even), custom_call_target="tpu_custom_call" | custom-call | flops 8 | bytes 8 | tf_op jit(solution)/shard_map/pallas_call | solution.py:494
  37.0 18.7 %all_to_all.10.own.refs_0_ = f32[32,2,2,8,128]{4,3,2,1,0:T(8,128)S(1)} all-to-all(f32[32,2,2,8,128]{4,3,2,1,0:T(8,128)S(1)} %shard_map.61), channel_id=1, replica_groups={{0,1,2,3,32,33,34,35,128,129,130,131,160,161,162,163,256,257,258,259,28..., dimensions={0} | all-to-all | bytes 1048576 | tf_op jit(solution)/shard_map/all_to_all | solution.py:538
  55.7 0.5 shard_map.62
  56.2 13.3 %collective-permute-start.4 = (f32[8,2,2,8,128]{4,3,2,1,0:T(8,128)S(1)}, f32[8,2,2,8,128]{4,3,2,1,0:T(8,128)S(1)}, u32[]{:S(2)}, u32[]{:S(2)}) collective-permute-start(f32[8,2,2,8,128]{4,3,2,1,0:T(8,128)S(1)} %get-tuple-element.63), channel_id=1, source_target_pairs={{0,64},{32,96},{64,0},{96,32},{128,192},{160,224},{192,128},{224,1... | collective-permute-start | bytes 393224 | tf_op jit(solution)/shard_map/ppermute | solution.py:550
  69.5 1.9 %collective-permute-start.6 = (f32[4,2,2,8,128]{4,3,2,1,0:T(8,128)S(1)}, f32[4,2,2,8,128]{4,3,2,1,0:T(8,128)S(1)}, u32[]{:S(2)}, u32[]{:S(2)}) collective-permute-start(f32[4,2,2,8,128]{4,3,2,1,0:T(8,128)S(1)} %get-tuple-element.68), channel_id=1, source_target_pairs={{0,64},{32,96},{64,0},{96,32},{128,192},{160,224},{192,128},{224,1... | collective-permute-start | bytes 196616 | tf_op jit(solution)/shard_map/ppermute | solution.py:551
  71.4 12.2 %collective-permute-done.4 = f32[8,2,2,8,128]{4,3,2,1,0:T(8,128)S(1)} collective-permute-done((f32[8,2,2,8,128]{4,3,2,1,0:T(8,128)S(1)}, f32[8,2,2,8,128]{4,3,2,1,0:T(8,128)S(1)}, u32[]{:S(2)}, u32[]{:S(2)}) %collective-permute-start.4) | collective-permute-done | bytes 131104 | tf_op jit(solution)/shard_map/ppermute | solution.py:550
  83.6 6.0 %collective-permute-start.5 = (f32[16,2,2,8,128]{4,3,2,1,0:T(8,128)S(1)}, f32[16,2,2,8,128]{4,3,2,1,0:T(8,128)S(1)}, u32[]{:S(2)}, u32[]{:S(2)}) collective-permute-start(f32[16,2,2,8,128]{4,3,2,1,0:T(8,128)S(1)} %get-tuple-element.64), channel_id=1, source_target_pairs={{0,64},{32,96},{64,0},{96,32},{128,192},{160,224},{192,128},{224,1... | collective-permute-start | bytes 786440 | tf_op jit(solution)/shard_map/ppermute | solution.py:575
  89.7 0.0 collective-permute-done.6
  89.7 0.4 shard_map.63
  90.2 3.1 %collective-permute-start.7 = (f32[24,2,8,128]{3,2,1,0:T(8,128)S(1)}, f32[24,2,8,128]{3,2,1,0:T(8,128)S(1)}, u32[]{:S(2)}, u32[]{:S(2)}) collective-permute-start(f32[24,2,8,128]{3,2,1,0:T(8,128)S(1)} %get-tuple-element.69), channel_id=1, source_target_pairs={{32,1},{1,32},{33,2},{2,33},{34,3},{3,34},{35,131},{131,35},{163,1... | collective-permute-start | bytes 589832 | tf_op jit(solution)/shard_map/ppermute | solution.py:507
  93.3 3.3 %collective-permute-start.8 = (f32[24,2,8,128]{3,2,1,0:T(8,128)S(1)}, f32[24,2,8,128]{3,2,1,0:T(8,128)S(1)}, u32[]{:S(2)}, u32[]{:S(2)}) collective-permute-start(f32[24,2,8,128]{3,2,1,0:T(8,128)S(1)} %get-tuple-element.70), channel_id=1, source_target_pairs={{0,32},{32,0},{1,33},{33,1},{2,34},{34,2},{3,35},{35,3},{131,163},... | collective-permute-start | bytes 589832 | tf_op jit(solution)/shard_map/ppermute | solution.py:508
  96.6 0.5 collective-permute-done.7
  97.2 0.5 collective-permute-done.8
  97.7 20.3 %while.12 = (s32[]{:T(128)}, f32[16,2,2,8,128]{4,3,2,1,0:T(8,128)}, f32[2,8,8,128]{3,2,1,0:T(8,128)S(1)}, s32[]{:T(128)}, f32[32,2,2,8,128]{4,3,2,1,0:T(8,128)S(...) while((s32[]{:T(128)}, f32[16,2,2,8,128]{4,3,2,1,0:T(8,128)}, ...), condition=%wide.region_1.0_spmd, body=%wide.region_0.0_spmd.sunk | while | flops 18 | bytes 1376445 | solution.py:577
  98.3 0.2 body.2
  98.6 6.9 %collective-permute-start = (f32[21,2,8,128]{3,2,1,0:T(8,128)S(1)}, f32[21,2,8,128]{3,2,1,0:T(8,128)S(1)}, u32[]{:S(2)}, u32[]{:S(2)}) collective-permute-start(f32[21,2,8,128]{3,2,1,0:T(8,128)S(1)} %get-tuple-element.145), channel_id=1, source_target_pairs={{4,8},{8,4},{36,40},{40,36},{5,9},{9,5},{37,41},{41,37},{6,10},{10... | collective-permute-start | bytes 516104 | tf_op jit(solution)/shard_map/while/body/ppermute | solution.py:507
  105.5 1.9 %collective-permute-start.1 = (f32[21,2,8,128]{3,2,1,0:T(8,128)S(1)}, f32[21,2,8,128]{3,2,1,0:T(8,128)S(1)}, u32[]{:S(2)}, u32[]{:S(2)}) collective-permute-start(f32[21,2,8,128]{3,2,1,0:T(8,128)S(1)} %get-tuple-element.146), channel_id=1, source_target_pairs={{0,4},{4,0},{32,36},{36,32},{1,5},{5,1},{33,37},{37,33},{2,6},{6,2... | collective-permute-start | bytes 516104 | tf_op jit(solution)/shard_map/while/body/ppermute | solution.py:508
  107.4 7.2 %collective-permute-done.refs_4_ = f32[21,2,8,128]{3,2,1,0:T(8,128)S(1)} collective-permute-done((f32[21,2,8,128]{3,2,1,0:T(8,128)S(1)}, f32[21,2,8,128]{3,2,1,0:T(8,128)S(1)}, u32[]{:S(2)}, u32[]{:S(2)}) %collective-permute-start) | collective-permute-done | bytes 172064 | tf_op jit(solution)/shard_map/while/body/ppermute | solution.py:507
  114.6 0.0 collective-permute-done.1.refs_5_
  114.6 2.7 %body.3 = (f32[16,2,2,8,128]{4,3,2,1,0:T(8,128)}, f32[2,8,8,128]{3,2,1,0:T(8,128)S(1)}) custom-call(f32[32,2,2,8,128]{4,3,2,1,0:T(8,128)S(1)} %get-tuple-element.171.refs_1_.refs_0_, f32[12,2,2,8,128]{4,3,2,1,0:T(8,128)S(1)} %get-tuple-element.172.refs_2_.refs_1_, f32[24,2,8,128]{3,2,1,0:T(8,128)S(1)} %get-tuple-element.173.refs_3_.refs_2_, ...), custom_call_target="tpu_custom_call" | custom-call | flops 8 | bytes 8 | tf_op jit(solution)/shard_map/while/body/pallas_call | solution.py:494
  118.0 0.0 collective-permute-done.5.refs_1_
  118.0 0.5 shard_map.64
  118.5 4.4 %collective-permute-start.9 = (f32[32,2,8,128]{3,2,1,0:T(8,128)S(1)}, f32[32,2,8,128]{3,2,1,0:T(8,128)S(1)}, u32[]{:S(2)}, u32[]{:S(2)}) collective-permute-start(f32[32,2,8,128]{3,2,1,0:T(8,128)S(1)} %get-tuple-element.72), channel_id=1, source_target_pairs={{32,1},{1,32},{33,2},{2,33},{34,3},{3,34},{35,131},{131,35},{163,1... | collective-permute-start | bytes 786440 | tf_op jit(solution)/shard_map/ppermute | solution.py:507
  123.0 0.0 copy-start.2
  123.0 2.8 %collective-permute-start.10 = (f32[32,2,8,128]{3,2,1,0:T(8,128)S(1)}, f32[32,2,8,128]{3,2,1,0:T(8,128)S(1)}, u32[]{:S(2)}, u32[]{:S(2)}) collective-permute-start(f32[32,2,8,128]{3,2,1,0:T(8,128)S(1)} %get-tuple-element.73), channel_id=1, source_target_pairs={{0,32},{32,0},{1,33},{33,1},{2,34},{34,2},{3,35},{35,3},{131,163},... | collective-permute-start | bytes 786440 | tf_op jit(solution)/shard_map/ppermute | solution.py:508
  125.8 1.5 collective-permute-done.9.refs_3_
  127.3 0.0 collective-permute-done.10.refs_4_
  127.3 0.3 shard_map.65
  127.7 3.4 %collective-permute-start.11 = (f32[36,2,8,128]{3,2,1,0:T(8,128)S(1)}, f32[36,2,8,128]{3,2,1,0:T(8,128)S(1)}, u32[]{:S(2)}, u32[]{:S(2)}) collective-permute-start(f32[36,2,8,128]{3,2,1,0:T(8,128)S(1)} %get-tuple-element.74), channel_id=1, source_target_pairs={{4,8},{8,4},{36,40},{40,36},{5,9},{9,5},{37,41},{41,37},{6,10},{10... | collective-permute-start | bytes 884744 | tf_op jit(solution)/shard_map/ppermute | solution.py:507
  131.1 1.9 %collective-permute-start.12 = (f32[36,2,8,128]{3,2,1,0:T(8,128)S(1)}, f32[36,2,8,128]{3,2,1,0:T(8,128)S(1)}, u32[]{:S(2)}, u32[]{:S(2)}) collective-permute-start(f32[36,2,8,128]{3,2,1,0:T(8,128)S(1)} %get-tuple-element.75), channel_id=1, source_target_pairs={{0,4},{4,0},{32,36},{36,32},{1,5},{5,1},{33,37},{37,33},{2,6},{6,2... | collective-permute-start | bytes 884744 | tf_op jit(solution)/shard_map/ppermute | solution.py:508
  133.0 4.3 %collective-permute-done.11.refs_5_ = f32[36,2,8,128]{3,2,1,0:T(8,128)S(1)} collective-permute-done((f32[36,2,8,128]{3,2,1,0:T(8,128)S(1)}, f32[36,2,8,128]{3,2,1,0:T(8,128)S(1)}, u32[]{:S(2)}, u32[]{:S(2)}) %collective-permute-start.11) | collective-permute-done | bytes 294944 | tf_op jit(solution)/shard_map/ppermute | solution.py:507
  137.3 2.5 %collective-permute-done.12.refs_6_ = f32[36,2,8,128]{3,2,1,0:T(8,128)S(1)} collective-permute-done((f32[36,2,8,128]{3,2,1,0:T(8,128)S(1)}, f32[36,2,8,128]{3,2,1,0:T(8,128)S(1)}, u32[]{:S(2)}, u32[]{:S(2)}) %collective-permute-start.12) | collective-permute-done | bytes 294944 | tf_op jit(solution)/shard_map/ppermute | solution.py:508
  139.8 0.0 copy-done.2
  139.8 3.2 %shard_map.66 = f32[32,2,2,8,128]{4,3,2,1,0:T(8,128)S(1)} custom-call(f32[32,2,2,8,128]{4,3,2,1,0:T(8,128)S(1)} %get-tuple-element.198, f32[16,2,2,8,128]{4,3,2,1,0:T(8,128)S(1)} %collective-permute-done.5.refs_1_, f32[2,8,8,128]{3,2,1,0:T(8,128)S(1)} %get-tuple-element.71.refs_2_, f32[32,2,8,128]{3,2,1,0:T(8,128)S(1)} %collective-permute-done.9.refs_3_, ...), custom_call_target="tpu_custom_call" | custom-call | flops 8 | bytes 8 | tf_op jit(solution)/shard_map/pallas_call | solution.py:494
  143.0 0.0 copy-start.1
  143.0 18.7 %all_to_all.11.got = f32[32,2,2,8,128]{4,3,2,1,0:T(8,128)S(1)} all-to-all(f32[32,2,2,8,128]{4,3,2,1,0:T(8,128)S(1)} %shard_map.66), channel_id=1, replica_groups={{0,1,2,3,32,33,34,35,128,129,130,131,160,161,162,163,256,257,258,259,28..., dimensions={0} | all-to-all | bytes 1048576 | tf_op jit(solution)/shard_map/all_to_all | solution.py:583
  161.8 0.0 copy-done.1
  161.8 1.5 shard_map.67
  (3 shorter events, 0.1 us)
Async XLA Ops:
  2.5 19.5 %collective-permute-start.3 = (f32[2,4,32,512]{3,2,1,0:T(8,128)}, f32[2,4,32,512]{3,2,1,0:T(8,128)S(1)}, u32[]{:S(2)}, u32[]{:S(2)}) collective-permute-start(f32[2,4,32,512]{3,2,1,0:T(8,128)} %shard_map.59.start), channel_id=1, source_target_pairs={{0,1},{1,0},{2,3},{3,2},{4,5},{5,4},{6,7},{7,6},{8,9},{9,8},{10,11... | collective-permute-start | bytes 1572872 | tf_op jit(solution)/shard_map/ppermute | solution.py:522
  6.4 24.6 %collective-permute-start.2 = (f32[2,4,32,512]{3,2,1,0:T(8,128)}, f32[2,4,32,512]{3,2,1,0:T(8,128)S(1)}, u32[]{:S(2)}, u32[]{:S(2)}) collective-permute-start(f32[2,4,32,512]{3,2,1,0:T(8,128)} %shard_map.59.start), channel_id=1, source_target_pairs={{1,2},{2,1},{3,4},{4,3},{5,6},{6,5},{7,8},{8,7},{9,10},{10,9},{11,... | collective-permute-start | bytes 1572872 | tf_op jit(solution)/shard_map/ppermute | solution.py:523
  20.8 1.1 copy-start
  56.2 27.4 %collective-permute-start.4 = (f32[8,2,2,8,128]{4,3,2,1,0:T(8,128)S(1)}, f32[8,2,2,8,128]{4,3,2,1,0:T(8,128)S(1)}, u32[]{:S(2)}, u32[]{:S(2)}) collective-permute-start(f32[8,2,2,8,128]{4,3,2,1,0:T(8,128)S(1)} %get-tuple-element.63), channel_id=1, source_target_pairs={{0,64},{32,96},{64,0},{96,32},{128,192},{160,224},{192,128},{224,1... | collective-permute-start | bytes 393224 | tf_op jit(solution)/shard_map/ppermute | solution.py:550
  69.5 20.2 %collective-permute-start.6 = (f32[4,2,2,8,128]{4,3,2,1,0:T(8,128)S(1)}, f32[4,2,2,8,128]{4,3,2,1,0:T(8,128)S(1)}, u32[]{:S(2)}, u32[]{:S(2)}) collective-permute-start(f32[4,2,2,8,128]{4,3,2,1,0:T(8,128)S(1)} %get-tuple-element.68), channel_id=1, source_target_pairs={{0,64},{32,96},{64,0},{96,32},{128,192},{160,224},{192,128},{224,1... | collective-permute-start | bytes 196616 | tf_op jit(solution)/shard_map/ppermute | solution.py:551
  83.6 34.4 %collective-permute-start.5 = (f32[16,2,2,8,128]{4,3,2,1,0:T(8,128)S(1)}, f32[16,2,2,8,128]{4,3,2,1,0:T(8,128)S(1)}, u32[]{:S(2)}, u32[]{:S(2)}) collective-permute-start(f32[16,2,2,8,128]{4,3,2,1,0:T(8,128)S(1)} %get-tuple-element.64), channel_id=1, source_target_pairs={{0,64},{32,96},{64,0},{96,32},{128,192},{160,224},{192,128},{224,1... | collective-permute-start | bytes 786440 | tf_op jit(solution)/shard_map/ppermute | solution.py:575
  90.2 7.0 %collective-permute-start.7 = (f32[24,2,8,128]{3,2,1,0:T(8,128)S(1)}, f32[24,2,8,128]{3,2,1,0:T(8,128)S(1)}, u32[]{:S(2)}, u32[]{:S(2)}) collective-permute-start(f32[24,2,8,128]{3,2,1,0:T(8,128)S(1)} %get-tuple-element.69), channel_id=1, source_target_pairs={{32,1},{1,32},{33,2},{2,33},{34,3},{3,34},{35,131},{131,35},{163,1... | collective-permute-start | bytes 589832 | tf_op jit(solution)/shard_map/ppermute | solution.py:507
  93.3 4.3 %collective-permute-start.8 = (f32[24,2,8,128]{3,2,1,0:T(8,128)S(1)}, f32[24,2,8,128]{3,2,1,0:T(8,128)S(1)}, u32[]{:S(2)}, u32[]{:S(2)}) collective-permute-start(f32[24,2,8,128]{3,2,1,0:T(8,128)S(1)} %get-tuple-element.70), channel_id=1, source_target_pairs={{0,32},{32,0},{1,33},{33,1},{2,34},{34,2},{3,35},{35,3},{131,163},... | collective-permute-start | bytes 589832 | tf_op jit(solution)/shard_map/ppermute | solution.py:508
  98.6 16.0 %collective-permute-start = (f32[21,2,8,128]{3,2,1,0:T(8,128)S(1)}, f32[21,2,8,128]{3,2,1,0:T(8,128)S(1)}, u32[]{:S(2)}, u32[]{:S(2)}) collective-permute-start(f32[21,2,8,128]{3,2,1,0:T(8,128)S(1)} %get-tuple-element.145), channel_id=1, source_target_pairs={{4,8},{8,4},{36,40},{40,36},{5,9},{9,5},{37,41},{41,37},{6,10},{10... | collective-permute-start | bytes 516104 | tf_op jit(solution)/shard_map/while/body/ppermute | solution.py:507
  105.5 9.1 %collective-permute-start.1 = (f32[21,2,8,128]{3,2,1,0:T(8,128)S(1)}, f32[21,2,8,128]{3,2,1,0:T(8,128)S(1)}, u32[]{:S(2)}, u32[]{:S(2)}) collective-permute-start(f32[21,2,8,128]{3,2,1,0:T(8,128)S(1)} %get-tuple-element.146), channel_id=1, source_target_pairs={{0,4},{4,0},{32,36},{36,32},{1,5},{5,1},{33,37},{37,33},{2,6},{6,2... | collective-permute-start | bytes 516104 | tf_op jit(solution)/shard_map/while/body/ppermute | solution.py:508
  118.5 8.8 %collective-permute-start.9 = (f32[32,2,8,128]{3,2,1,0:T(8,128)S(1)}, f32[32,2,8,128]{3,2,1,0:T(8,128)S(1)}, u32[]{:S(2)}, u32[]{:S(2)}) collective-permute-start(f32[32,2,8,128]{3,2,1,0:T(8,128)S(1)} %get-tuple-element.72), channel_id=1, source_target_pairs={{32,1},{1,32},{33,2},{2,33},{34,3},{3,34},{35,131},{131,35},{163,1... | collective-permute-start | bytes 786440 | tf_op jit(solution)/shard_map/ppermute | solution.py:507
  123.0 16.8 %copy-start.2 = (f32[16,2,2,8,128]{4,3,2,1,0:T(8,128)S(1)}, f32[16,2,2,8,128]{4,3,2,1,0:T(8,128)}, u32[]{:S(2)}) copy-start(f32[16,2,2,8,128]{4,3,2,1,0:T(8,128)} %get-tuple-element.76.refs_7_) | copy-start | bytes 786436
  123.0 4.3 %collective-permute-start.10 = (f32[32,2,8,128]{3,2,1,0:T(8,128)S(1)}, f32[32,2,8,128]{3,2,1,0:T(8,128)S(1)}, u32[]{:S(2)}, u32[]{:S(2)}) collective-permute-start(f32[32,2,8,128]{3,2,1,0:T(8,128)S(1)} %get-tuple-element.73), channel_id=1, source_target_pairs={{0,32},{32,0},{1,33},{33,1},{2,34},{34,2},{3,35},{35,3},{131,163},... | collective-permute-start | bytes 786440 | tf_op jit(solution)/shard_map/ppermute | solution.py:508
  127.7 9.7 %collective-permute-start.11 = (f32[36,2,8,128]{3,2,1,0:T(8,128)S(1)}, f32[36,2,8,128]{3,2,1,0:T(8,128)S(1)}, u32[]{:S(2)}, u32[]{:S(2)}) collective-permute-start(f32[36,2,8,128]{3,2,1,0:T(8,128)S(1)} %get-tuple-element.74), channel_id=1, source_target_pairs={{4,8},{8,4},{36,40},{40,36},{5,9},{9,5},{37,41},{41,37},{6,10},{10... | collective-permute-start | bytes 884744 | tf_op jit(solution)/shard_map/ppermute | solution.py:507
  131.1 8.7 %collective-permute-start.12 = (f32[36,2,8,128]{3,2,1,0:T(8,128)S(1)}, f32[36,2,8,128]{3,2,1,0:T(8,128)S(1)}, u32[]{:S(2)}, u32[]{:S(2)}) collective-permute-start(f32[36,2,8,128]{3,2,1,0:T(8,128)S(1)} %get-tuple-element.75), channel_id=1, source_target_pairs={{0,4},{4,0},{32,36},{36,32},{1,5},{5,1},{33,37},{37,33},{2,6},{6,2... | collective-permute-start | bytes 884744 | tf_op jit(solution)/shard_map/ppermute | solution.py:508
  143.0 18.7 %copy-start.1 = (f32[2,4,32,512]{3,2,1,0:T(8,128)S(1)}, f32[2,4,32,512]{3,2,1,0:T(8,128)}, u32[]{:S(2)}) copy-start(f32[2,4,32,512]{3,2,1,0:T(8,128)} %shard_map.59.start) | copy-start | bytes 1572868

commit v6 on v5

--- a/solution.py
+++ b/solution.py
@@ -400,13 +400,11 @@
     end_up = is_top & (lanes >= 96)
     end_down = is_bottom & (lanes < 32)
 
-    def z_up(v):
-        w = jnp.where(is_bottom, pltpu.roll(v, 96, 2), v)
-        return jnp.where(end_up, v, pltpu.roll(w, 7, 1))
-
-    def z_down(v):
-        w = jnp.where(is_top, pltpu.roll(v, 32, 2), v)
-        return jnp.where(end_down, v, pltpu.roll(w, 1, 1))
+    def z_next(p, u, lanes_on, near, far, by, end):
+        u_turned = pltpu.roll(u, by, 1)
+        crossed = pltpu.roll(jnp.where(far, u_turned, p), lanes_on, 2)
+        p_turned = pltpu.roll(jnp.where(near, crossed, p), by, 1)
+        return jnp.where(end, p, p_turned), jnp.where(end, u, jnp.where(far, crossed, u_turned))
 
     for j in range(1, phase.steps + 1):
         src, dst = (j + 1) % 2, j % 2
@@ -416,16 +414,18 @@
             starts.append(hi - 4)
         for r in starts:
             pc, uc = state[src, 0, r : r + 4], state[src, 1, r : r + 4]
+            p_up, u_up = z_next(pc, uc, 96, is_bottom, is_top, 7, end_up)
+            p_down, u_down = z_next(pc, uc, 32, is_top, is_bottom, 1, end_down)
             rate = growth(
                 pc, uc,
                 state[src, 0, r - 1 : r + 3], state[src, 0, r + 1 : r + 5],
                 pltpu.roll(pc, 1, 2), pltpu.roll(pc, 127, 2),
-                z_down(pc), z_up(pc),
+                p_down, p_up,
             )
             ulap = (
                 (state[src, 1, r - 1 : r + 3] + state[src, 1, r + 1 : r + 5])
                 + (pltpu.roll(uc, 1, 2) + pltpu.roll(uc, 127, 2))
-                + (z_down(uc) + z_up(uc))
+                + (u_down + u_up)
                 - 6.0 * uc
             )
             gain = COARSE_RATE * rate

time: 164 us -> 164 us (level)
  no operation moved by 1% of the time
where the time goes in v6:
time: 164 us; the launch traced here: 163 us
  starting transfers between devices  67.4 us (41%)
  waiting for transfers between devices  37.8 us (23%)
  blocking collectives  37.4 us (23%)
  Pallas kernels  17 us (10%)
    all_to_all x1, blocking collectives, local(): lax.all_to_all(got, AXES, 0, 0, tiled=True, axis_index_groups=PLANE_GROUPS)  18.7 us
    all_to_all x1, blocking collectives, local(): lax.all_to_all(packed, AXES, 0, 0, tiled=True, axis_index_groups=PLANE_GR...  18.7 us
    ppermute x4, starting transfers between devices, exchange(): got_odd = lax.ppermute(odd, axis, pairs(1))  17.9 us
    pallas_call x10, Pallas kernels, call(): pl.pallas_call(kernel, out_shape=shapes if len(shapes) > 1 else shapes[0]...  16.5 us
    ppermute x1, starting transfers between devices, local(): odd = lax.ppermute(start, 'space', space_pairs(1))  14.4 us
    ppermute x4, waiting for transfers between devices, exchange(): got_odd = lax.ppermute(odd, axis, pairs(1))  13.5 us
    ppermute x1, starting transfers between devices, local(): near = lax.ppermute(near, 'tm', ACROSS)  13.3 us
    ppermute x1, waiting for transfers between devices, local(): near = lax.ppermute(near, 'tm', ACROSS)  12.2 us
  transfers between devices with their start and end apart: 13, of which 8 were waited for; matrix products, arithmetic and copies ran while one was open for 0% of the time, Pallas kernels for 2%

profile of v6, /device:TPU:1, one launch (start us, length us, event | category | flops | bytes accessed | tf_op | source)
XLA Modules:
  0.0 162.9 jit_solution(4930055791336050565)
XLA Ops:
  0.6 1.8 %shard_map.59.start = f32[2,4,32,512]{3,2,1,0:T(8,128)} custom-call(s32[3,8]{1,0:T(4,128)} %bitcast.2, f32[1,4,32,512]{3,2,1,0:T(8,128)} %p_in.1, f32[1,4,32,512]{3,2,1,0:T(8,128)} %u_in.1, f32[4,32,512]{2,1,0:T(8,128)} %u_start.1), custom_call_target="tpu_custom_call" | custom-call | flops 8 | bytes 8 | tf_op jit(solution)/shard_map/pallas_call | solution.py:494
  2.5 3.9 %collective-permute-start.3 = (f32[2,4,32,512]{3,2,1,0:T(8,128)}, f32[2,4,32,512]{3,2,1,0:T(8,128)S(1)}, u32[]{:S(2)}, u32[]{:S(2)}) collective-permute-start(f32[2,4,32,512]{3,2,1,0:T(8,128)} %shard_map.59.start), channel_id=1, source_target_pairs={{0,1},{1,0},{2,3},{3,2},{4,5},{5,4},{6,7},{7,6},{8,9},{9,8},{10,11... | collective-permute-start | bytes 1572872 | tf_op jit(solution)/shard_map/ppermute | solution.py:522
  6.4 14.4 %collective-permute-start.2 = (f32[2,4,32,512]{3,2,1,0:T(8,128)}, f32[2,4,32,512]{3,2,1,0:T(8,128)S(1)}, u32[]{:S(2)}, u32[]{:S(2)}) collective-permute-start(f32[2,4,32,512]{3,2,1,0:T(8,128)} %shard_map.59.start), channel_id=1, source_target_pairs={{1,2},{2,1},{3,4},{4,3},{5,6},{6,5},{7,8},{8,7},{9,10},{10,9},{11,... | collective-permute-start | bytes 1572872 | tf_op jit(solution)/shard_map/ppermute | solution.py:523
  20.8 0.0 copy-start
  20.9 1.0 copy-done
  22.0 0.0 collective-permute-done.3.even
  22.0 9.1 %collective-permute-done.2.odd = f32[2,4,32,512]{3,2,1,0:T(8,128)S(1)} collective-permute-done((f32[2,4,32,512]{3,2,1,0:T(8,128)}, f32[2,4,32,512]{3,2,1,0:T(8,128)S(1)}, u32[]{:S(2)}, u32[]{:S(2)}) %collective-permute-start.2) | collective-permute-done | bytes 524320 | tf_op jit(solution)/shard_map/ppermute | solution.py:523
  31.0 5.9 %shard_map.61 = f32[32,2,2,8,128]{4,3,2,1,0:T(8,128)S(1)} custom-call(f32[2,4,32,512]{3,2,1,0:T(8,128)S(1)} %shard_map.60.start, f32[2,4,32,512]{3,2,1,0:T(8,128)S(1)} %collective-permute-done.2.odd, f32[2,4,32,512]{3,2,1,0:T(8,128)S(1)} %collective-permute-done.3.even), custom_call_target="tpu_custom_call" | custom-call | flops 8 | bytes 8 | tf_op jit(solution)/shard_map/pallas_call | solution.py:494
  37.0 18.7 %all_to_all.10.own.refs_0_ = f32[32,2,2,8,128]{4,3,2,1,0:T(8,128)S(1)} all-to-all(f32[32,2,2,8,128]{4,3,2,1,0:T(8,128)S(1)} %shard_map.61), channel_id=1, replica_groups={{0,1,2,3,32,33,34,35,128,129,130,131,160,161,162,163,256,257,258,259,28..., dimensions={0} | all-to-all | bytes 1048576 | tf_op jit(solution)/shard_map/all_to_all | solution.py:538
  55.7 0.5 shard_map.62
  56.2 13.3 %collective-permute-start.4 = (f32[8,2,2,8,128]{4,3,2,1,0:T(8,128)S(1)}, f32[8,2,2,8,128]{4,3,2,1,0:T(8,128)S(1)}, u32[]{:S(2)}, u32[]{:S(2)}) collective-permute-start(f32[8,2,2,8,128]{4,3,2,1,0:T(8,128)S(1)} %get-tuple-element.63), channel_id=1, source_target_pairs={{0,64},{32,96},{64,0},{96,32},{128,192},{160,224},{192,128},{224,1... | collective-permute-start | bytes 393224 | tf_op jit(solution)/shard_map/ppermute | solution.py:550
  69.5 1.9 %collective-permute-start.6 = (f32[4,2,2,8,128]{4,3,2,1,0:T(8,128)S(1)}, f32[4,2,2,8,128]{4,3,2,1,0:T(8,128)S(1)}, u32[]{:S(2)}, u32[]{:S(2)}) collective-permute-start(f32[4,2,2,8,128]{4,3,2,1,0:T(8,128)S(1)} %get-tuple-element.68), channel_id=1, source_target_pairs={{0,64},{32,96},{64,0},{96,32},{128,192},{160,224},{192,128},{224,1... | collective-permute-start | bytes 196616 | tf_op jit(solution)/shard_map/ppermute | solution.py:551
  71.4 12.2 %collective-permute-done.4 = f32[8,2,2,8,128]{4,3,2,1,0:T(8,128)S(1)} collective-permute-done((f32[8,2,2,8,128]{4,3,2,1,0:T(8,128)S(1)}, f32[8,2,2,8,128]{4,3,2,1,0:T(8,128)S(1)}, u32[]{:S(2)}, u32[]{:S(2)}) %collective-permute-start.4) | collective-permute-done | bytes 131104 | tf_op jit(solution)/shard_map/ppermute | solution.py:550
  83.6 6.0 %collective-permute-start.5 = (f32[16,2,2,8,128]{4,3,2,1,0:T(8,128)S(1)}, f32[16,2,2,8,128]{4,3,2,1,0:T(8,128)S(1)}, u32[]{:S(2)}, u32[]{:S(2)}) collective-permute-start(f32[16,2,2,8,128]{4,3,2,1,0:T(8,128)S(1)} %get-tuple-element.64), channel_id=1, source_target_pairs={{0,64},{32,96},{64,0},{96,32},{128,192},{160,224},{192,128},{224,1... | collective-permute-start | bytes 786440 | tf_op jit(solution)/shard_map/ppermute | solution.py:575
  89.7 0.0 collective-permute-done.6
  89.7 0.4 shard_map.63
  90.2 3.1 %collective-permute-start.7 = (f32[24,2,8,128]{3,2,1,0:T(8,128)S(1)}, f32[24,2,8,128]{3,2,1,0:T(8,128)S(1)}, u32[]{:S(2)}, u32[]{:S(2)}) collective-permute-start(f32[24,2,8,128]{3,2,1,0:T(8,128)S(1)} %get-tuple-element.69), channel_id=1, source_target_pairs={{32,1},{1,32},{33,2},{2,33},{34,3},{3,34},{35,131},{131,35},{163,1... | collective-permute-start | bytes 589832 | tf_op jit(solution)/shard_map/ppermute | solution.py:507
  93.3 3.3 %collective-permute-start.8 = (f32[24,2,8,128]{3,2,1,0:T(8,128)S(1)}, f32[24,2,8,128]{3,2,1,0:T(8,128)S(1)}, u32[]{:S(2)}, u32[]{:S(2)}) collective-permute-start(f32[24,2,8,128]{3,2,1,0:T(8,128)S(1)} %get-tuple-element.70), channel_id=1, source_target_pairs={{0,32},{32,0},{1,33},{33,1},{2,34},{34,2},{3,35},{35,3},{131,163},... | collective-permute-start | bytes 589832 | tf_op jit(solution)/shard_map/ppermute | solution.py:508
  96.6 0.5 collective-permute-done.7
  97.2 0.5 collective-permute-done.8
  97.7 20.2 %while.12 = (s32[]{:T(128)}, f32[16,2,2,8,128]{4,3,2,1,0:T(8,128)}, f32[2,8,8,128]{3,2,1,0:T(8,128)S(1)}, s32[]{:T(128)}, f32[32,2,2,8,128]{4,3,2,1,0:T(8,128)S(...) while((s32[]{:T(128)}, f32[16,2,2,8,128]{4,3,2,1,0:T(8,128)}, ...), condition=%wide.region_1.0_spmd, body=%wide.region_0.0_spmd.sunk | while | flops 18 | bytes 1376445 | solution.py:577
  98.3 0.2 body.2
  98.6 6.9 %collective-permute-start = (f32[21,2,8,128]{3,2,1,0:T(8,128)S(1)}, f32[21,2,8,128]{3,2,1,0:T(8,128)S(1)}, u32[]{:S(2)}, u32[]{:S(2)}) collective-permute-start(f32[21,2,8,128]{3,2,1,0:T(8,128)S(1)} %get-tuple-element.145), channel_id=1, source_target_pairs={{4,8},{8,4},{36,40},{40,36},{5,9},{9,5},{37,41},{41,37},{6,10},{10... | collective-permute-start | bytes 516104 | tf_op jit(solution)/shard_map/while/body/ppermute | solution.py:507
  105.5 1.9 %collective-permute-start.1 = (f32[21,2,8,128]{3,2,1,0:T(8,128)S(1)}, f32[21,2,8,128]{3,2,1,0:T(8,128)S(1)}, u32[]{:S(2)}, u32[]{:S(2)}) collective-permute-start(f32[21,2,8,128]{3,2,1,0:T(8,128)S(1)} %get-tuple-element.146), channel_id=1, source_target_pairs={{0,4},{4,0},{32,36},{36,32},{1,5},{5,1},{33,37},{37,33},{2,6},{6,2... | collective-permute-start | bytes 516104 | tf_op jit(solution)/shard_map/while/body/ppermute | solution.py:508
  107.4 7.2 %collective-permute-done.refs_4_ = f32[21,2,8,128]{3,2,1,0:T(8,128)S(1)} collective-permute-done((f32[21,2,8,128]{3,2,1,0:T(8,128)S(1)}, f32[21,2,8,128]{3,2,1,0:T(8,128)S(1)}, u32[]{:S(2)}, u32[]{:S(2)}) %collective-permute-start) | collective-permute-done | bytes 172064 | tf_op jit(solution)/shard_map/while/body/ppermute | solution.py:507
  114.6 0.0 collective-permute-done.1.refs_5_
  114.6 2.6 %body.3 = (f32[16,2,2,8,128]{4,3,2,1,0:T(8,128)}, f32[2,8,8,128]{3,2,1,0:T(8,128)S(1)}) custom-call(f32[32,2,2,8,128]{4,3,2,1,0:T(8,128)S(1)} %get-tuple-element.171.refs_1_.refs_0_, f32[12,2,2,8,128]{4,3,2,1,0:T(8,128)S(1)} %get-tuple-element.172.refs_2_.refs_1_, f32[24,2,8,128]{3,2,1,0:T(8,128)S(1)} %get-tuple-element.173.refs_3_.refs_2_, ...), custom_call_target="tpu_custom_call" | custom-call | flops 8 | bytes 8 | tf_op jit(solution)/shard_map/while/body/pallas_call | solution.py:494
  117.9 0.0 collective-permute-done.5.refs_1_
  117.9 0.5 shard_map.64
  118.4 4.4 %collective-permute-start.9 = (f32[32,2,8,128]{3,2,1,0:T(8,128)S(1)}, f32[32,2,8,128]{3,2,1,0:T(8,128)S(1)}, u32[]{:S(2)}, u32[]{:S(2)}) collective-permute-start(f32[32,2,8,128]{3,2,1,0:T(8,128)S(1)} %get-tuple-element.72), channel_id=1, source_target_pairs={{32,1},{1,32},{33,2},{2,33},{34,3},{3,34},{35,131},{131,35},{163,1... | collective-permute-start | bytes 786440 | tf_op jit(solution)/shard_map/ppermute | solution.py:507
  122.8 0.0 copy-start.2
  122.9 2.8 %collective-permute-start.10 = (f32[32,2,8,128]{3,2,1,0:T(8,128)S(1)}, f32[32,2,8,128]{3,2,1,0:T(8,128)S(1)}, u32[]{:S(2)}, u32[]{:S(2)}) collective-permute-start(f32[32,2,8,128]{3,2,1,0:T(8,128)S(1)} %get-tuple-element.73), channel_id=1, source_target_pairs={{0,32},{32,0},{1,33},{33,1},{2,34},{34,2},{3,35},{35,3},{131,163},... | collective-permute-start | bytes 786440 | tf_op jit(solution)/shard_map/ppermute | solution.py:508
  125.6 1.5 collective-permute-done.9.refs_3_
  127.2 0.0 collective-permute-done.10.refs_4_
  127.2 0.3 shard_map.65
  127.5 3.4 %collective-permute-start.11 = (f32[36,2,8,128]{3,2,1,0:T(8,128)S(1)}, f32[36,2,8,128]{3,2,1,0:T(8,128)S(1)}, u32[]{:S(2)}, u32[]{:S(2)}) collective-permute-start(f32[36,2,8,128]{3,2,1,0:T(8,128)S(1)} %get-tuple-element.74), channel_id=1, source_target_pairs={{4,8},{8,4},{36,40},{40,36},{5,9},{9,5},{37,41},{41,37},{6,10},{10... | collective-permute-start | bytes 884744 | tf_op jit(solution)/shard_map/ppermute | solution.py:507
  131.0 1.9 %collective-permute-start.12 = (f32[36,2,8,128]{3,2,1,0:T(8,128)S(1)}, f32[36,2,8,128]{3,2,1,0:T(8,128)S(1)}, u32[]{:S(2)}, u32[]{:S(2)}) collective-permute-start(f32[36,2,8,128]{3,2,1,0:T(8,128)S(1)} %get-tuple-element.75), channel_id=1, source_target_pairs={{0,4},{4,0},{32,36},{36,32},{1,5},{5,1},{33,37},{37,33},{2,6},{6,2... | collective-permute-start | bytes 884744 | tf_op jit(solution)/shard_map/ppermute | solution.py:508
  132.9 4.3 %collective-permute-done.11.refs_5_ = f32[36,2,8,128]{3,2,1,0:T(8,128)S(1)} collective-permute-done((f32[36,2,8,128]{3,2,1,0:T(8,128)S(1)}, f32[36,2,8,128]{3,2,1,0:T(8,128)S(1)}, u32[]{:S(2)}, u32[]{:S(2)}) %collective-permute-start.11) | collective-permute-done | bytes 294944 | tf_op jit(solution)/shard_map/ppermute | solution.py:507
  137.2 2.5 %collective-permute-done.12.refs_6_ = f32[36,2,8,128]{3,2,1,0:T(8,128)S(1)} collective-permute-done((f32[36,2,8,128]{3,2,1,0:T(8,128)S(1)}, f32[36,2,8,128]{3,2,1,0:T(8,128)S(1)}, u32[]{:S(2)}, u32[]{:S(2)}) %collective-permute-start.12) | collective-permute-done | bytes 294944 | tf_op jit(solution)/shard_map/ppermute | solution.py:508
  139.7 0.0 copy-done.2
  139.7 3.0 %shard_map.66 = f32[32,2,2,8,128]{4,3,2,1,0:T(8,128)S(1)} custom-call(f32[32,2,2,8,128]{4,3,2,1,0:T(8,128)S(1)} %get-tuple-element.198, f32[16,2,2,8,128]{4,3,2,1,0:T(8,128)S(1)} %collective-permute-done.5.refs_1_, f32[2,8,8,128]{3,2,1,0:T(8,128)S(1)} %get-tuple-element.71.refs_2_, f32[32,2,8,128]{3,2,1,0:T(8,128)S(1)} %collective-permute-done.9.refs_3_, ...), custom_call_target="tpu_custom_call" | custom-call | flops 8 | bytes 8 | tf_op jit(solution)/shard_map/pallas_call | solution.py:494
  142.7 0.0 copy-start.1
  142.7 18.7 %all_to_all.11.got = f32[32,2,2,8,128]{4,3,2,1,0:T(8,128)S(1)} all-to-all(f32[32,2,2,8,128]{4,3,2,1,0:T(8,128)S(1)} %shard_map.66), channel_id=1, replica_groups={{0,1,2,3,32,33,34,35,128,129,130,131,160,161,162,163,256,257,258,259,28..., dimensions={0} | all-to-all | bytes 1048576 | tf_op jit(solution)/shard_map/all_to_all | solution.py:583
  161.4 0.0 copy-done.1
  161.4 1.5 shard_map.67
  (3 shorter events, 0.1 us)
Async XLA Ops:
  2.5 19.5 %collective-permute-start.3 = (f32[2,4,32,512]{3,2,1,0:T(8,128)}, f32[2,4,32,512]{3,2,1,0:T(8,128)S(1)}, u32[]{:S(2)}, u32[]{:S(2)}) collective-permute-start(f32[2,4,32,512]{3,2,1,0:T(8,128)} %shard_map.59.start), channel_id=1, source_target_pairs={{0,1},{1,0},{2,3},{3,2},{4,5},{5,4},{6,7},{7,6},{8,9},{9,8},{10,11... | collective-permute-start | bytes 1572872 | tf_op jit(solution)/shard_map/ppermute | solution.py:522
  6.4 24.6 %collective-permute-start.2 = (f32[2,4,32,512]{3,2,1,0:T(8,128)}, f32[2,4,32,512]{3,2,1,0:T(8,128)S(1)}, u32[]{:S(2)}, u32[]{:S(2)}) collective-permute-start(f32[2,4,32,512]{3,2,1,0:T(8,128)} %shard_map.59.start), channel_id=1, source_target_pairs={{1,2},{2,1},{3,4},{4,3},{5,6},{6,5},{7,8},{8,7},{9,10},{10,9},{11,... | collective-permute-start | bytes 1572872 | tf_op jit(solution)/shard_map/ppermute | solution.py:523
  20.8 1.1 copy-start
  56.2 27.4 %collective-permute-start.4 = (f32[8,2,2,8,128]{4,3,2,1,0:T(8,128)S(1)}, f32[8,2,2,8,128]{4,3,2,1,0:T(8,128)S(1)}, u32[]{:S(2)}, u32[]{:S(2)}) collective-permute-start(f32[8,2,2,8,128]{4,3,2,1,0:T(8,128)S(1)} %get-tuple-element.63), channel_id=1, source_target_pairs={{0,64},{32,96},{64,0},{96,32},{128,192},{160,224},{192,128},{224,1... | collective-permute-start | bytes 393224 | tf_op jit(solution)/shard_map/ppermute | solution.py:550
  69.5 20.2 %collective-permute-start.6 = (f32[4,2,2,8,128]{4,3,2,1,0:T(8,128)S(1)}, f32[4,2,2,8,128]{4,3,2,1,0:T(8,128)S(1)}, u32[]{:S(2)}, u32[]{:S(2)}) collective-permute-start(f32[4,2,2,8,128]{4,3,2,1,0:T(8,128)S(1)} %get-tuple-element.68), channel_id=1, source_target_pairs={{0,64},{32,96},{64,0},{96,32},{128,192},{160,224},{192,128},{224,1... | collective-permute-start | bytes 196616 | tf_op jit(solution)/shard_map/ppermute | solution.py:551
  83.6 34.2 %collective-permute-start.5 = (f32[16,2,2,8,128]{4,3,2,1,0:T(8,128)S(1)}, f32[16,2,2,8,128]{4,3,2,1,0:T(8,128)S(1)}, u32[]{:S(2)}, u32[]{:S(2)}) collective-permute-start(f32[16,2,2,8,128]{4,3,2,1,0:T(8,128)S(1)} %get-tuple-element.64), channel_id=1, source_target_pairs={{0,64},{32,96},{64,0},{96,32},{128,192},{160,224},{192,128},{224,1... | collective-permute-start | bytes 786440 | tf_op jit(solution)/shard_map/ppermute | solution.py:575
  90.2 7.0 %collective-permute-start.7 = (f32[24,2,8,128]{3,2,1,0:T(8,128)S(1)}, f32[24,2,8,128]{3,2,1,0:T(8,128)S(1)}, u32[]{:S(2)}, u32[]{:S(2)}) collective-permute-start(f32[24,2,8,128]{3,2,1,0:T(8,128)S(1)} %get-tuple-element.69), channel_id=1, source_target_pairs={{32,1},{1,32},{33,2},{2,33},{34,3},{3,34},{35,131},{131,35},{163,1... | collective-permute-start | bytes 589832 | tf_op jit(solution)/shard_map/ppermute | solution.py:507
  93.3 4.3 %collective-permute-start.8 = (f32[24,2,8,128]{3,2,1,0:T(8,128)S(1)}, f32[24,2,8,128]{3,2,1,0:T(8,128)S(1)}, u32[]{:S(2)}, u32[]{:S(2)}) collective-permute-start(f32[24,2,8,128]{3,2,1,0:T(8,128)S(1)} %get-tuple-element.70), channel_id=1, source_target_pairs={{0,32},{32,0},{1,33},{33,1},{2,34},{34,2},{3,35},{35,3},{131,163},... | collective-permute-start | bytes 589832 | tf_op jit(solution)/shard_map/ppermute | solution.py:508
  98.6 16.0 %collective-permute-start = (f32[21,2,8,128]{3,2,1,0:T(8,128)S(1)}, f32[21,2,8,128]{3,2,1,0:T(8,128)S(1)}, u32[]{:S(2)}, u32[]{:S(2)}) collective-permute-start(f32[21,2,8,128]{3,2,1,0:T(8,128)S(1)} %get-tuple-element.145), channel_id=1, source_target_pairs={{4,8},{8,4},{36,40},{40,36},{5,9},{9,5},{37,41},{41,37},{6,10},{10... | collective-permute-start | bytes 516104 | tf_op jit(solution)/shard_map/while/body/ppermute | solution.py:507
  105.5 9.1 %collective-permute-start.1 = (f32[21,2,8,128]{3,2,1,0:T(8,128)S(1)}, f32[21,2,8,128]{3,2,1,0:T(8,128)S(1)}, u32[]{:S(2)}, u32[]{:S(2)}) collective-permute-start(f32[21,2,8,128]{3,2,1,0:T(8,128)S(1)} %get-tuple-element.146), channel_id=1, source_target_pairs={{0,4},{4,0},{32,36},{36,32},{1,5},{5,1},{33,37},{37,33},{2,6},{6,2... | collective-permute-start | bytes 516104 | tf_op jit(solution)/shard_map/while/body/ppermute | solution.py:508
  118.4 8.8 %collective-permute-start.9 = (f32[32,2,8,128]{3,2,1,0:T(8,128)S(1)}, f32[32,2,8,128]{3,2,1,0:T(8,128)S(1)}, u32[]{:S(2)}, u32[]{:S(2)}) collective-permute-start(f32[32,2,8,128]{3,2,1,0:T(8,128)S(1)} %get-tuple-element.72), channel_id=1, source_target_pairs={{32,1},{1,32},{33,2},{2,33},{34,3},{3,34},{35,131},{131,35},{163,1... | collective-permute-start | bytes 786440 | tf_op jit(solution)/shard_map/ppermute | solution.py:507
  122.8 16.8 %copy-start.2 = (f32[16,2,2,8,128]{4,3,2,1,0:T(8,128)S(1)}, f32[16,2,2,8,128]{4,3,2,1,0:T(8,128)}, u32[]{:S(2)}) copy-start(f32[16,2,2,8,128]{4,3,2,1,0:T(8,128)} %get-tuple-element.76.refs_7_) | copy-start | bytes 786436
  122.9 4.3 %collective-permute-start.10 = (f32[32,2,8,128]{3,2,1,0:T(8,128)S(1)}, f32[32,2,8,128]{3,2,1,0:T(8,128)S(1)}, u32[]{:S(2)}, u32[]{:S(2)}) collective-permute-start(f32[32,2,8,128]{3,2,1,0:T(8,128)S(1)} %get-tuple-element.73), channel_id=1, source_target_pairs={{0,32},{32,0},{1,33},{33,1},{2,34},{34,2},{3,35},{35,3},{131,163},... | collective-permute-start | bytes 786440 | tf_op jit(solution)/shard_map/ppermute | solution.py:508
  127.5 9.7 %collective-permute-start.11 = (f32[36,2,8,128]{3,2,1,0:T(8,128)S(1)}, f32[36,2,8,128]{3,2,1,0:T(8,128)S(1)}, u32[]{:S(2)}, u32[]{:S(2)}) collective-permute-start(f32[36,2,8,128]{3,2,1,0:T(8,128)S(1)} %get-tuple-element.74), channel_id=1, source_target_pairs={{4,8},{8,4},{36,40},{40,36},{5,9},{9,5},{37,41},{41,37},{6,10},{10... | collective-permute-start | bytes 884744 | tf_op jit(solution)/shard_map/ppermute | solution.py:507
  131.0 8.7 %collective-permute-start.12 = (f32[36,2,8,128]{3,2,1,0:T(8,128)S(1)}, f32[36,2,8,128]{3,2,1,0:T(8,128)S(1)}, u32[]{:S(2)}, u32[]{:S(2)}) collective-permute-start(f32[36,2,8,128]{3,2,1,0:T(8,128)S(1)} %get-tuple-element.75), channel_id=1, source_target_pairs={{0,4},{4,0},{32,36},{36,32},{1,5},{5,1},{33,37},{37,33},{2,6},{6,2... | collective-permute-start | bytes 884744 | tf_op jit(solution)/shard_map/ppermute | solution.py:508
  142.7 18.7 %copy-start.1 = (f32[2,4,32,512]{3,2,1,0:T(8,128)S(1)}, f32[2,4,32,512]{3,2,1,0:T(8,128)}, u32[]{:S(2)}) copy-start(f32[2,4,32,512]{3,2,1,0:T(8,128)} %shard_map.59.start) | copy-start | bytes 1572868
